TPU v7x, 32 devices: a whole 2x2x4 slice. The times are simulated.
32 devices in a mesh: dp: 8 (over z, core), fsdp: 4 (over y, x).
Axes of the slice: x: 2, y: 2, z: 4, core: 2. Of those that a mesh axis runs over, the one named last changes fastest.
Arguments:
- tokens: bfloat16 [8192, 2048], P(('dp', 'fsdp')), may hold values from -6 to 6
- positions: int32 [8192], P(('dp', 'fsdp')), may hold values from 0 to 1023, as said below
- cotangent: bfloat16 [8192, 2048], P(('dp', 'fsdp')), may hold values from -6 to 6
- w_attn: float32 [2048, 8192], P(('dp', 'fsdp')), may hold values from -0.125 to 0.125
- w_gate_up: float32 [2048, 16384], P(('dp', 'fsdp')), may hold values from -0.125 to 0.125
- w_down: float32 [2048, 8192], P(('dp', 'fsdp')), may hold values from -0.0625 to 0.0625
- gains: float32 [2048, 4], P(('dp', 'fsdp')), may hold values from 0.5 to 2, as said below
- m_attn: float32 [2048, 8192], P(('dp', 'fsdp')), may hold values from -56 to 56
- v_attn: float32 [2048, 8192], P(('dp', 'fsdp')), may hold values from 409.6 to 1638.4
- m_gate_up: float32 [2048, 16384], P(('dp', 'fsdp')), may hold values from -40 to 40
- v_gate_up: float32 [2048, 16384], P(('dp', 'fsdp')), may hold values from 81.92 to 327.68
- m_down: float32 [2048, 8192], P(('dp', 'fsdp')), may hold values from -56 to 56
- v_down: float32 [2048, 8192], P(('dp', 'fsdp')), may hold values from 409.6 to 1638.4
- m_gains: float32 [2048, 4], P(('dp', 'fsdp')), may hold values from -56 to 56
- v_gains: float32 [2048, 4], P(('dp', 'fsdp')), may hold values from 409.6 to 1638.4
Outputs:
- output: bfloat16 [8192, 2048], P(('dp', 'fsdp'))
- grad_tokens: float32 [8192, 2048], P(('dp', 'fsdp'))
- grad_attn: float32 [2048, 8192], P(('dp', 'fsdp'))
- grad_gate_up: float32 [2048, 16384], P(('dp', 'fsdp'))
- grad_down: float32 [2048, 8192], P(('dp', 'fsdp'))
- grad_gains: float32 [2048, 4], P(('dp', 'fsdp'))
- new_attn: float32 [2048, 8192], P(('dp', 'fsdp'))
- new_gate_up: float32 [2048, 16384], P(('dp', 'fsdp'))
- new_down: float32 [2048, 8192], P(('dp', 'fsdp'))
- new_gains: float32 [2048, 4], P(('dp', 'fsdp'))
- new_m_attn: float32 [2048, 8192], P(('dp', 'fsdp'))
- new_v_attn: float32 [2048, 8192], P(('dp', 'fsdp'))
- new_m_gate_up: float32 [2048, 16384], P(('dp', 'fsdp'))
- new_v_gate_up: float32 [2048, 16384], P(('dp', 'fsdp'))
- new_m_down: float32 [2048, 8192], P(('dp', 'fsdp'))
- new_v_down: float32 [2048, 8192], P(('dp', 'fsdp'))
- new_m_gains: float32 [2048, 4], P(('dp', 'fsdp'))
- new_v_gains: float32 [2048, 4], P(('dp', 'fsdp'))
Inputs may be any that keep to these rules, and one draw needn't show every extreme that they name: Within each sequence of 1024 rows the positions count up from 0 by one and restart at 0 at most once, where a second document begins; the first sequence is one document. `gains`: Positive.
All inputs are finite; a program needn't handle non-finite values.
Results may differ from a plain program's by a relative error of at most 0.02.
Values may be sent and summed in bfloat16 or wider, within the bound.
No kernel may reach another device: no remote copies, remote signals or barrier semaphores. Data moves between devices by JAX's collectives and lax.ppermute only.
A program may use at most 296 MiB of HBM per device.

v0:
```python
import math

import jax
import jax.numpy as jnp
from jax import lax
from jax.sharding import PartitionSpec as P

D = 2048
HEADS = 16
HEAD_DIM = 128
FF = 8192


norm_eps = 1e-06
rope_base = 500000.0
learn_rate = 0.004
gain_rate = 0.25
beta_one = 0.9
beta_two = 0.95
decay_rate = 0.1
adam_eps = 1e-08
correct_one = 1.0 - beta_one**2
correct_two = 1.0 - beta_two**2
neg_large = -1e30


def rms_scale(values, gain_vec):
    return (
        values * lax.rsqrt(jnp.mean(values * values, axis=-1, keepdims=True) + norm_eps) * gain_vec
    )


def rope_tables(positions):
    half_dim = HEAD_DIM // 2
    frequency = jnp.exp(
        jnp.arange(half_dim, dtype=jnp.float32) * (-2.0 * math.log(rope_base) / HEAD_DIM)
    )
    angles = positions.astype(jnp.float32)[:, None] * frequency[None, :]
    return (jnp.cos(angles)[:, None, :], jnp.sin(angles)[:, None, :])


def rotate(values, cosine, sine_tab):
    half_dim = values.shape[-1] // 2
    first_half = values[..., :half_dim]
    second_half = values[..., half_dim:]
    return jnp.concatenate(
        [
            first_half * cosine - second_half * sine_tab,
            second_half * cosine + first_half * sine_tab,
        ],
        axis=-1,
    )


def prepare(qkv_raw, gain_query, gain_key, cosine, sine_tab):
    amount = qkv_raw.shape[0]
    query_norm = rms_scale(qkv_raw[:, :D], gain_query).reshape(amount, HEADS, HEAD_DIM)
    key_norm = rms_scale(qkv_raw[:, D : 2 * D], gain_key).reshape(amount, HEADS, HEAD_DIM)
    query_rot = rotate(query_norm, cosine, sine_tab).reshape(amount, D)
    key_rot = rotate(key_norm, cosine, sine_tab).reshape(amount, D)
    return (query_rot, key_rot, qkv_raw[:, 2 * D :])


def contract_last(left, right):
    return lax.dot_general(
        left, right, (((1,), (1,)), ((), ())), preferred_element_type=jnp.float32
    )


def value_grad(weight_low, grad_scaled):
    return jnp.einsum(
        "hqk,qhd->khd",
        weight_low.astype(jnp.float32),
        grad_scaled,
        precision=lax.Precision.HIGHEST,
        preferred_element_type=jnp.float32,
    )


def adamw_step(weight, gradient, moment, second, decay_coef, rate_value):
    moment_new = beta_one * moment + (1.0 - beta_one) * gradient
    second_new = beta_two * second + (1.0 - beta_two) * gradient * gradient
    step_ratio = moment_new / correct_one / (jnp.sqrt(second_new / correct_two) + adam_eps)
    return (
        weight * (1.0 - rate_value * decay_coef) - rate_value * step_ratio,
        moment_new,
        second_new,
    )


def per_device(
    tokens,
    positions,
    cotangent,
    w_attn,
    w_gate_up,
    w_down,
    gains,
    m_attn,
    v_attn,
    m_gate_up,
    v_gate_up,
    m_down,
    v_down,
    m_gains,
    v_gains,
):
    local_rows = tokens.shape[0]
    first_row = lax.axis_index("fsdp") * local_rows
    scale = 1.0 / math.sqrt(HEAD_DIM)
    attn_low = w_attn.astype(jnp.bfloat16)
    gains_low = gains.astype(jnp.bfloat16)
    gate_up_low = w_gate_up.astype(jnp.bfloat16)
    down_low = w_down.astype(jnp.bfloat16)
    attn_full, gains_full = (
        lax.all_gather(attn_low, ("dp", "fsdp"), axis=0, tiled=True),
        lax.all_gather(gains_low, ("dp", "fsdp"), axis=0, tiled=True),
    )
    gain_values = gains_full.astype(jnp.float32)
    token_values = tokens.astype(jnp.float32)
    cosine, sine_tab = rope_tables(positions)
    qkv_raw = jnp.dot(tokens, attn_full[:, : 3 * D], preferred_element_type=jnp.float32)
    query_rot, key_rot, value_flat = prepare(
        qkv_raw, gain_values[:, 0], gain_values[:, 1], cosine, sine_tab
    )
    query_low = query_rot.astype(jnp.bfloat16).reshape(local_rows, HEADS, HEAD_DIM)
    key_low = key_rot.astype(jnp.bfloat16)
    value_low = value_flat.astype(jnp.bfloat16)
    row_index = first_row + jnp.arange(local_rows, dtype=jnp.int32)
    first_key = row_index - positions

    def score_block(key_portion):
        amount = key_portion.shape[0]
        key_heads = key_portion.reshape(amount, HEADS, HEAD_DIM)
        scores = (
            jnp.einsum("qhd,khd->hqk", query_low, key_heads, preferred_element_type=jnp.float32)
            * scale
        )
        key_index = jnp.arange(amount, dtype=jnp.int32)
        allowed = (key_index[None, :] <= row_index[:, None]) & (
            key_index[None, :] >= first_key[:, None]
        )
        return (jnp.where(allowed[None], scores, neg_large), key_heads)

    attend_running_max = jnp.full((HEADS, local_rows), neg_large, jnp.float32)
    key_portion = lax.all_gather(key_low, "fsdp", axis=0, tiled=True)
    value_portion = lax.all_gather(value_low, "fsdp", axis=0, tiled=True)
    scores, unused = score_block(key_portion)
    value_heads = value_portion.reshape(value_portion.shape[0], HEADS, HEAD_DIM)
    new_max = jnp.maximum(attend_running_max, jnp.max(scores, axis=-1))
    weights = jnp.exp(scores - new_max[:, :, None])
    denom_sum = jnp.sum(weights, axis=-1)
    update = jnp.einsum(
        "hqk,khd->qhd",
        weights.astype(jnp.bfloat16),
        value_heads,
        preferred_element_type=jnp.float32,
    )
    accum = update
    running_max, denom_sum, accum = (new_max, denom_sum, accum)
    log_total = running_max + jnp.log(denom_sum)
    attended = accum / jnp.transpose(denom_sum)[:, :, None]
    attended_low = attended.reshape(local_rows, D).astype(jnp.bfloat16)
    branch_attn = jnp.dot(attended_low, attn_full[:, 3 * D :], preferred_element_type=jnp.float32)
    attn_normed, attn_pull = jax.vjp(rms_scale, branch_attn, gain_values[:, 2])
    hidden_state = token_values + attn_normed
    hidden_low = hidden_state.astype(jnp.bfloat16)
    columns = hidden_low
    gate_up = jnp.dot(
        columns,
        lax.all_gather(gate_up_low, ("dp", "fsdp"), axis=0, tiled=True),
        preferred_element_type=jnp.float32,
    )
    gate_part = gate_up[:, :FF]
    up_part = gate_up[:, FF:]
    silu_gate = jax.nn.silu(gate_part)
    activ_low = (silu_gate * up_part).astype(jnp.bfloat16)
    mlp_branch = contract_last(
        activ_low, lax.all_gather(down_low, ("dp", "fsdp"), axis=0, tiled=True)
    )
    mlp_normed, mlp_pull = jax.vjp(rms_scale, mlp_branch, gain_values[:, 3])
    output = (hidden_state + mlp_normed).astype(jnp.bfloat16)
    grad_out = cotangent.astype(jnp.float32)
    grad_mlp, grad_gain_mlp = mlp_pull(grad_out)
    grad_mlp_low = grad_mlp.astype(jnp.bfloat16)
    columns = grad_mlp_low
    grad_activ = jnp.dot(
        columns,
        lax.all_gather(down_low, ("dp", "fsdp"), axis=0, tiled=True),
        preferred_element_type=jnp.float32,
    )
    sigmoid_gate = jax.nn.sigmoid(gate_part)
    grad_gate = grad_activ * up_part * sigmoid_gate * (1.0 + gate_part * (1.0 - sigmoid_gate))
    grad_up = grad_activ * silu_gate
    grad_gate_up_low = jnp.concatenate([grad_gate, grad_up], axis=1).astype(jnp.bfloat16)
    grad_hidden = grad_out + contract_last(
        grad_gate_up_low, lax.all_gather(gate_up_low, ("dp", "fsdp"), axis=0, tiled=True)
    )
    grad_branch, grad_gain_attn = attn_pull(grad_hidden)
    grad_branch_low = grad_branch.astype(jnp.bfloat16)
    grad_att_low = (
        contract_last(grad_branch_low, attn_full[:, 3 * D :])
        .astype(jnp.bfloat16)
        .reshape(local_rows, HEADS, HEAD_DIM)
    )
    row_delta = jnp.transpose(jnp.sum(grad_att_low.astype(jnp.float32) * attended, axis=-1))
    key_portion = lax.all_gather(key_low, "fsdp", axis=0, tiled=True)
    value_portion = lax.all_gather(value_low, "fsdp", axis=0, tiled=True)
    amount = key_portion.shape[0]
    scores, key_heads = score_block(key_portion)
    value_heads = value_portion.reshape(amount, HEADS, HEAD_DIM)
    prob_vals = jnp.exp(scores - log_total[:, :, None])
    weight_low = jnp.exp(scores - running_max[:, :, None]).astype(jnp.bfloat16)
    grad_probs = jnp.einsum(
        "qhd,khd->hqk", grad_att_low, value_heads, preferred_element_type=jnp.float32
    )
    grad_scores = (prob_vals * (grad_probs - row_delta[:, :, None])).astype(jnp.bfloat16)
    weight_low, grad_scores = (weight_low, grad_scores)
    back_result = (
        jnp.einsum("hqk,khd->qhd", grad_scores, key_heads, preferred_element_type=jnp.float32)
        * scale
    )
    max_all, denom_all, delta_all, first_all = (
        lax.all_gather(jnp.transpose(running_max), "fsdp", axis=0, tiled=True),
        lax.all_gather(jnp.transpose(denom_sum), "fsdp", axis=0, tiled=True),
        lax.all_gather(jnp.transpose(row_delta), "fsdp", axis=0, tiled=True),
        lax.all_gather(first_key.astype(jnp.float32), "fsdp", axis=0, tiled=True),
    )
    own_keys = key_low.reshape(local_rows, HEADS, HEAD_DIM)
    own_values = value_low.reshape(local_rows, HEADS, HEAD_DIM)
    query_portion = lax.all_gather(query_low.reshape(local_rows, D), "fsdp", axis=0, tiled=True)
    grad_portion = lax.all_gather(grad_att_low.reshape(local_rows, D), "fsdp", axis=0, tiled=True)
    amount = query_portion.shape[0]
    query_heads = query_portion.reshape(amount, HEADS, HEAD_DIM)
    grad_heads = grad_portion.reshape(amount, HEADS, HEAD_DIM)
    max_part = jnp.transpose(max_all)
    lse_part = max_part + jnp.log(jnp.transpose(denom_all))
    delta_part = jnp.transpose(delta_all)
    query_first = first_all.astype(jnp.int32)
    query_index = jnp.arange(amount, dtype=jnp.int32)
    scores = (
        jnp.einsum("qhd,khd->hqk", query_heads, own_keys, preferred_element_type=jnp.float32)
        * scale
    )
    allowed = (row_index[None, :] <= query_index[:, None]) & (
        row_index[None, :] >= query_first[:, None]
    )
    scores = jnp.where(allowed[None], scores, neg_large)
    prob_vals = jnp.exp(scores - lse_part[:, :, None])
    weight_low = jnp.exp(scores - max_part[:, :, None]).astype(jnp.bfloat16)
    grad_probs = jnp.einsum(
        "qhd,khd->hqk", grad_heads, own_values, preferred_element_type=jnp.float32
    )
    grad_scores = (prob_vals * (grad_probs - delta_part[:, :, None])).astype(jnp.bfloat16)
    scaled_rows = grad_heads.astype(jnp.float32) / denom_all[:, :, None]
    grad_keys_own = (
        jnp.einsum("hqk,qhd->khd", grad_scores, query_heads, preferred_element_type=jnp.float32)
        * scale
    )
    grad_values_own = value_grad(weight_low, scaled_rows)
    grad_key_local = grad_keys_own.reshape(local_rows, D)
    grad_value_local = grad_values_own.reshape(local_rows, D)

    def prepare_local(qkv_in, gain_query, gain_key):
        return prepare(qkv_in, gain_query, gain_key, cosine, sine_tab)

    unused_out, prepare_pull = jax.vjp(prepare_local, qkv_raw, gain_values[:, 0], gain_values[:, 1])
    grad_qkv, grad_gain_query, grad_gain_key = prepare_pull(
        (back_result.reshape(local_rows, D), grad_key_local, grad_value_local)
    )
    grad_qkv_low = grad_qkv.astype(jnp.bfloat16)
    grad_tokens = grad_hidden + contract_last(grad_qkv_low, attn_full[:, : 3 * D])
    gains_term = jnp.stack([grad_gain_query, grad_gain_key, grad_gain_attn, grad_gain_mlp], axis=1)
    dp_count = lax.axis_size("dp")
    fsdp_count = lax.axis_size("fsdp")
    owned_rows = w_attn.shape[0]
    fsdp_place = lax.axis_index("fsdp")

    def picked_rows(portion):
        amount = portion.shape[0]
        return lax.dynamic_index_in_dim(
            portion.reshape(amount, dp_count, fsdp_count, owned_rows), fsdp_place, 2, keepdims=False
        )

    def outer_rows(left, right):
        return jnp.einsum(
            "npr,nc->prc", picked_rows(left), right, preferred_element_type=jnp.float32
        )

    token_p = lax.all_gather(tokens, "fsdp", axis=0, tiled=True)
    dqkv_p = lax.all_gather(grad_qkv_low, "fsdp", axis=0, tiled=True)
    attended_p = lax.all_gather(attended_low, "fsdp", axis=0, tiled=True)
    dz_p = lax.all_gather(grad_branch_low, "fsdp", axis=0, tiled=True)
    hidden_p = lax.all_gather(hidden_low, "fsdp", axis=0, tiled=True)
    dau_p = lax.all_gather(grad_gate_up_low, "fsdp", axis=0, tiled=True)
    dm_p = lax.all_gather(grad_mlp_low, "fsdp", axis=0, tiled=True)
    activ_p = lax.all_gather(activ_low, "fsdp", axis=0, tiled=True)
    attn_sum = jnp.concatenate([outer_rows(token_p, dqkv_p), outer_rows(attended_p, dz_p)], axis=2)
    gate_up_sum = outer_rows(hidden_p, dau_p)
    down_sum = outer_rows(dm_p, activ_p)
    attn_part, gate_up_part, down_part = (
        lax.psum_scatter(attn_sum, "dp", scatter_dimension=0, tiled=True),
        lax.psum_scatter(gate_up_sum, "dp", scatter_dimension=0, tiled=True),
        lax.psum_scatter(down_sum, "dp", scatter_dimension=0, tiled=True),
    )
    grad_attn = attn_part.reshape(owned_rows, 4 * D)
    grad_gate_up = gate_up_part.reshape(owned_rows, 2 * FF)
    grad_down = down_part.reshape(owned_rows, FF)
    grad_gains = lax.psum_scatter(gains_term, ("dp", "fsdp"), scatter_dimension=0, tiled=True)
    new_attn, new_m_attn, new_v_attn = adamw_step(
        w_attn, grad_attn, m_attn, v_attn, decay_rate, learn_rate
    )
    new_gate_up, new_m_gate_up, new_v_gate_up = adamw_step(
        w_gate_up, grad_gate_up, m_gate_up, v_gate_up, decay_rate, learn_rate
    )
    new_down, new_m_down, new_v_down = adamw_step(
        w_down, grad_down, m_down, v_down, decay_rate, learn_rate
    )
    new_gains, new_m_gains, new_v_gains = adamw_step(
        gains, grad_gains, m_gains, v_gains, 0.0, gain_rate
    )
    return (
        output,
        grad_tokens,
        grad_attn,
        grad_gate_up,
        grad_down,
        grad_gains,
        new_attn,
        new_gate_up,
        new_down,
        new_gains,
        new_m_attn,
        new_v_attn,
        new_m_gate_up,
        new_v_gate_up,
        new_m_down,
        new_v_down,
        new_m_gains,
        new_v_gains,
    )


def solution(mesh):
    in_specs = (
        P(("dp", "fsdp"), None),
        P(("dp", "fsdp")),
        P(("dp", "fsdp"), None),
        P(("dp", "fsdp"), None),
        P(("dp", "fsdp"), None),
        P(("dp", "fsdp"), None),
        P(("dp", "fsdp"), None),
        P(("dp", "fsdp"), None),
        P(("dp", "fsdp"), None),
        P(("dp", "fsdp"), None),
        P(("dp", "fsdp"), None),
        P(("dp", "fsdp"), None),
        P(("dp", "fsdp"), None),
        P(("dp", "fsdp"), None),
        P(("dp", "fsdp"), None),
    )
    out_specs = (
        P(("dp", "fsdp"), None),
        P(("dp", "fsdp"), None),
        P(("dp", "fsdp"), None),
        P(("dp", "fsdp"), None),
        P(("dp", "fsdp"), None),
        P(("dp", "fsdp"), None),
        P(("dp", "fsdp"), None),
        P(("dp", "fsdp"), None),
        P(("dp", "fsdp"), None),
        P(("dp", "fsdp"), None),
        P(("dp", "fsdp"), None),
        P(("dp", "fsdp"), None),
        P(("dp", "fsdp"), None),
        P(("dp", "fsdp"), None),
        P(("dp", "fsdp"), None),
        P(("dp", "fsdp"), None),
        P(("dp", "fsdp"), None),
        P(("dp", "fsdp"), None),
    )
    return jax.shard_map(
        per_device, mesh=mesh, in_specs=in_specs, out_specs=out_specs, check_vma=False
    )
```

profile of v0, /device:TPU:0, one launch (start us, length us, event | category | flops | bytes accessed | tf_op | source)
XLA Modules:
  0.0 2708.3 jit_solution(15565976438542855199)
XLA Ops:
  10.1 70.8 %all-gather = bf16[32,64,4]{1,2,0:T(4,128)(2,1)S(1)} all-gather(bf16[1,64,4]{1,2,0:T(4,128)(2,1)S(1)} %convert_bitcast_fusion), channel_id=1, replica_groups=mesh['dp'=8,'fsdp'=4] {'dp','fsdp'}, dimensions={0}, use_global_device_ids=true | all-gather | bytes 16896 | tf_op jit(solution)/shard_map/all_gather | solution.py:117
  82.2 127.1 %all-gather.18.cloned.1.call-done = bf16[2048,8192]{1,0:T(8,128)(2,1)} async-done(((bf16[64,8192]{1,0:T(8,128)(2,1)}), bf16[2048,8192]{1,0:T(8,128)(2,1)}) %all-gather.18.cloned.1.call-update) | async-done | bytes 33554448 | tf_op jit(solution)/shard_map/all_gather | solution.py:116
  209.3 11.6 fusion.4
  245.3 37.3 %all-gather.22.cloned.1.call-done = bf16[1024,2048]{0,1:T(8,128)(2,1)} async-done(((bf16[256,2048]{0,1:T(8,128)(2,1)}), bf16[1024,2048]{0,1:T(8,128)(2,1)}) %all-gather.22.cloned.1.call-update) | async-done | bytes 4194320 | tf_op jit(solution)/shard_map/all_gather | solution.py:146
  287.6 6.5 copy-done
  298.6 39.1 %all-gather.20.cloned.1.call-done = bf16[1024,2048]{1,0:T(8,128)(2,1)} async-done(((bf16[256,2048]{1,0:T(8,128)(2,1)}), bf16[1024,2048]{1,0:T(8,128)(2,1)}) %all-gather.20.cloned.1.call-update) | async-done | bytes 4194320 | tf_op jit(solution)/shard_map/all_gather | solution.py:147
  337.7 11.3 fusion.108
  349.0 7.4 multiply_reduce_fusion.6
  358.2 339.2 %all-gather.24.cloned.1.call-done = bf16[2048,16384]{1,0:T(8,128)(2,1)} async-done(((bf16[64,16384]{1,0:T(8,128)(2,1)}), bf16[2048,16384]{1,0:T(8,128)(2,1)}) %all-gather.24.cloned.1.call-update) | async-done | bytes 67108880 | tf_op jit(solution)/shard_map/all_gather | solution.py:171
  697.3 32.8 %fusion.109 = f32[256,16384]{1,0:T(8,128)} fusion(bf16[256,2048]{1,0:T(8,128)(2,1)S(1)} %fusion.65, bf16[2048,16384]{1,0:T(8,128)(2,1)} %all-gather.24.cloned.1.call-done), kind=kOutput, calls=%fused_computation.177 | convolution fusion | flops 17179869184 | bytes 84934656 | tf_op jit(solution)/shard_map/dot_general | solution.py:169
  730.1 9.1 multiply_convert_fusion.4
  739.2 154.5 %all-gather.26.cloned.1.call-done = bf16[2048,8192]{1,0:T(8,128)(2,1)} async-done(((bf16[64,8192]{1,0:T(8,128)(2,1)}), bf16[2048,8192]{1,0:T(8,128)(2,1)}) %all-gather.26.cloned.1.call-update) | async-done | bytes 33554448 | tf_op jit(solution)/shard_map/all_gather | solution.py:179
  893.6 16.3 multiply_reduce_fusion.5
  912.8 23.2 multiply_convert_fusion.3
  936.0 30.4 %multiply_reduce_fusion = (f32[2048]{0:T(1024)S(1)}, f32[256]{0:T(256)S(1)}, f32[256,2048]{1,0:T(8,128)}) fusion(f32[256,2048]{1,0:T(8,128)} %copy-done.8, f32[256]{0:T(256)S(1)} %fusion.87, f32[2048]{0:T(1024)S(1)} %bitcast.192, bf16[2048,16384]{1,0:T(8,128)(2,1)} %all-gather.24.cloned.1.call-done, bf16[256,8192]{1,0:T(8,128)(2,1)} %get-tuple-element.45, ...), kind=kOutput, calls=%fused_computation.87 | convolution fusion | flops 17200838656 | bytes 80758784 | tf_op jit(solution)/shard_map/dot_general | solution.py:65
  971.0 7.1 fusion.42
  982.4 8.2 all-gather.1
  990.9 8.2 all_gather.71
  999.2 7.8 all_gather.74
  1007.0 10.4 fusion.110
  1019.8 8.2 all_gather.75
  1028.0 13.2 multiply_bitcast_fusion
  1041.2 6.4 copy.135
  1047.6 12.9 fusion.15
  1063.1 15.7 multiply_bitcast_fusion.1
  1092.5 9.3 pad_maximum_fusion.1
  1103.9 6.8 copy.121
  1110.8 135.2 %all-gather.46.cloned.1.call-done = bf16[1024,8192]{1,0:T(8,128)(2,1)} async-done(((bf16[256,8192]{1,0:T(8,128)(2,1)}), bf16[1024,8192]{1,0:T(8,128)(2,1)}) %all-gather.46.cloned.1.call-update) | async-done | bytes 16777232 | tf_op jit(solution)/shard_map/all_gather | solution.py:297
  1245.9 15.8 fusion.6
  1261.8 39.0 %all-gather.36.cloned.1.call-done = bf16[1024,2048]{0,1:T(8,128)(2,1)} async-done(((bf16[256,2048]{0,1:T(8,128)(2,1)}), bf16[1024,2048]{0,1:T(8,128)(2,1)}) %all-gather.36.cloned.1.call-update) | async-done | bytes 4194320 | tf_op jit(solution)/shard_map/all_gather | solution.py:292
  1300.8 55.2 %all-gather.38.cloned.1.call-done = bf16[1024,2048]{1,0:T(8,128)(2,1)} async-done(((bf16[256,2048]{1,0:T(8,128)(2,1)}), bf16[1024,2048]{1,0:T(8,128)(2,1)}) %all-gather.38.cloned.1.call-update) | async-done | bytes 4194320 | tf_op jit(solution)/shard_map/all_gather | solution.py:293
  1356.0 6.9 fusion.34
  1362.8 47.4 %all-gather.32.cloned.1.call-done = bf16[1024,2048]{0,1:T(8,128)(2,1)} async-done(((bf16[256,2048]{0,1:T(8,128)(2,1)}), bf16[1024,2048]{0,1:T(8,128)(2,1)}) %all-gather.32.cloned.1.call-update) | async-done | bytes 4194320 | tf_op jit(solution)/shard_map/all_gather | solution.py:290
  1410.2 125.0 %all-gather.34.cloned.1.call-done = bf16[1024,6144]{1,0:T(8,128)(2,1)} async-done(((bf16[256,6144]{1,0:T(8,128)(2,1)}), bf16[1024,6144]{1,0:T(8,128)(2,1)}) %all-gather.34.cloned.1.call-update) | async-done | bytes 12582928 | tf_op jit(solution)/shard_map/all_gather | solution.py:291
  1535.2 9.7 fusion.10
  1544.9 6.2 pad_maximum_fusion
  1551.2 38.5 %all-gather.40.cloned.1.call-done = bf16[1024,2048]{1,0:T(8,128)(2,1)} async-done(((bf16[256,2048]{1,0:T(8,128)(2,1)}), bf16[1024,2048]{1,0:T(8,128)(2,1)}) %all-gather.40.cloned.1.call-update) | async-done | bytes 4194320 | tf_op jit(solution)/shard_map/all_gather | solution.py:294
  1589.6 6.5 copy.120
  1596.2 292.4 %all-gather.42.cloned.1.call-done = bf16[1024,16384]{1,0:T(8,128)(2,1)} async-done(((bf16[256,16384]{1,0:T(8,128)(2,1)}), bf16[1024,16384]{1,0:T(8,128)(2,1)}) %all-gather.42.cloned.1.call-update) | async-done | bytes 33554448 | tf_op jit(solution)/shard_map/all_gather | solution.py:295
  1888.6 31.6 %fusion = f32[8,64,16384]{2,1,0:T(8,128)} fusion(bf16[1024,16384]{1,0:T(8,128)(2,1)} %all-gather.42.cloned.1.call-done, bf16[1024,8,4,64]{0,3,2,1:T(8,128)(2,1)} %bitcast.168, s32[]{:T(128)S(6)} %select_n.18), kind=kOutput, calls=%fused_computation | convolution fusion | flops 17179869184 | bytes 68157440 | tf_op jit(solution)/shard_map/npr,nc->prc/dot_general | solution.py:286
  1922.0 13.2 fusion.39
  1935.2 90.9 %reduce-scatter.13.cloned.1.call-done = f32[64,4]{1,0:T(8,128)} async-done(((f32[2048,4]{1,0:T(8,128)}), f32[64,4]{1,0:T(8,128)}) %reduce-scatter.13.cloned.1.call-update) | async-done | bytes 1040
  2027.6 166.0 %reduce-scatter.11.cloned.1.call-done = f32[1,64,8192]{2,1,0:T(8,128)} async-done(((f32[8,64,8192]{2,1,0:T(8,128)}), f32[1,64,8192]{2,1,0:T(8,128)}) %reduce-scatter.11.cloned.1.call-update) | async-done | bytes 2097168 | tf_op jit(solution)/shard_map/reduce_scatter | solution.py:304
  2193.6 7.1 multiply_subtract_fusion.1
  2200.8 162.4 %reduce-scatter.7.cloned.1.call-done = f32[1,64,8192]{2,1,0:T(8,128)} async-done(((f32[8,64,8192]{2,1,0:T(8,128)}), f32[1,64,8192]{2,1,0:T(8,128)}) %reduce-scatter.7.cloned.1.call-update) | async-done | bytes 2097168 | tf_op jit(solution)/shard_map/reduce_scatter | solution.py:302
  2363.2 6.5 multiply_subtract_fusion.2
  2369.7 320.5 %reduce-scatter.9.cloned.1.call-done = f32[1,64,16384]{2,1,0:T(8,128)} async-done(((f32[8,64,16384]{2,1,0:T(8,128)}), f32[1,64,16384]{2,1,0:T(8,128)}) %reduce-scatter.9.cloned.1.call-update) | async-done | bytes 4194320 | tf_op jit(solution)/shard_map/reduce_scatter | solution.py:303
  2690.2 11.5 multiply_subtract_fusion
  (183 shorter events, 75.4 us)
Async XLA Ops:
  7.2 73.8 %copy-start.41 = (s32[256]{0:T(256)S(1)}, s32[256]{0:T(256)}, u32[]{:S(2)}) copy-start(s32[256]{0:T(256)} %param.16) | copy-start | bytes 3076
  7.2 202.1 %copy-start.3 = (bf16[256,2048]{1,0:T(8,128)(2,1)S(1)}, bf16[256,2048]{1,0:T(8,128)(2,1)}, u32[]{:S(2)}) copy-start(bf16[256,2048]{1,0:T(8,128)(2,1)} %param.15) | copy-start | bytes 3145732
  7.2 202.1 %all-gather.18.cloned.1.call-start = ((), (), s32[]{:S(2)}) async-start(), calls=%async_computation.4 | async-start | bytes 34603008 | tf_op jit(solution)/shard_map/all_gather | solution.py:116
  10.0 272.5 %all-gather.22.cloned.1.call-start = ((), (), s32[]{:S(2)}) async-start(), calls=%async_computation.6 | async-start | bytes 5242880 | tf_op jit(solution)/shard_map/all_gather | solution.py:146
  82.1 143.5 %copy-start.13 = (f32[256,64]{1,0:T(8,128)}, f32[256,64]{1,0:T(8,128)S(1)}, u32[]{:S(2)}) copy-start(f32[256,64]{1,0:T(8,128)S(1)} %get-tuple-element.74) | copy-start | bytes 196612
  82.2 143.5 %copy-start.15 = (f32[256,64]{1,0:T(8,128)}, f32[256,64]{1,0:T(8,128)S(1)}, u32[]{:S(2)}) copy-start(f32[256,64]{1,0:T(8,128)S(1)} %get-tuple-element.75) | copy-start | bytes 196612
  82.2 139.9 %copy-start.20 = (f32[2048,1]{0,1:T(1,128)}, f32[2048,1]{0,1:T(1,128)S(1)}, u32[]{:S(2)}) copy-start(f32[2048,1]{0,1:T(1,128)S(1)} %get-tuple-element.70) | copy-start | bytes 24580
  82.2 139.9 %copy-start.22 = (f32[2048,1]{0,1:T(1,128)}, f32[2048,1]{0,1:T(1,128)S(1)}, u32[]{:S(2)}) copy-start(f32[2048,1]{0,1:T(1,128)S(1)} %get-tuple-element.71) | copy-start | bytes 24580
  230.3 4.1 copy-start.4
  231.7 106.1 %all-gather.20.cloned.1.call-start = ((), (), s32[]{:S(2)}) async-start(), calls=%async_computation.5 | async-start | bytes 5242880 | tf_op jit(solution)/shard_map/all_gather | solution.py:147
  234.4 462.9 %all-gather.24.cloned.1.call-start = ((), (), s32[]{:S(2)}) async-start(), calls=%async_computation.7 | async-start | bytes 69206016 | tf_op jit(solution)/shard_map/all_gather | solution.py:171
  238.4 655.2 %all-gather.26.cloned.1.call-start = ((), (), s32[]{:S(2)}) async-start(), calls=%async_computation.8 | async-start | bytes 34603008 | tf_op jit(solution)/shard_map/all_gather | solution.py:179
  241.1 765.8 %all-gather.30.cloned.1.call-start = ((), (), s32[]{:S(2)}) async-start(), calls=%async_computation.10 | async-start | bytes 5242880 | tf_op jit(solution)/shard_map/all_gather | solution.py:231
  245.1 796.1 %all-gather.28.cloned.1.call-start = ((), (), s32[]{:S(2)}) async-start(), calls=%async_computation.9 | async-start | bytes 5242880 | tf_op jit(solution)/shard_map/all_gather | solution.py:232
  287.6 6.5 copy-start
  287.6 11.0 copy-start.18
  349.0 7.4 copy-start.17
  358.2 371.9 %copy-start.9 = (bf16[256,2048]{1,0:T(8,128)(2,1)}, bf16[256,2048]{1,0:T(8,128)(2,1)S(1)}, u32[]{:S(2)}) copy-start(bf16[256,2048]{1,0:T(8,128)(2,1)S(1)} %fusion.65) | copy-start | bytes 3145732
  893.6 16.3 copy-start.11
  978.1 125.8 %all-gather.44.cloned.1.call-start = ((), (), s32[]{:S(2)}) async-start(), calls=%async_computation.19 | async-start | bytes 5242880 | tf_op jit(solution)/shard_map/all_gather | solution.py:296
  978.8 267.1 %all-gather.46.cloned.1.call-start = ((), (), s32[]{:S(2)}) async-start(), calls=%async_computation.20 | async-start | bytes 20971520 | tf_op jit(solution)/shard_map/all_gather | solution.py:297
  979.6 321.2 %all-gather.36.cloned.1.call-start = ((), (), s32[]{:S(2)}) async-start(), calls=%async_computation.13 | async-start | bytes 5242880 | tf_op jit(solution)/shard_map/all_gather | solution.py:292
  980.2 10.5 copy-start.37
  980.2 10.7 copy-start.19
  980.2 26.8 copy-start.5
  980.2 375.7 %all-gather.38.cloned.1.call-start = ((), (), s32[]{:S(2)}) async-start(), calls=%async_computation.14 | async-start | bytes 5242880 | tf_op jit(solution)/shard_map/all_gather | solution.py:293
  980.9 429.3 %all-gather.32.cloned.1.call-start = ((), (), s32[]{:S(2)}) async-start(), calls=%async_computation.11 | async-start | bytes 5242880 | tf_op jit(solution)/shard_map/all_gather | solution.py:290
  982.3 552.9 %all-gather.34.cloned.1.call-start = ((), (), s32[]{:S(2)}) async-start(), calls=%async_computation.12 | async-start | bytes 15728640 | tf_op jit(solution)/shard_map/all_gather | solution.py:291
  1007.0 10.4 copy-start.10
  1063.1 15.7 copy-start.14
  1063.1 15.7 copy-start.16
  1078.8 4.9 copy-start.21
  1078.8 4.9 copy-start.23
  1078.8 4.9 copy-start.26
  1078.8 4.9 copy-start.28
  1083.8 4.1 slice-start.1
  1091.8 497.8 %all-gather.40.cloned.1.call-start = ((), (), s32[]{:S(2)}) async-start(), calls=%async_computation.16 | async-start | bytes 5242880 | tf_op jit(solution)/shard_map/all_gather | solution.py:294
  1092.4 796.1 %all-gather.42.cloned.1.call-start = ((), (), s32[]{:S(2)}) async-start(), calls=%async_computation.17 | async-start | bytes 41943040 | tf_op jit(solution)/shard_map/all_gather | solution.py:295
  1101.8 924.4 %reduce-scatter.13.cloned.1.call-start = ((), (), s32[]{:S(2)}) async-start(), calls=%async_computation.22 | async-start | bytes 1081344
  1103.8 1089.8 %reduce-scatter.11.cloned.1.call-start = ((), (), s32[]{:S(2)}) async-start(), calls=%async_computation.21 | async-start | bytes 18874368 | tf_op jit(solution)/shard_map/reduce_scatter | solution.py:304
  1261.8 1101.4 %reduce-scatter.7.cloned.1.call-start = ((), (), s32[]{:S(2)}) async-start(), calls=%async_computation.15 | async-start | bytes 18874368 | tf_op jit(solution)/shard_map/reduce_scatter | solution.py:302
  1535.2 9.7 copy-start.12
  1551.1 1139.0 %reduce-scatter.9.cloned.1.call-start = ((), (), s32[]{:S(2)}) async-start(), calls=%async_computation.18 | async-start | bytes 37748736 | tf_op jit(solution)/shard_map/reduce_scatter | solution.py:303
  1922.0 104.9 %copy-start.35 = (f32[64,4]{0,1:T(4,128)S(1)}, f32[64,4]{0,1:T(4,128)}, u32[]{:S(2)}) copy-start(f32[64,4]{0,1:T(4,128)} %param.21) | copy-start | bytes 3076
  1922.0 104.9 %copy-start.39 = (f32[64,4]{0,1:T(4,128)S(1)}, f32[64,4]{0,1:T(4,128)}, u32[]{:S(2)}) copy-start(f32[64,4]{0,1:T(4,128)} %param.28) | copy-start | bytes 3076
  1922.0 104.9 %copy-start.40 = (f32[64,4]{0,1:T(4,128)S(1)}, f32[64,4]{0,1:T(4,128)}, u32[]{:S(2)}) copy-start(f32[64,4]{0,1:T(4,128)} %param.29) | copy-start | bytes 3076
  2027.0 173.8 %copy-start.33 = (f32[64,4]{0,1:T(4,128)}, f32[64,4]{0,1:T(4,128)S(1)}, u32[]{:S(2)}) copy-start(f32[64,4]{0,1:T(4,128)S(1)} %copy.129) | copy-start | bytes 3076
  2027.6 335.6 %copy-start.7 = (f32[64,8192]{1,0:T(8,128)S(1)}, f32[64,8192]{1,0:T(8,128)}, u32[]{:S(2)}) copy-start(f32[64,8192]{1,0:T(8,128)} %param.18) | copy-start | bytes 6291460
  (15 other events, 34.6 us)
Sparse Core Ops, SparseCore 0:
  11.5 197.7 all-gather.17
  231.8 50.7 all-gather.21
  285.0 52.6 all-gather.19
  341.0 356.2 all-gather.23
  700.6 192.9 all-gather.25
  895.9 50.7 all-gather.29
  978.2 52.6 all-gather.27
  1033.3 52.6 all-gather.43
  1088.5 157.4 all-gather.45
  1248.2 52.5 all-gather.35
  1303.2 52.6 all-gather.37
  1357.6 52.5 all-gather.31
  1412.6 122.5 all-gather.33
  1536.9 52.6 all-gather.39
  1591.3 297.2 all-gather.41
  1891.2 134.8 reduce-scatter.12
  2029.0 164.5 reduce-scatter.10
  2196.5 166.6 reduce-scatter.6
  2366.2 323.8 reduce-scatter.8
where the time goes:
time: 2720 us; the launch traced here: 2710 us
  waiting for transfers between devices  2170 us (80%)
  matrix products  274 us (10%)
  blocking collectives  103 us (4%)
  other arithmetic  94 us (3%)
  local copies, waits for them, and re-layouts  48.1 us (2%)
    all_gather x1, waiting for transfers between devices, per_device(): lax.all_gather(gate_up_low, ('dp', 'fsdp'), axis=0, tiled=True)  339 us
    reduce_scatter x1, waiting for transfers between devices, per_device(): lax.psum_scatter(gate_up_sum, 'dp', scatter_dimension=0, tiled=True)  320 us
    all_gather x1, waiting for transfers between devices, per_device(): dau_p = lax.all_gather(grad_gate_up_low, 'fsdp', axis=0, tiled=True)  292 us
    reduce_scatter x1, waiting for transfers between devices, per_device(): lax.psum_scatter(down_sum, 'dp', scatter_dimension=0, tiled=True)  166 us
    reduce_scatter x1, waiting for transfers between devices, per_device(): lax.psum_scatter(attn_sum, 'dp', scatter_dimension=0, tiled=True)  162 us
    all_gather x1, waiting for transfers between devices, per_device(): lax.all_gather(down_low, ('dp', 'fsdp'), axis=0, tiled=True)  154 us
    all_gather x1, waiting for transfers between devices, per_device(): activ_p = lax.all_gather(activ_low, 'fsdp', axis=0, tiled=True)  135 us
    all_gather x1, waiting for transfers between devices, per_device(): lax.all_gather(attn_low, ('dp', 'fsdp'), axis=0, tiled=True)  127 us
  transfers between devices with their start and end apart: 19, of which 16 were waited for; matrix products, arithmetic and copies ran while one was open for 14% of the time, Pallas kernels for 0%

commit v1 on v0

v1 whole, which is shorter than its diff:
```python
import math

import jax
import jax.numpy as jnp
from jax import lax
from jax.sharding import PartitionSpec as P

HEAD_DIM = 128

norm_eps = 1e-06
rope_base = 500000.0
learn_rate = 0.004
gain_rate = 0.25
beta_one = 0.9
beta_two = 0.95
decay_rate = 0.1
adam_eps = 1e-08
correct_one = 1.0 - beta_one**2
correct_two = 1.0 - beta_two**2
neg_large = -1e30
bf16 = jnp.bfloat16
f32 = jnp.float32
GAIN_COLS = 128


def mm(left, right, dims):
    return lax.dot_general(left, right, (dims, ((), ())), preferred_element_type=f32)


def rotate(values, cosine, sine_tab):
    half_dim = values.shape[-1] // 2
    first_half = values[..., :half_dim]
    second_half = values[..., half_dim:]
    return jnp.concatenate(
        [
            first_half * cosine - second_half * sine_tab,
            second_half * cosine + first_half * sine_tab,
        ],
        axis=-1,
    )


def adamw_step(weight, gradient, moment, second, decay_coef, rate_value):
    moment_new = beta_one * moment + (1.0 - beta_one) * gradient
    second_new = beta_two * second + (1.0 - beta_two) * gradient * gradient
    step_ratio = moment_new / correct_one / (jnp.sqrt(second_new / correct_two) + adam_eps)
    return (
        weight * (1.0 - rate_value * decay_coef) - rate_value * step_ratio,
        moment_new,
        second_new,
    )


class Plane:
    def __init__(self, count):
        self.count = count
        self.square = count == 4
        self.place = lax.axis_index("fsdp")

    def swap(self, values, bit):
        return lax.ppermute(values, "fsdp", [(i, i ^ bit) for i in range(self.count)])

    def gather(self, block, axis):
        if not self.square:
            return lax.all_gather(block, "fsdp", axis=axis, tiled=True)
        other = 1 - axis
        size, cut = block.shape[axis], block.shape[other] // 2
        by_x, by_y = self.swap(block, 1), self.swap(block, 2)
        low = self.swap(lax.slice_in_dim(by_x, 0, cut, axis=other), 2)
        high = self.swap(lax.slice_in_dim(by_y, cut, 2 * cut, axis=other), 1)
        shape = list(block.shape)
        shape[axis] = size * 4
        out = jnp.zeros(shape, block.dtype)
        for part, bit, offset in ((block, 0, 0), (by_x, 1, 0), (by_y, 2, 0), (low, 3, 0), (high, 3, cut)):
            start = [0, 0]
            start[axis] = (self.place ^ bit) * size
            start[other] = offset
            out = lax.dynamic_update_slice(out, part, start)
        return out

    def scatter(self, partial, axis):
        if not self.square:
            return lax.psum_scatter(
                partial, "fsdp", scatter_dimension=axis, tiled=True
            ).astype(f32)
        other = 1 - axis
        size, cut = partial.shape[axis] // 4, partial.shape[other] // 2
        place = self.place

        def piece(bit, offset):
            start = [0, 0]
            start[axis] = (place ^ bit) * size
            start[other] = offset
            extent = [0, 0]
            extent[axis] = size
            extent[other] = cut
            return lax.dynamic_slice(partial, start, extent)

        halves = []
        for offset, first, second in ((0, 1, 2), (cut, 2, 1)):
            mine = self.swap(piece(first, offset), first)
            relay = self.swap(piece(3, offset), first)
            relay = (piece(second, offset).astype(f32) + relay.astype(f32)).astype(bf16)
            halves.append(
                piece(0, offset).astype(f32) + mine.astype(f32) + self.swap(relay, second).astype(f32)
            )
        return jnp.concatenate(halves, axis=other)

    def total(self, values):
        if not self.square:
            return lax.psum(values, "fsdp")
        return values + self.swap(values, 1) + self.swap(values, 2) + self.swap(values, 3)

    def gather_small(self, values):
        if not self.square:
            return lax.all_gather(values, "fsdp", axis=0, tiled=True)
        parts = [values] + [self.swap(values, bit) for bit in (1, 2, 3)]
        return jnp.concatenate(
            [
                lax.select_n(self.place ^ j, *parts)
                for j in range(4)
            ],
            axis=0,
        )


def per_device(
    tokens,
    positions,
    cotangent,
    w_attn,
    w_gate_up,
    w_down,
    gains,
    m_attn,
    v_attn,
    m_gate_up,
    v_gate_up,
    m_down,
    v_down,
    m_gains,
    v_gains,
):
    rows, width = tokens.shape
    owned = w_attn.shape[0]
    hidden = w_down.shape[1]
    count = lax.axis_size("fsdp")
    plane = Plane(count)
    place = plane.place
    length = rows * count
    part = width // count
    heads = part // HEAD_DIM
    wide = hidden // count
    scale = 1.0 / math.sqrt(HEAD_DIM)

    def spread(weight, groups, extra=None):
        columns = weight.shape[1] // (groups * count)
        block = (
            weight.astype(bf16)
            .reshape(owned, groups, count, columns)
            .transpose(2, 0, 1, 3)
            .reshape(count, owned, groups * columns)
        )
        if extra is not None:
            block = jnp.concatenate(
                [block, jnp.broadcast_to(extra[None], (count,) + extra.shape)], axis=2
            )
        block = block.reshape(count * owned, block.shape[2])
        return lax.all_to_all(block, "fsdp", 0, 0, tiled=True)

    gain_block = jnp.pad(gains.astype(bf16), ((0, 0), (0, GAIN_COLS - gains.shape[1])))
    attn_all = lax.all_gather(spread(w_attn, 4, gain_block), "dp", axis=0, tiled=True)
    gate_up_all = lax.all_gather(spread(w_gate_up, 2), "dp", axis=0, tiled=True)
    down_all = lax.all_gather(spread(w_down, 1), "dp", axis=0, tiled=True)
    qkv_weight = attn_all[:, : 3 * part]
    out_weight = attn_all[:, 3 * part : 4 * part]
    gain_values = attn_all[:, 4 * part : 4 * part + 4].astype(f32)
    gain_part = lax.dynamic_slice_in_dim(gain_values, place * part, part, 0)

    token_full = plane.gather(tokens, 0)
    position_full = plane.gather_small(positions)
    cot_part = lax.all_to_all(
        cotangent.reshape(rows, count, part).transpose(1, 0, 2).reshape(count * rows, part),
        "fsdp",
        0,
        0,
        tiled=True,
    ).astype(f32)

    half_dim = HEAD_DIM // 2
    frequency = jnp.exp(
        jnp.arange(half_dim, dtype=f32) * (-2.0 * math.log(rope_base) / HEAD_DIM)
    )
    angles = position_full.astype(f32)[:, None] * frequency[None, :]
    cosine, sine_tab = jnp.cos(angles)[:, None, :], jnp.sin(angles)[:, None, :]
    row_index = jnp.arange(length, dtype=jnp.int32)
    first_key = row_index - position_full
    allowed = (row_index[None, :] <= row_index[:, None]) & (
        row_index[None, :] >= first_key[:, None]
    )

    qkv = mm(token_full, qkv_weight, ((1,), (0,)))
    query_raw, key_raw, value_raw = qkv[:, :part], qkv[:, part : 2 * part], qkv[:, 2 * part :]
    squares = plane.total(
        jnp.stack([jnp.sum(query_raw * query_raw, axis=1), jnp.sum(key_raw * key_raw, axis=1)])
    )
    inverse = lax.rsqrt(squares / width + norm_eps)
    query_inv, key_inv = inverse[0][:, None], inverse[1][:, None]
    query_hat, key_hat = query_raw * query_inv, key_raw * key_inv

    def turned(values, gain):
        return (
            rotate((values * gain[None, :]).reshape(length, heads, HEAD_DIM), cosine, sine_tab)
            .astype(bf16)
        )

    query = turned(query_hat, gain_part[:, 0])
    key = turned(key_hat, gain_part[:, 1])
    value = value_raw.astype(bf16).reshape(length, heads, HEAD_DIM)

    def score():
        scores = jnp.einsum("qhd,khd->hqk", query, key, preferred_element_type=f32) * scale
        return jnp.where(allowed[None], scores, neg_large)

    scores = score()
    top = jnp.max(scores, axis=-1)
    weights = jnp.exp(scores - top[:, :, None])
    denom = jnp.sum(weights, axis=-1)
    attended = jnp.einsum(
        "hqk,khd->qhd", weights.astype(bf16), value, preferred_element_type=f32
    ) / jnp.transpose(denom)[:, :, None]
    attended_low = attended.reshape(length, part).astype(bf16)
    attended_full = plane.gather(attended_low, 1)

    branch = mm(attended_full, out_weight, ((1,), (0,)))
    branch_inv = lax.rsqrt(plane.total(jnp.sum(branch * branch, axis=1)) / width + norm_eps)[:, None]
    branch_hat = branch * branch_inv
    token_part = lax.dynamic_slice_in_dim(token_full, place * part, part, 1).astype(f32)
    hidden_low = (token_part + branch_hat * gain_part[None, :, 2]).astype(bf16)
    hidden_full = plane.gather(hidden_low, 1)

    gate_up = mm(hidden_full, gate_up_all, ((1,), (0,)))
    gate, up = gate_up[:, :wide], gate_up[:, wide:]
    activ = (jax.nn.silu(gate) * up).astype(bf16)
    mlp = plane.scatter(mm(activ, down_all, ((1,), (1,))).astype(bf16), 0)
    mlp_inv = lax.rsqrt(jnp.mean(mlp * mlp, axis=1, keepdims=True) + norm_eps)
    mlp_hat = mlp * mlp_inv
    hidden_rows = lax.dynamic_slice_in_dim(hidden_full, place * rows, rows, 0).astype(f32)
    output = (hidden_rows + mlp_hat * gain_values[None, :, 3]).astype(bf16)

    grad_out = cotangent.astype(f32)
    scaled = grad_out * gain_values[None, :, 3]
    grad_mlp = mlp_inv * (scaled - mlp_hat * jnp.mean(scaled * mlp_hat, axis=1, keepdims=True))
    grad_gain_mlp = jnp.sum(grad_out * mlp_hat, axis=0)
    grad_mlp_full = plane.gather(grad_mlp.astype(bf16), 0)

    def reduced(partial, groups):
        mine = lax.psum_scatter(partial, "dp", scatter_dimension=0, tiled=True)
        got = lax.all_to_all(mine, "fsdp", 0, 0, tiled=True)
        columns = partial.shape[1] // groups
        return (
            got.reshape(count, owned, groups, columns)
            .transpose(1, 2, 0, 3)
            .reshape(owned, groups * count * columns)
            .astype(f32)
        )

    grad_down = reduced(mm(grad_mlp_full, activ, ((0,), (0,))).astype(bf16), 1)
    grad_activ = mm(grad_mlp_full, down_all, ((1,), (0,)))
    sigmoid = jax.nn.sigmoid(gate)
    grad_gate = grad_activ * up * sigmoid * (1.0 + gate * (1.0 - sigmoid))
    grad_up = grad_activ * (gate * sigmoid)
    grad_gate_up_low = jnp.concatenate([grad_gate, grad_up], axis=1).astype(bf16)
    grad_gate_up = reduced(mm(hidden_full, grad_gate_up_low, ((0,), (0,))).astype(bf16), 2)
    grad_hidden = cot_part + plane.scatter(
        mm(grad_gate_up_low, gate_up_all, ((1,), (1,))).astype(bf16), 1
    )

    scaled = grad_hidden * gain_part[None, :, 2]
    grad_gain_attn = jnp.sum(grad_hidden * branch_hat, axis=0)
    inner = plane.total(jnp.sum(scaled * branch_hat, axis=1))[:, None] / width
    grad_branch = (branch_inv * (scaled - branch_hat * inner)).astype(bf16)
    grad_out_weight = mm(attended_full, grad_branch, ((0,), (0,))).astype(bf16)
    grad_att = (
        plane.scatter(mm(grad_branch, out_weight, ((1,), (1,))).astype(bf16), 1)
        .astype(bf16)
        .reshape(length, heads, HEAD_DIM)
    )
    delta = jnp.transpose(jnp.sum(grad_att.astype(f32) * attended, axis=-1))
    scores = score()
    prob = jnp.exp(scores - (top + jnp.log(denom))[:, :, None])
    weight_low = jnp.exp(scores - top[:, :, None]).astype(bf16)
    grad_probs = jnp.einsum("qhd,khd->hqk", grad_att, value, preferred_element_type=f32)
    grad_scores = (prob * (grad_probs - delta[:, :, None])).astype(bf16)
    grad_query = (
        jnp.einsum("hqk,khd->qhd", grad_scores, key, preferred_element_type=f32) * scale
    )
    grad_key = (
        jnp.einsum("hqk,qhd->khd", grad_scores, query, preferred_element_type=f32) * scale
    )
    scaled_rows = (grad_att.astype(f32) / jnp.transpose(denom)[:, :, None]).astype(bf16)
    grad_value = jnp.einsum("hqk,qhd->khd", weight_low, scaled_rows, preferred_element_type=f32)

    query_back = rotate(grad_query, cosine, -sine_tab).reshape(length, part)
    key_back = rotate(grad_key, cosine, -sine_tab).reshape(length, part)
    grad_gain_query = jnp.sum(query_back * query_hat, axis=0)
    grad_gain_key = jnp.sum(key_back * key_hat, axis=0)
    query_back = query_back * gain_part[None, :, 0]
    key_back = key_back * gain_part[None, :, 1]
    inner = plane.total(
        jnp.stack([jnp.sum(query_back * query_hat, axis=1), jnp.sum(key_back * key_hat, axis=1)])
    ) / width
    grad_qkv_low = jnp.concatenate(
        [
            query_inv * (query_back - query_hat * inner[0][:, None]),
            key_inv * (key_back - key_hat * inner[1][:, None]),
            grad_value.reshape(length, part),
        ],
        axis=1,
    ).astype(bf16)
    grad_qkv_weight = mm(token_full, grad_qkv_low, ((0,), (0,))).astype(bf16)

    own_gains = jnp.stack([grad_gain_query, grad_gain_key, grad_gain_attn], axis=1)
    gain_cols = lax.dynamic_update_slice(
        jnp.zeros((width, GAIN_COLS), f32), own_gains, (place * part, 0)
    )
    gain_cols = lax.dynamic_update_slice(gain_cols, grad_gain_mlp[:, None], (0, 3))
    attn_partial = jnp.concatenate(
        [grad_qkv_weight, grad_out_weight, gain_cols.astype(bf16)], axis=1
    )
    mine = lax.psum_scatter(attn_partial, "dp", scatter_dimension=0, tiled=True)
    got = lax.all_to_all(mine, "fsdp", 0, 0, tiled=True).reshape(count, owned, 4 * part + GAIN_COLS)
    grad_attn = (
        got[:, :, : 4 * part]
        .reshape(count, owned, 4, part)
        .transpose(1, 2, 0, 3)
        .reshape(owned, 4 * width)
        .astype(f32)
    )
    grad_gains = jnp.sum(got[:, :, 4 * part : 4 * part + 4].astype(f32), axis=0)

    back = mm(grad_qkv_low, qkv_weight, ((1,), (1,)))
    own_cols = lax.dynamic_slice_in_dim(back, place * part, part, 1) + grad_hidden
    back = lax.dynamic_update_slice(back, own_cols, (0, place * part))
    grad_tokens = plane.scatter(back.astype(bf16), 0)

    new_attn, new_m_attn, new_v_attn = adamw_step(
        w_attn, grad_attn, m_attn, v_attn, decay_rate, learn_rate
    )
    new_gate_up, new_m_gate_up, new_v_gate_up = adamw_step(
        w_gate_up, grad_gate_up, m_gate_up, v_gate_up, decay_rate, learn_rate
    )
    new_down, new_m_down, new_v_down = adamw_step(
        w_down, grad_down, m_down, v_down, decay_rate, learn_rate
    )
    new_gains, new_m_gains, new_v_gains = adamw_step(
        gains, grad_gains, m_gains, v_gains, 0.0, gain_rate
    )
    return (
        output,
        grad_tokens,
        grad_attn,
        grad_gate_up,
        grad_down,
        grad_gains,
        new_attn,
        new_gate_up,
        new_down,
        new_gains,
        new_m_attn,
        new_v_attn,
        new_m_gate_up,
        new_v_gate_up,
        new_m_down,
        new_v_down,
        new_m_gains,
        new_v_gains,
    )


def solution(mesh):
    matrix, vector = P(("dp", "fsdp"), None), P(("dp", "fsdp"))
    in_specs = (matrix, vector) + (matrix,) * 13
    return jax.shard_map(
        per_device, mesh=mesh, in_specs=in_specs, out_specs=(matrix,) * 18, check_vma=False
    )
```

time: 2720 us -> 1010 us (0.37)
  waiting for transfers between devices: 2170 us -> 425 us
  starting transfers between devices: 0.94 us -> 79.7 us
  local copies, waits for them, and re-layouts: 48.1 us -> 126 us
  matrix products: 274 us -> 205 us
  blocking collectives: 103 us -> 48.7 us
    all_gather x15 -> x3, waiting for transfers between devices: 1430 us -> 55.9 us  [the longest x1 49.9 us: per_device(): down_all = lax.all_gather(spread(w_down, 1), 'dp', axis=0, tiled=True)]
    reduce_scatter x3, waiting for transfers between devices: 649 us -> 133 us  [the longest x2 133 us: reduced(): mine = lax.psum_scatter(partial, 'dp', scatter_dimension=0, tiled=True)]
    ppermute x0 -> x55, waiting for transfers between devices: none -> 204 us  [swap(): lax.ppermute(values, 'fsdp', [(i, i ^ bit) for i in range(self.count)])]
    all_gather x5 -> x0, blocking collectives: 103 us -> none  [the longest x1 70.8 us: per_device(): lax.all_gather(gains_low, ('dp', 'fsdp'), axis=0, tiled=True)]
    unnamed x20 -> x6, waiting for transfers between devices: 94.2 us -> 0.1 us
    dot_general x18, matrix products: 274 us -> 205 us  [the longest x12 160 us: mm(): lax.dot_general(left, right, (dims, ((), ())), preferred_element_type=f32)]
    ppermute x0 -> x55, starting transfers between devices: none -> 59.9 us  [swap(): lax.ppermute(values, 'fsdp', [(i, i ^ bit) for i in range(self.count)])]
    all_to_all x0 -> x2, blocking collectives: none -> 48.7 us  [spread(): return lax.all_to_all(block, 'fsdp', 0, 0, tiled=True)]
  transfers between devices with their start and end apart: 19 -> 66, of which waited for: 16 -> 46; matrix products, arithmetic and copies ran while one was open for 14% -> 34% of each run, Pallas kernels for 0% -> 0%
where the time goes in v1:
time: 1010 us; the launch traced here: 1000 us
  waiting for transfers between devices  425 us (42%)
  matrix products  205 us (20%)
  local copies, waits for them, and re-layouts  126 us (12%)
  other arithmetic  101 us (10%)
  starting transfers between devices  79.7 us (8%)
  blocking collectives  48.7 us (5%)
  between operations  15.8 us (2%)
    ppermute x55, waiting for transfers between devices, swap(): lax.ppermute(values, 'fsdp', [(i, i ^ bit) for i in range(self.count)])  204 us
    dot_general x12, matrix products, mm(): lax.dot_general(left, right, (dims, ((), ())), preferred_element_type=f32)  160 us
    reduce_scatter x2, waiting for transfers between devices, reduced(): mine = lax.psum_scatter(partial, 'dp', scatter_dimension=0, tiled=True)  133 us
    ppermute x55, starting transfers between devices, swap(): lax.ppermute(values, 'fsdp', [(i, i ^ bit) for i in range(self.count)])  59.9 us
    all_gather x1, waiting for transfers between devices, per_device(): down_all = lax.all_gather(spread(w_down, 1), 'dp', axis=0, tiled=True)  49.9 us
    all_to_all x2, blocking collectives, spread(): return lax.all_to_all(block, 'fsdp', 0, 0, tiled=True)  48.7 us
    unnamed x141, local copies, waits for them, and re-layouts  27.1 us
    sub x4, other arithmetic, adamw_step(): weight * (1.0 - rate_value * decay_coef) - rate_value * step_ratio  25.1 us
  transfers between devices with their start and end apart: 66, of which 46 were waited for; matrix products, arithmetic and copies ran while one was open for 34% of the time, Pallas kernels for 0%

profile of v1, /device:TPU:0, one launch (start us, length us, event | category | flops | bytes accessed | tf_op | source)
XLA Modules:
  0.0 1000.8 jit_solution(6982497248516469450)
XLA Ops:
  11.9 20.0 %all_to_all.66 = bf16[4,64,2176]{2,1,0:T(8,128)(2,1)S(1)} all-to-all(bf16[4,64,2176]{2,1,0:T(8,128)(2,1)S(1)} %pad_maximum_fusion.11), channel_id=1, replica_groups=mesh['dp'=8,'fsdp'=4] {'fsdp'}, dimensions={0} | all-to-all | bytes 2228224 | tf_op jit(solution)/shard_map/all_to_all | solution.py:169
  45.3 28.7 %all_to_all.67 = bf16[4,64,4096]{2,1,0:T(8,128)(2,1)} all-to-all(bf16[4,64,4096]{2,1,0:T(8,128)(2,1)} %all_to_all.46), channel_id=1, replica_groups=mesh['dp'=8,'fsdp'=4] {'fsdp'}, dimensions={0} | all-to-all | bytes 4194304 | tf_op jit(solution)/shard_map/all_to_all | solution.py:169
  91.2 10.8 %collective-permute-done.6 = s32[256]{0:T(256)S(1)} collective-permute-done((s32[256]{0:T(256)S(1)}, s32[256]{0:T(256)S(1)}, u32[]{:S(2)}, u32[]{:S(2)}) %collective-permute-start.6) | collective-permute-done | bytes 1056 | tf_op jit(solution)/shard_map/ppermute | solution.py:61
  108.8 8.5 all-to-all-done.2
  130.0 11.4 %fusion.6 = f32[1024,1536]{1,0:T(8,128)S(1)} fusion(bf16[1024,2048]{0,1:T(8,128)(2,1)} %constant_dynamic-update-slice_fusion.20, bf16[2048,2176]{0,1:T(8,128)(2,1)} %all-gather.4.cloned.1.call-done), kind=kOutput, calls=%fused_computation.19 | convolution fusion | flops 6442450944 | bytes 16777216 | tf_op jit(solution)/shard_map/dot_general | solution.py:27
  172.3 12.4 %fusion.61 = (bf16[1024,4,128]{0,2,1:T(8,128)(2,1)S(1)}, f32[1024,4,128]{0,2,1:T(8,128)}) fusion(f32[1024,4]{0,1:T(4,128)S(1)} %bitcast.156, f32[4,1024,1024]{1,2,0:T(8,128)} %copy-done.9, f32[4,1024]{1,0:T(4,128)S(1)} %get-tuple-element.200, pred[1024,1024]{0,1:T(8,128)(4,1)S(1)} %copy-done.17, f32[1024,1536]{1,0:T(8,128)} %copy-done), kind=kOutput, calls=%fused_computation.211 | convolution fusion | flops 1091567616 | bytes 22052864 | tf_op jit(solution)/shard_map/hqk,khd->qhd/dot_general | solution.py:229
  186.2 18.9 %collective-permute-done.10 = bf16[1024,512]{0,1:T(8,128)(2,1)S(1)} collective-permute-done((bf16[1024,512]{0,1:T(8,128)(2,1)S(1)}, bf16[1024,512]{0,1:T(8,128)(2,1)S(1)}, u32[]{:S(2)}, u32[]{:S(2)}) %collective-permute-start.10) | collective-permute-done | bytes 1048608 | tf_op jit(solution)/shard_map/ppermute | solution.py:61
  208.5 7.0 collective-permute-done.12
  216.7 5.5 multiply_reduce_fusion.5
  235.5 18.2 %collective-permute-done.17 = bf16[1024,512]{0,1:T(8,128)(2,1)S(1)} collective-permute-done((bf16[1024,512]{0,1:T(8,128)(2,1)S(1)}, bf16[1024,512]{0,1:T(8,128)(2,1)S(1)}, u32[]{:S(2)}, u32[]{:S(2)}) %collective-permute-start.17) | collective-permute-done | bytes 1048608 | tf_op jit(solution)/shard_map/ppermute | solution.py:61
  258.1 4.9 collective-permute-done.19
  264.8 6.0 all-gather.6.cloned.1.call-done
  270.8 22.9 %fusion.62 = f32[1024,4096]{1,0:T(8,128)S(1)} fusion(bf16[1024,2048]{0,1:T(8,128)(2,1)} %constant_dynamic-update-slice_fusion.17, bf16[2048,4096]{1,0:T(8,128)(2,1)} %all-gather.6.cloned.1.call-done), kind=kOutput, calls=%fused_computation.212 | convolution fusion | flops 17179869184 | bytes 37748736 | tf_op jit(solution)/shard_map/dot_general | solution.py:27
  293.6 5.8 copy-done.8
  303.3 49.9 %all-gather.8.cloned.1.call-done = bf16[2048,2048]{1,0:T(8,128)(2,1)} async-done(((bf16[256,2048]{1,0:T(8,128)(2,1)}), bf16[2048,2048]{1,0:T(8,128)(2,1)}) %all-gather.8.cloned.1.call-update) | async-done | bytes 8388624 | tf_op jit(solution)/shard_map/all_gather | solution.py:174
  353.3 12.5 %convolution_convert_fusion.4 = bf16[1024,2048]{0,1:T(8,128)(2,1)S(1)} fusion(bf16[1024,2048]{1,0:T(8,128)(2,1)} %multiply_convert_fusion.3, bf16[2048,2048]{1,0:T(8,128)(2,1)} %all-gather.8.cloned.1.call-done), kind=kOutput, calls=%fused_computation.31 | convolution fusion | flops 8592031744 | bytes 16777216 | tf_op jit(solution)/shard_map/dot_general | solution.py:27
  369.7 11.2 %collective-permute-done.22 = bf16[256,1024]{0,1:T(8,128)(2,1)S(1)} collective-permute-done((bf16[256,1024]{0,1:T(8,128)(2,1)S(1)}, bf16[256,1024]{0,1:T(8,128)(2,1)S(1)}, u32[]{:S(2)}, u32[]{:S(2)}) %collective-permute-start.22) | collective-permute-done | bytes 524320 | tf_op jit(solution)/shard_map/ppermute | solution.py:61
  383.2 8.3 collective-permute-done.21
  399.6 5.6 collective-permute-done.24
  416.6 19.0 %collective-permute-done.27 = bf16[256,2048]{0,1:T(8,128)(2,1)S(1)} collective-permute-done((bf16[256,2048]{0,1:T(8,128)(2,1)S(1)}, bf16[256,2048]{0,1:T(8,128)(2,1)S(1)}, u32[]{:S(2)}, u32[]{:S(2)}) %collective-permute-start.27) | collective-permute-done | bytes 1048608 | tf_op jit(solution)/shard_map/ppermute | solution.py:61
  439.9 8.1 collective-permute-done.29
  450.7 10.9 %convolution_convert_fusion.1 = bf16[2048,2048]{1,0:T(8,128)(2,1)} fusion(bf16[1024,2048]{0,1:T(8,128)(2,1)S(1)} %constant_dynamic-update-slice_fusion.19, bf16[1024,2048]{1,0:T(8,128)(2,1)S(1)} %copy-done.16), kind=kOutput, calls=%fused_computation.14 | convolution fusion | flops 8594128896 | bytes 16777216 | tf_op jit(solution)/shard_map/dot_general | solution.py:27
  461.7 20.2 %multiply_convert_fusion.2 = (bf16[1024,2048]{1,0:T(8,128)(2,1)S(1)}, bf16[1024,2048]{1,0:T(8,128)(2,1)S(1)}) fusion(f32[1024,4096]{1,0:T(8,128)} %copy-done.8, bf16[1024,2048]{0,1:T(8,128)(2,1)} %copy-done.23, bf16[2048,2048]{1,0:T(8,128)(2,1)} %all-gather.8.cloned.1.call-done), kind=kOutput, calls=%fused_computation.10 | convolution fusion | flops 8617197568 | bytes 37748736 | tf_op jit(solution)/shard_map/dot_general | solution.py:27
  481.9 23.2 %fusion.11 = bf16[1024,2048]{0,1:T(8,128)(2,1)S(1)} fusion(bf16[2048,4096]{1,0:T(8,128)(2,1)} %all-gather.6.cloned.1.call-done, bf16[1024,2048]{1,0:T(8,128)(2,1)S(1)} %get-tuple-element.138, bf16[1024,2048]{1,0:T(8,128)(2,1)S(1)} %get-tuple-element.137), kind=kOutput, calls=%fused_computation.29 | convolution fusion | flops 17198743552 | bytes 29360128 | tf_op jit(solution)/shard_map/dot_general | solution.py:27
  509.8 11.4 %collective-permute-done.32 = bf16[512,512]{0,1:T(8,128)(2,1)S(1)} collective-permute-done((bf16[512,512]{0,1:T(8,128)(2,1)S(1)}, bf16[512,512]{0,1:T(8,128)(2,1)S(1)}, u32[]{:S(2)}, u32[]{:S(2)}) %collective-permute-start.32) | collective-permute-done | bytes 524320 | tf_op jit(solution)/shard_map/ppermute | solution.py:61
  533.3 8.4 collective-permute-done.33
  547.0 5.3 collective-permute-done.34
  571.0 6.7 collective-permute-done.41
  580.0 5.7 collective-permute-done.40
  585.8 5.8 collective-permute-done.42
  608.9 9.8 multiply_convert_fusion
  618.8 4.7 multiply_bitcast_fusion.1
  627.4 4.8 multiply_subtract_fusion.4
  639.1 9.9 convolution_convert_fusion.6
  652.1 5.7 multiply_convert_fusion.5
  657.9 10.6 %convolution_convert_fusion.2 = bf16[2048,1536]{0,1:T(8,128)(2,1)S(1)} fusion(bf16[1024,2048]{0,1:T(8,128)(2,1)} %constant_dynamic-update-slice_fusion.20, bf16[1024,512]{1,0:T(8,128)(2,1)S(1)} %copy-done.40, bf16[1024,512]{1,0:T(8,128)(2,1)S(1)} %get-tuple-element.140, bf16[1024,512]{1,0:T(8,128)(2,1)S(1)} %get-tuple-element.139), kind=kOutput, calls=%fused_computation.15 | convolution fusion | flops 6455033856 | bytes 13631488 | tf_op jit(solution)/shard_map/dot_general | solution.py:27
  672.9 25.5 %convolution_convert_fusion = bf16[2048,4096]{1,0:T(8,128)(2,1)} fusion(bf16[1024,2048]{0,1:T(8,128)(2,1)} %constant_dynamic-update-slice_fusion.17, bf16[1024,2048]{1,0:T(8,128)(2,1)} %copy-done.64, bf16[1024,2048]{1,0:T(8,128)(2,1)} %copy-done.63), kind=kOutput, calls=%fused_computation.3 | convolution fusion | flops 17205035008 | bytes 29360128 | tf_op jit(solution)/shard_map/dot_general | solution.py:27
  699.6 9.4 fusion.4
  731.0 10.1 %collective-permute-done.50 = bf16[256,1024]{1,0:T(8,128)(2,1)S(1)} collective-permute-done((bf16[256,1024]{1,0:T(8,128)(2,1)S(1)}, bf16[256,1024]{1,0:T(8,128)(2,1)S(1)}, u32[]{:S(2)}, u32[]{:S(2)}) %collective-permute-start.50) | collective-permute-done | bytes 524320 | tf_op jit(solution)/shard_map/ppermute | solution.py:61
  743.4 8.9 collective-permute-done.49
  779.8 6.6 multiply_subtract_fusion.1
  800.9 132.9 %reduce-scatter.6.cloned.1.call-done = bf16[256,4096]{1,0:T(8,128)(2,1)} async-done(((bf16[2048,4096]{1,0:T(8,128)(2,1)}), bf16[256,4096]{1,0:T(8,128)(2,1)}) %reduce-scatter.6.cloned.1.call-update) | async-done | bytes 2097168 | tf_op jit(solution)/shard_map/reduce_scatter | solution.py:258
  938.4 6.5 multiply_subtract_fusion.2
  945.0 16.5 %all-to-all-done.5 = bf16[4,64,4096]{2,1,0:T(8,128)(2,1)} async-done(((bf16[4,64,4096]{2,1,0:T(8,128)(2,1)}), bf16[4,64,4096]{2,1,0:T(8,128)(2,1)}, u32[]{:S(2)}, u32[]{:S(2)}) %all-to-all-start.5) | async-done | bytes 2097184 | tf_op jit(solution)/shard_map/all_to_all | solution.py:259
  961.5 6.6 reshape.342
  968.0 8.1 copy.293
  976.2 6.1 reshape.339
  982.2 11.5 %multiply_subtract_fusion = (f32[64,16384]{1,0:T(8,128)}, f32[64,16384]{1,0:T(8,128)}, f32[64,16384]{1,0:T(8,128)}) fusion(f32[64,16384]{1,0:T(8,128)} %param.19, f32[64,16384]{1,0:T(8,128)} %reshape.339, f32[64,16384]{1,0:T(8,128)} %param.24, f32[64,16384]{1,0:T(8,128)} %param.25), kind=kLoop, calls=%fused_computation.24 | loop fusion | flops 14680064 | bytes 29360128 | tf_op jit(solution)/shard_map/sub | solution.py:48
  (382 shorter events, 297.6 us)
Async XLA Ops:
  7.2 122.8 %all-gather.4.cloned.1.call-start = ((), (), s32[]{:S(2)}) async-start(), calls=%async_computation.10 | async-start | bytes 10027008 | tf_op jit(solution)/shard_map/all_gather | solution.py:172
  33.3 237.5 %all-gather.6.cloned.1.call-start = ((), (), s32[]{:S(2)}) async-start(), calls=%async_computation.11 | async-start | bytes 18874368 | tf_op jit(solution)/shard_map/all_gather | solution.py:173
  75.3 28.2 %collective-permute-start = (bf16[256,2048]{0,1:T(8,128)(2,1)}, bf16[256,2048]{0,1:T(8,128)(2,1)}, u32[]{:S(2)}, u32[]{:S(2)}) collective-permute-start(bf16[256,2048]{0,1:T(8,128)(2,1)} %copy.197), channel_id=1, source_target_pairs={{0,1},{1,0},{2,3},{3,2},{4,5},{5,4},{6,7},{7,6},{8,9},{9,8},{10,11... | collective-permute-start | bytes 3145736 | tf_op jit(solution)/shard_map/ppermute | solution.py:61
  76.2 15.0 %collective-permute-start.5 = (s32[256]{0:T(256)S(1)}, s32[256]{0:T(256)S(1)}, u32[]{:S(2)}, u32[]{:S(2)}) collective-permute-start(s32[256]{0:T(256)S(1)} %copy-done.62), channel_id=1, source_target_pairs={{0,2},{1,3},{2,0},{3,1},{4,6},{5,7},{6,4},{7,5},{8,10},{9,11},{10,... | collective-permute-start | bytes 3080 | tf_op jit(solution)/shard_map/ppermute | solution.py:61
  76.8 25.2 %collective-permute-start.6 = (s32[256]{0:T(256)S(1)}, s32[256]{0:T(256)S(1)}, u32[]{:S(2)}, u32[]{:S(2)}) collective-permute-start(s32[256]{0:T(256)S(1)} %copy-done.62), channel_id=1, source_target_pairs={{0,3},{1,2},{2,1},{3,0},{4,7},{5,6},{6,5},{7,4},{8,11},{9,10},{10,... | collective-permute-start | bytes 3080 | tf_op jit(solution)/shard_map/ppermute | solution.py:61
  78.8 23.2 %collective-permute-start.4 = (s32[256]{0:T(256)S(1)}, s32[256]{0:T(256)S(1)}, u32[]{:S(2)}, u32[]{:S(2)}) collective-permute-start(s32[256]{0:T(256)S(1)} %copy-done.62), channel_id=1, source_target_pairs={{0,1},{1,0},{2,3},{3,2},{4,5},{5,4},{6,7},{7,6},{8,9},{9,8},{10,11... | collective-permute-start | bytes 3080 | tf_op jit(solution)/shard_map/ppermute | solution.py:61
  79.7 39.1 %collective-permute-start.1 = (bf16[256,2048]{0,1:T(8,128)(2,1)}, bf16[256,2048]{0,1:T(8,128)(2,1)}, u32[]{:S(2)}, u32[]{:S(2)}) collective-permute-start(bf16[256,2048]{0,1:T(8,128)(2,1)} %copy.197), channel_id=1, source_target_pairs={{0,2},{1,3},{2,0},{3,1},{4,6},{5,7},{6,4},{7,5},{8,10},{9,11},{10,... | collective-permute-start | bytes 3145736 | tf_op jit(solution)/shard_map/ppermute | solution.py:61
  82.7 34.5 %all-to-all-start.2 = ((bf16[4,64,2048]{2,1,0:T(8,128)(2,1)}), bf16[4,64,2048]{2,1,0:T(8,128)(2,1)S(1)}, u32[]{:S(2)}, u32[]{:S(2)}) async-start(bf16[4,64,2048]{2,1,0:T(8,128)(2,1)} %copy.210), calls=%async_computation.2 | async-start | bytes 2097152 | tf_op jit(solution)/shard_map/all_to_all | solution.py:169
  86.3 267.0 %all-gather.8.cloned.1.call-start = ((), (), s32[]{:S(2)}) async-start(), calls=%async_computation.12 | async-start | bytes 9437184 | tf_op jit(solution)/shard_map/all_gather | solution.py:174
  104.6 21.1 %collective-permute-start.2 = (bf16[256,1024]{0,1:T(8,128)(2,1)S(1)}, bf16[256,1024]{0,1:T(8,128)(2,1)}, u32[]{:S(2)}, u32[]{:S(2)}) collective-permute-start(bf16[256,1024]{0,1:T(8,128)(2,1)S(1)} %slice.141), channel_id=1, source_target_pairs={{0,2},{1,3},{2,0},{3,1},{4,6},{5,7},{6,4},{7,5},{8,10},{9,11},{10,... | collective-permute-start | bytes 1572872 | tf_op jit(solution)/shard_map/ppermute | solution.py:61
  118.3 636.4 %reduce-scatter.8.cloned.1.call-start = ((), (), s32[]{:S(2)}) async-start(), calls=%async_computation.15 | async-start | bytes 9437184 | tf_op jit(solution)/shard_map/reduce_scatter | solution.py:258
  184.7 20.4 %collective-permute-start.10 = (bf16[1024,512]{0,1:T(8,128)(2,1)S(1)}, bf16[1024,512]{0,1:T(8,128)(2,1)S(1)}, u32[]{:S(2)}, u32[]{:S(2)}) collective-permute-start(bf16[1024,512]{0,1:T(8,128)(2,1)S(1)} %bitcast.143), channel_id=1, source_target_pairs={{0,1},{1,0},{2,3},{3,2},{4,5},{5,4},{6,7},{7,6},{8,9},{9,8},{10,11... | collective-permute-start | bytes 3145736 | tf_op jit(solution)/shard_map/ppermute | solution.py:61
  185.4 21.5 %collective-permute-start.11 = (bf16[1024,512]{0,1:T(8,128)(2,1)S(1)}, bf16[1024,512]{0,1:T(8,128)(2,1)S(1)}, u32[]{:S(2)}, u32[]{:S(2)}) collective-permute-start(bf16[1024,512]{0,1:T(8,128)(2,1)S(1)} %bitcast.144), channel_id=1, source_target_pairs={{0,2},{1,3},{2,0},{3,1},{4,6},{5,7},{6,4},{7,5},{8,10},{9,11},{10,... | collective-permute-start | bytes 3145736 | tf_op jit(solution)/shard_map/ppermute | solution.py:61
  206.9 9.8 collective-permute-start.13
  233.3 20.4 %collective-permute-start.17 = (bf16[1024,512]{0,1:T(8,128)(2,1)S(1)}, bf16[1024,512]{0,1:T(8,128)(2,1)S(1)}, u32[]{:S(2)}, u32[]{:S(2)}) collective-permute-start(bf16[1024,512]{0,1:T(8,128)(2,1)S(1)} %get-tuple-element.136), channel_id=1, source_target_pairs={{0,1},{1,0},{2,3},{3,2},{4,5},{5,4},{6,7},{7,6},{8,9},{9,8},{10,11... | collective-permute-start | bytes 3145736 | tf_op jit(solution)/shard_map/ppermute | solution.py:61
  234.6 20.1 %collective-permute-start.18 = (bf16[1024,512]{0,1:T(8,128)(2,1)S(1)}, bf16[1024,512]{0,1:T(8,128)(2,1)S(1)}, u32[]{:S(2)}, u32[]{:S(2)}) collective-permute-start(bf16[1024,512]{0,1:T(8,128)(2,1)S(1)} %get-tuple-element.136), channel_id=1, source_target_pairs={{0,2},{1,3},{2,0},{3,1},{4,6},{5,7},{6,4},{7,5},{8,10},{9,11},{10,... | collective-permute-start | bytes 3145736 | tf_op jit(solution)/shard_map/ppermute | solution.py:61
  366.1 14.8 %collective-permute-start.22 = (bf16[256,1024]{0,1:T(8,128)(2,1)S(1)}, bf16[256,1024]{0,1:T(8,128)(2,1)S(1)}, u32[]{:S(2)}, u32[]{:S(2)}) collective-permute-start(bf16[256,1024]{0,1:T(8,128)(2,1)S(1)} %get-tuple-element.170), channel_id=1, source_target_pairs={{0,1},{1,0},{2,3},{3,2},{4,5},{5,4},{6,7},{7,6},{8,9},{9,8},{10,11... | collective-permute-start | bytes 1572872 | tf_op jit(solution)/shard_map/ppermute | solution.py:61
  367.7 23.8 %collective-permute-start.21 = (bf16[256,1024]{0,1:T(8,128)(2,1)S(1)}, bf16[256,1024]{0,1:T(8,128)(2,1)S(1)}, u32[]{:S(2)}, u32[]{:S(2)}) collective-permute-start(bf16[256,1024]{0,1:T(8,128)(2,1)S(1)} %get-tuple-element.167), channel_id=1, source_target_pairs={{0,1},{1,0},{2,3},{3,2},{4,5},{5,4},{6,7},{7,6},{8,9},{9,8},{10,11... | collective-permute-start | bytes 1572872 | tf_op jit(solution)/shard_map/ppermute | solution.py:61
  368.2 23.3 %collective-permute-start.25 = (bf16[256,1024]{0,1:T(8,128)(2,1)S(1)}, bf16[256,1024]{0,1:T(8,128)(2,1)S(1)}, u32[]{:S(2)}, u32[]{:S(2)}) collective-permute-start(bf16[256,1024]{0,1:T(8,128)(2,1)S(1)} %get-tuple-element.168), channel_id=1, source_target_pairs={{0,2},{1,3},{2,0},{3,1},{4,6},{5,7},{6,4},{7,5},{8,10},{9,11},{10,... | collective-permute-start | bytes 1572872 | tf_op jit(solution)/shard_map/ppermute | solution.py:61
  381.1 14.9 %collective-permute-start.23 = (bf16[256,1024]{0,1:T(8,128)(2,1)S(1)}, bf16[256,1024]{0,1:T(8,128)(2,1)S(1)}, u32[]{:S(2)}, u32[]{:S(2)}) collective-permute-start(bf16[256,1024]{0,1:T(8,128)(2,1)S(1)} %add_convert_fusion.13), channel_id=1, source_target_pairs={{0,2},{1,3},{2,0},{3,1},{4,6},{5,7},{6,4},{7,5},{8,10},{9,11},{10,... | collective-permute-start | bytes 1572872 | tf_op jit(solution)/shard_map/ppermute | solution.py:61
  382.7 22.4 %collective-permute-start.24 = (bf16[256,1024]{0,1:T(8,128)(2,1)S(1)}, bf16[256,1024]{0,1:T(8,128)(2,1)}, u32[]{:S(2)}, u32[]{:S(2)}) collective-permute-start(bf16[256,1024]{0,1:T(8,128)(2,1)S(1)} %get-tuple-element.169), channel_id=1, source_target_pairs={{0,2},{1,3},{2,0},{3,1},{4,6},{5,7},{6,4},{7,5},{8,10},{9,11},{10,... | collective-permute-start | bytes 1572872 | tf_op jit(solution)/shard_map/ppermute | solution.py:61
  413.5 22.0 %collective-permute-start.27 = (bf16[256,2048]{0,1:T(8,128)(2,1)S(1)}, bf16[256,2048]{0,1:T(8,128)(2,1)S(1)}, u32[]{:S(2)}, u32[]{:S(2)}) collective-permute-start(bf16[256,2048]{0,1:T(8,128)(2,1)S(1)} %get-tuple-element.134), channel_id=1, source_target_pairs={{0,1},{1,0},{2,3},{3,2},{4,5},{5,4},{6,7},{7,6},{8,9},{9,8},{10,11... | collective-permute-start | bytes 3145736 | tf_op jit(solution)/shard_map/ppermute | solution.py:61
  415.1 24.2 %collective-permute-start.28 = (bf16[256,2048]{0,1:T(8,128)(2,1)S(1)}, bf16[256,2048]{0,1:T(8,128)(2,1)S(1)}, u32[]{:S(2)}, u32[]{:S(2)}) collective-permute-start(bf16[256,2048]{0,1:T(8,128)(2,1)S(1)} %get-tuple-element.134), channel_id=1, source_target_pairs={{0,2},{1,3},{2,0},{3,1},{4,6},{5,7},{6,4},{7,5},{8,10},{9,11},{10,... | collective-permute-start | bytes 3145736 | tf_op jit(solution)/shard_map/ppermute | solution.py:61
  435.6 12.5 %collective-permute-start.29 = (bf16[256,1024]{0,1:T(8,128)(2,1)S(1)}, bf16[256,1024]{0,1:T(8,128)(2,1)S(1)}, u32[]{:S(2)}, u32[]{:S(2)}) collective-permute-start(bf16[256,1024]{0,1:T(8,128)(2,1)S(1)} %slice.162), channel_id=1, source_target_pairs={{0,2},{1,3},{2,0},{3,1},{4,6},{5,7},{6,4},{7,5},{8,10},{9,11},{10,... | collective-permute-start | bytes 1572872 | tf_op jit(solution)/shard_map/ppermute | solution.py:61
  506.4 14.9 %collective-permute-start.32 = (bf16[512,512]{0,1:T(8,128)(2,1)S(1)}, bf16[512,512]{0,1:T(8,128)(2,1)S(1)}, u32[]{:S(2)}, u32[]{:S(2)}) collective-permute-start(bf16[512,512]{0,1:T(8,128)(2,1)S(1)} %get-tuple-element.164), channel_id=1, source_target_pairs={{0,1},{1,0},{2,3},{3,2},{4,5},{5,4},{6,7},{7,6},{8,9},{9,8},{10,11... | collective-permute-start | bytes 1572872 | tf_op jit(solution)/shard_map/ppermute | solution.py:61
  506.6 25.9 %collective-permute-start.31 = (bf16[512,512]{0,1:T(8,128)(2,1)}, bf16[512,512]{0,1:T(8,128)(2,1)S(1)}, u32[]{:S(2)}, u32[]{:S(2)}) collective-permute-start(bf16[512,512]{0,1:T(8,128)(2,1)} %get-tuple-element.161), channel_id=1, source_target_pairs={{0,1},{1,0},{2,3},{3,2},{4,5},{5,4},{6,7},{7,6},{8,9},{9,8},{10,11... | collective-permute-start | bytes 1572872 | tf_op jit(solution)/shard_map/ppermute | solution.py:61
  508.4 24.1 %collective-permute-start.35 = (bf16[512,512]{0,1:T(8,128)(2,1)S(1)}, bf16[512,512]{0,1:T(8,128)(2,1)S(1)}, u32[]{:S(2)}, u32[]{:S(2)}) collective-permute-start(bf16[512,512]{0,1:T(8,128)(2,1)S(1)} %get-tuple-element.162), channel_id=1, source_target_pairs={{0,2},{1,3},{2,0},{3,1},{4,6},{5,7},{6,4},{7,5},{8,10},{9,11},{10,... | collective-permute-start | bytes 1572872 | tf_op jit(solution)/shard_map/ppermute | solution.py:61
  522.2 19.5 %collective-permute-start.33 = (bf16[512,512]{0,1:T(8,128)(2,1)}, bf16[512,512]{0,1:T(8,128)(2,1)}, u32[]{:S(2)}, u32[]{:S(2)}) collective-permute-start(bf16[512,512]{0,1:T(8,128)(2,1)} %add_convert_fusion.11), channel_id=1, source_target_pairs={{0,2},{1,3},{2,0},{3,1},{4,6},{5,7},{6,4},{7,5},{8,10},{9,11},{10,... | collective-permute-start | bytes 1572872 | tf_op jit(solution)/shard_map/ppermute | solution.py:61
  523.6 22.9 %all-to-all-start.3 = ((bf16[4,256,512]{1,2,0:T(8,128)(2,1)}), bf16[4,256,512]{1,2,0:T(8,128)(2,1)S(1)}, u32[]{:S(2)}, u32[]{:S(2)}) async-start(bf16[4,256,512]{1,2,0:T(8,128)(2,1)} %bitcast.19), calls=%async_computation.3 | async-start | bytes 2097152 | tf_op jit(solution)/shard_map/all_to_all | solution.py:182
  527.1 246.6 %reduce-scatter.4.cloned.1.call-start = ((), (), s32[]{:S(2)}) async-start(), calls=%async_computation.13 | async-start | bytes 10027008 | tf_op jit(solution)/shard_map/reduce_scatter | solution.py:331
  527.2 25.1 %collective-permute-start.34 = (bf16[512,512]{0,1:T(8,128)(2,1)S(1)}, bf16[512,512]{0,1:T(8,128)(2,1)}, u32[]{:S(2)}, u32[]{:S(2)}) collective-permute-start(bf16[512,512]{0,1:T(8,128)(2,1)S(1)} %get-tuple-element.163), channel_id=1, source_target_pairs={{0,2},{1,3},{2,0},{3,1},{4,6},{5,7},{6,4},{7,5},{8,10},{9,11},{10,... | collective-permute-start | bytes 1572872 | tf_op jit(solution)/shard_map/ppermute | solution.py:61
  567.3 10.4 %collective-permute-start.41 = (bf16[512,512]{1,0:T(8,128)(2,1)S(1)}, bf16[512,512]{1,0:T(8,128)(2,1)S(1)}, u32[]{:S(2)}, u32[]{:S(2)}) collective-permute-start(bf16[512,512]{1,0:T(8,128)(2,1)S(1)} %get-tuple-element.158), channel_id=1, source_target_pairs={{0,1},{1,0},{2,3},{3,2},{4,5},{5,4},{6,7},{7,6},{8,9},{9,8},{10,11... | collective-permute-start | bytes 1572872 | tf_op jit(solution)/shard_map/ppermute | solution.py:61
  569.0 16.8 %collective-permute-start.40 = (bf16[512,512]{1,0:T(8,128)(2,1)S(1)}, bf16[512,512]{1,0:T(8,128)(2,1)S(1)}, u32[]{:S(2)}, u32[]{:S(2)}) collective-permute-start(bf16[512,512]{1,0:T(8,128)(2,1)S(1)} %get-tuple-element.155), channel_id=1, source_target_pairs={{0,1},{1,0},{2,3},{3,2},{4,5},{5,4},{6,7},{7,6},{8,9},{9,8},{10,11... | collective-permute-start | bytes 1572872 | tf_op jit(solution)/shard_map/ppermute | solution.py:61
  569.3 16.5 %collective-permute-start.44 = (bf16[512,512]{1,0:T(8,128)(2,1)S(1)}, bf16[512,512]{1,0:T(8,128)(2,1)S(1)}, u32[]{:S(2)}, u32[]{:S(2)}) collective-permute-start(bf16[512,512]{1,0:T(8,128)(2,1)S(1)} %get-tuple-element.156), channel_id=1, source_target_pairs={{0,2},{1,3},{2,0},{3,1},{4,6},{5,7},{6,4},{7,5},{8,10},{9,11},{10,... | collective-permute-start | bytes 1572872 | tf_op jit(solution)/shard_map/ppermute | solution.py:61
  577.9 13.7 %collective-permute-start.42 = (bf16[512,512]{1,0:T(8,128)(2,1)S(1)}, bf16[512,512]{1,0:T(8,128)(2,1)S(1)}, u32[]{:S(2)}, u32[]{:S(2)}) collective-permute-start(bf16[512,512]{1,0:T(8,128)(2,1)S(1)} %add_convert_fusion.9), channel_id=1, source_target_pairs={{0,2},{1,3},{2,0},{3,1},{4,6},{5,7},{6,4},{7,5},{8,10},{9,11},{10,... | collective-permute-start | bytes 1572872 | tf_op jit(solution)/shard_map/ppermute | solution.py:61
  578.6 20.5 %collective-permute-start.43 = (bf16[512,512]{1,0:T(8,128)(2,1)}, bf16[512,512]{1,0:T(8,128)(2,1)}, u32[]{:S(2)}, u32[]{:S(2)}) collective-permute-start(bf16[512,512]{1,0:T(8,128)(2,1)} %get-tuple-element.157), channel_id=1, source_target_pairs={{0,2},{1,3},{2,0},{3,1},{4,6},{5,7},{6,4},{7,5},{8,10},{9,11},{10,... | collective-permute-start | bytes 1572872 | tf_op jit(solution)/shard_map/ppermute | solution.py:61
  635.5 16.5 %collective-permute-start.48 = (f32[2,1024]{1,0:T(2,128)S(1)}, f32[2,1024]{1,0:T(2,128)S(1)}, u32[]{:S(2)}, u32[]{:S(2)}) collective-permute-start(f32[2,1024]{1,0:T(2,128)S(1)} %pad_maximum_fusion.22), channel_id=1, source_target_pairs={{0,3},{1,2},{2,1},{3,0},{4,7},{5,6},{6,5},{7,4},{8,11},{9,10},{10,... | collective-permute-start | bytes 24584 | tf_op jit(solution)/shard_map/ppermute | solution.py:61
  636.9 15.1 %collective-permute-start.47 = (f32[2,1024]{1,0:T(2,128)S(1)}, f32[2,1024]{1,0:T(2,128)S(1)}, u32[]{:S(2)}, u32[]{:S(2)}) collective-permute-start(f32[2,1024]{1,0:T(2,128)S(1)} %pad_maximum_fusion.22), channel_id=1, source_target_pairs={{0,2},{1,3},{2,0},{3,1},{4,6},{5,7},{6,4},{7,5},{8,10},{9,11},{10,... | collective-permute-start | bytes 24584 | tf_op jit(solution)/shard_map/ppermute | solution.py:61
  638.5 13.6 %collective-permute-start.46 = (f32[2,1024]{1,0:T(2,128)S(1)}, f32[2,1024]{1,0:T(2,128)S(1)}, u32[]{:S(2)}, u32[]{:S(2)}) collective-permute-start(f32[2,1024]{1,0:T(2,128)S(1)} %pad_maximum_fusion.22), channel_id=1, source_target_pairs={{0,1},{1,0},{2,3},{3,2},{4,5},{5,4},{6,7},{7,6},{8,9},{9,8},{10,11... | collective-permute-start | bytes 24584 | tf_op jit(solution)/shard_map/ppermute | solution.py:61
  672.8 260.9 %reduce-scatter.6.cloned.1.call-start = ((), (), s32[]{:S(2)}) async-start(), calls=%async_computation.14 | async-start | bytes 18874368 | tf_op jit(solution)/shard_map/reduce_scatter | solution.py:258
  729.0 12.2 %collective-permute-start.50 = (bf16[256,1024]{1,0:T(8,128)(2,1)S(1)}, bf16[256,1024]{1,0:T(8,128)(2,1)S(1)}, u32[]{:S(2)}, u32[]{:S(2)}) collective-permute-start(bf16[256,1024]{1,0:T(8,128)(2,1)S(1)} %get-tuple-element.152), channel_id=1, source_target_pairs={{0,1},{1,0},{2,3},{3,2},{4,5},{5,4},{6,7},{7,6},{8,9},{9,8},{10,11... | collective-permute-start | bytes 1572872 | tf_op jit(solution)/shard_map/ppermute | solution.py:61
  730.0 22.4 %collective-permute-start.49 = (bf16[256,1024]{1,0:T(8,128)(2,1)S(1)}, bf16[256,1024]{1,0:T(8,128)(2,1)S(1)}, u32[]{:S(2)}, u32[]{:S(2)}) collective-permute-start(bf16[256,1024]{1,0:T(8,128)(2,1)S(1)} %get-tuple-element.149), channel_id=1, source_target_pairs={{0,1},{1,0},{2,3},{3,2},{4,5},{5,4},{6,7},{7,6},{8,9},{9,8},{10,11... | collective-permute-start | bytes 1572872 | tf_op jit(solution)/shard_map/ppermute | solution.py:61
  731.0 21.4 %collective-permute-start.53 = (bf16[256,1024]{1,0:T(8,128)(2,1)S(1)}, bf16[256,1024]{1,0:T(8,128)(2,1)S(1)}, u32[]{:S(2)}, u32[]{:S(2)}) collective-permute-start(bf16[256,1024]{1,0:T(8,128)(2,1)S(1)} %get-tuple-element.150), channel_id=1, source_target_pairs={{0,2},{1,3},{2,0},{3,1},{4,6},{5,7},{6,4},{7,5},{8,10},{9,11},{10,... | collective-permute-start | bytes 1572872 | tf_op jit(solution)/shard_map/ppermute | solution.py:61
  741.3 12.1 %collective-permute-start.51 = (bf16[256,1024]{1,0:T(8,128)(2,1)S(1)}, bf16[256,1024]{1,0:T(8,128)(2,1)S(1)}, u32[]{:S(2)}, u32[]{:S(2)}) collective-permute-start(bf16[256,1024]{1,0:T(8,128)(2,1)S(1)} %add_convert_fusion.5), channel_id=1, source_target_pairs={{0,2},{1,3},{2,0},{3,1},{4,6},{5,7},{6,4},{7,5},{8,10},{9,11},{10,... | collective-permute-start | bytes 1572872 | tf_op jit(solution)/shard_map/ppermute | solution.py:61
  741.4 18.4 %collective-permute-start.52 = (bf16[256,1024]{1,0:T(8,128)(2,1)}, bf16[256,1024]{1,0:T(8,128)(2,1)}, u32[]{:S(2)}, u32[]{:S(2)}) collective-permute-start(bf16[256,1024]{1,0:T(8,128)(2,1)} %get-tuple-element.151), channel_id=1, source_target_pairs={{0,2},{1,3},{2,0},{3,1},{4,6},{5,7},{6,4},{7,5},{8,10},{9,11},{10,... | collective-permute-start | bytes 1572872 | tf_op jit(solution)/shard_map/ppermute | solution.py:61
  754.6 15.0 %all-to-all-start.6 = ((bf16[4,64,2048]{2,1,0:T(8,128)(2,1)}), bf16[4,64,2048]{2,1,0:T(8,128)(2,1)S(1)}, u32[]{:S(2)}, u32[]{:S(2)}) async-start(bf16[4,64,2048]{2,1,0:T(8,128)(2,1)} %bitcast.146), calls=%async_computation.9 | async-start | bytes 2097152 | tf_op jit(solution)/shard_map/all_to_all | solution.py:259
  776.3 13.3 %all-to-all-start.4 = ((bf16[4,64,2176]{2,1,0:T(8,128)(2,1)}), bf16[4,64,2176]{2,1,0:T(8,128)(2,1)S(1)}, u32[]{:S(2)}, u32[]{:S(2)}) async-start(bf16[4,64,2176]{2,1,0:T(8,128)(2,1)} %bitcast.131), calls=%async_computation.5 | async-start | bytes 2228224 | tf_op jit(solution)/shard_map/all_to_all | solution.py:332
  933.8 27.7 %all-to-all-start.5 = ((bf16[4,64,4096]{2,1,0:T(8,128)(2,1)}), bf16[4,64,4096]{2,1,0:T(8,128)(2,1)}, u32[]{:S(2)}, u32[]{:S(2)}) async-start(bf16[4,64,4096]{2,1,0:T(8,128)(2,1)} %bitcast.136), calls=%async_computation.7 | async-start | bytes 4194304 | tf_op jit(solution)/shard_map/all_to_all | solution.py:259
  (85 other events, 1026.9 us)
Sparse Core Ops, SparseCore 0:
  33.4 86.3 all-gather.3
  121.4 149.2 all-gather.5
  272.9 80.2 all-gather.7
  461.8 86.9 reduce-scatter.7
  673.0 91.8 reduce-scatter.3
  767.1 166.6 reduce-scatter.5

commit v2 on v1

v2 whole, which is shorter than its diff:
```python
import functools
import math

import jax
import jax.numpy as jnp
from jax import lax
from jax.experimental import pallas as pl
from jax.experimental.pallas import tpu as pltpu
from jax.experimental.layout import Layout, with_layout_constraint
from jax.sharding import Mesh
from jax.sharding import PartitionSpec as P

HEAD_DIM = 128

norm_eps = 1e-06
rope_base = 500000.0
learn_rate = 0.004
gain_rate = 0.25
beta_one = 0.9
beta_two = 0.95
decay_rate = 0.1
adam_eps = 1e-08
correct_one = 1.0 - beta_one**2
correct_two = 1.0 - beta_two**2
neg_large = -1e30
bf16 = jnp.bfloat16
f32 = jnp.float32
GAIN_COLS = 128
TILE = 512


def mm(left, right, dims):
    return lax.dot_general(left, right, (dims, ((), ())), preferred_element_type=f32)


def adamw_step(weight, gradient, moment, second, decay_coef, rate_value):
    moment_new = beta_one * moment + (1.0 - beta_one) * gradient
    second_new = beta_two * second + (1.0 - beta_two) * gradient * gradient
    step_ratio = moment_new / correct_one / (jnp.sqrt(second_new / correct_two) + adam_eps)
    return (
        weight * (1.0 - rate_value * decay_coef) - rate_value * step_ratio,
        moment_new,
        second_new,
    )


def spread_body(tile, *refs):
    out = refs[-1]
    if tile:
        for i in range(refs[0].shape[1] // tile):
            for g, ref in enumerate(refs[:-1]):
                start = (i * len(refs[:-1]) + g) * tile
                out[:, start : start + tile] = ref[:, i * tile : (i + 1) * tile].astype(bf16)
        return
    start = 0
    for ref in refs[:-1]:
        out[:, start : start + ref.shape[1]] = ref[...].astype(bf16)
        start += ref.shape[1]


def spread_kernel(weight, groups, count, extra, tile):
    owned, columns = weight.shape
    size = columns // (groups * count)
    specs = [
        pl.BlockSpec((owned, size), lambda f, g=g: (0, g * count + f)) for g in range(groups)
    ]
    operands = [weight] * groups
    wide = groups * size
    if extra is not None:
        specs.append(pl.BlockSpec(extra.shape, lambda f: (0, 0)))
        operands.append(extra)
        wide += extra.shape[1]
    return pl.pallas_call(
        functools.partial(spread_body, tile),
        grid=(count,),
        in_specs=specs,
        out_specs=pl.BlockSpec((owned, wide), lambda f: (f, 0)),
        out_shape=jax.ShapeDtypeStruct((count * owned, wide), bf16),
        compiler_params=pltpu.CompilerParams(vmem_limit_bytes=40 * 1024 * 1024),
        cost_estimate=pl.CostEstimate(
            flops=0, bytes_accessed=6 * owned * columns, transcendentals=0
        ),
    )(*operands)


def adamw_body(tile, *refs):
    grad_in, weight, moment, second, grad_out, new_weight, new_moment, new_second = refs
    if tile:
        groups = grad_in.shape[1] // weight.shape[1]
        for i in range(weight.shape[1] // tile):
            start = pl.multiple_of((i * groups + pl.program_id(1)) * tile, tile)
            grad_out[:, i * tile : (i + 1) * tile] = grad_in[:, pl.ds(start, tile)].astype(f32)
    else:
        grad_out[...] = grad_in[...].astype(f32)
    new_weight[...], new_moment[...], new_second[...] = adamw_step(
        weight[...], grad_out[...], moment[...], second[...], decay_rate, learn_rate
    )


def adamw_kernel(gradient, weight, moment, second, groups, count, tile=0):
    owned, columns = weight.shape
    size = columns // (groups * count)
    whole = pl.BlockSpec((owned, size), lambda f, g: (0, g * count + f))
    if tile:
        grad_spec = pl.BlockSpec((owned, groups * size), lambda f, g: (f, 0))
    else:
        grad_spec = pl.BlockSpec((owned, size), lambda f, g: (f, g))
    return pl.pallas_call(
        functools.partial(adamw_body, tile),
        grid=(count, groups),
        in_specs=[grad_spec, whole, whole, whole],
        out_specs=[whole] * 4,
        out_shape=[jax.ShapeDtypeStruct(weight.shape, f32)] * 4,
        compiler_params=pltpu.CompilerParams(vmem_limit_bytes=40 * 1024 * 1024),
        cost_estimate=pl.CostEstimate(
            flops=12 * owned * columns, bytes_accessed=30 * owned * columns, transcendentals=0
        ),
    )(gradient, weight, moment, second)


def dot(left, right, left_dim, right_dim):
    return lax.dot_general(
        left, right, (((left_dim,), (right_dim,)), ((), ())), preferred_element_type=f32
    )


def visible(first_ref, low, high):
    shape = (high - low, high)
    row = lax.broadcasted_iota(jnp.int32, shape, 0) + low
    column = lax.broadcasted_iota(jnp.int32, shape, 1)
    return (column <= row) & (column >= first_ref[low:high, :])


def attend_body(block, scale, *refs):
    query_in, key_in, value_in, inverse, gain, cosine, sine, first = refs[:8]
    query_out, key_out, value_out, attended, lse = refs[8:]

    def turned(values, column):
        normed = values * inverse[:, column : column + 1] * gain[column : column + 1, :]
        return (normed * cosine[...] + pltpu.roll(normed, HEAD_DIM // 2, 1) * sine[...]).astype(bf16)

    query_out[...] = turned(query_in[...], 0)
    key_out[...] = turned(key_in[...], 1)
    value_out[...] = value_in[...].astype(bf16)
    for low in range(0, query_in.shape[0], block):
        high = low + block
        scores = dot(query_out[low:high, :], key_out[:high, :], 1, 1) * scale
        scores = jnp.where(visible(first, low, high), scores, neg_large)
        top = jnp.max(scores, axis=1, keepdims=True)
        weights = jnp.exp(scores - top)
        denom = jnp.sum(weights, axis=1, keepdims=True)
        attended[low:high, :] = (
            dot(weights.astype(bf16), value_out[:high, :], 1, 0) / denom
        ).astype(bf16)
        lse[0, low:high, :] = top + jnp.log(denom)


def attend_back_body(block, scale, *refs):
    query, key, value, attended, grad_att, lse = refs[:6]
    query_in, key_in, inverse, gain, cosine, sine, first = refs[6:13]
    query_grad, key_grad, value_grad, gain_grad, inner = refs[13:18]
    grad_low, key_sum, value_sum = refs[18:]
    grad_low[...] = grad_att[...].astype(bf16)
    delta = jnp.sum(
        grad_low[...].astype(f32) * attended[...].astype(f32), axis=1, keepdims=True
    )
    key_sum[...] = jnp.zeros_like(key_sum)
    value_sum[...] = jnp.zeros_like(value_sum)
    for low in range(0, query.shape[0], block):
        high = low + block
        scores = dot(query[low:high, :], key[:high, :], 1, 1) * scale
        prob = jnp.where(
            visible(first, low, high), jnp.exp(scores - lse[0, low:high, :]), 0.0
        )
        grad_prob = dot(grad_low[low:high, :], value[:high, :], 1, 1)
        grad_scores = (prob * (grad_prob - delta[low:high, :])).astype(bf16)
        query_grad[low:high, :] = dot(grad_scores, key[:high, :], 1, 0) * scale
        key_sum[:high, :] += dot(grad_scores, query[low:high, :], 0, 0)
        value_sum[:high, :] += dot(prob.astype(bf16), grad_low[low:high, :], 0, 0)
    value_grad[...] = value_sum[...].astype(bf16)
    lane = lax.broadcasted_iota(jnp.int32, inner.shape, 1)

    @pl.when(pl.program_id(0) == 0)
    def _():
        inner[...] = jnp.zeros_like(inner)

    gain_grad[...] = jnp.zeros_like(gain_grad)
    for column, turned, raw, out in (
        (0, query_grad[...], query_in, query_grad),
        (1, key_sum[...] * scale, key_in, key_grad),
    ):
        back = turned * cosine[...] - pltpu.roll(turned, HEAD_DIM // 2, 1) * sine[...]
        hat = raw[...] * inverse[:, column : column + 1]
        gain_grad[column : column + 1, :] = jnp.sum(back * hat, axis=0, keepdims=True)
        back = back * gain[column : column + 1, :]
        out[...] = back
        inner[...] += jnp.where(
            lane == column, jnp.sum(back * hat, axis=1, keepdims=True), 0.0
        )


def attend_kernels(length, heads):
    block = math.gcd(length, 256)
    scale = 1.0 / math.sqrt(HEAD_DIM)
    part = heads * HEAD_DIM

    def own(shift=0):
        return pl.BlockSpec((length, HEAD_DIM), lambda h: (0, h + shift))

    def same(width):
        return pl.BlockSpec((length, width), lambda h: (0, 0))

    gain_spec = pl.BlockSpec((8, HEAD_DIM), lambda h: (0, h))
    lse_spec = pl.BlockSpec((1, length, 1), lambda h: (h, 0, 0))
    tables = [same(2), gain_spec, same(HEAD_DIM), same(HEAD_DIM), same(1)]
    low_shape = jax.ShapeDtypeStruct((length, part), bf16)
    wide_shape = jax.ShapeDtypeStruct((length, part), f32)
    work = 2 * heads * length * length * HEAD_DIM
    params = pltpu.CompilerParams(vmem_limit_bytes=48 * 1024 * 1024)

    def forward(qkv, *rest):
        return pl.pallas_call(
            functools.partial(attend_body, block, scale),
            grid=(heads,),
            in_specs=[own(), own(heads), own(2 * heads)] + tables,
            out_specs=[own()] * 4 + [lse_spec],
            out_shape=[low_shape] * 4 + [jax.ShapeDtypeStruct((heads, length, 1), f32)],
            compiler_params=params,
            cost_estimate=pl.CostEstimate(
                flops=2 * work, bytes_accessed=20 * length * part, transcendentals=0
            ),
        )(qkv, qkv, qkv, *rest)

    def backward(query, key, value, attended, grad_att, lse, qkv, *rest):
        return pl.pallas_call(
            functools.partial(attend_back_body, block, scale),
            grid=(heads,),
            in_specs=[own()] * 5 + [lse_spec, own(), own(heads)] + tables,
            out_specs=[own()] * 3 + [gain_spec, same(HEAD_DIM)],
            out_shape=[
                wide_shape,
                wide_shape,
                low_shape,
                jax.ShapeDtypeStruct((8, part), f32),
                jax.ShapeDtypeStruct((length, HEAD_DIM), f32),
            ],
            scratch_shapes=[
                pltpu.VMEM((length, HEAD_DIM), bf16),
                pltpu.VMEM((length, HEAD_DIM), f32),
                pltpu.VMEM((length, HEAD_DIM), f32),
            ],
            compiler_params=params,
            cost_estimate=pl.CostEstimate(
                flops=5 * work, bytes_accessed=30 * length * part, transcendentals=0
            ),
        )(query, key, value, attended, grad_att, lse, qkv, qkv, *rest)

    return forward, backward


def qkv_back_body(query_grad, key_grad, value_grad, raw, inverse, inner, out):
    part = query_grad.shape[1]
    for column, grad in ((0, query_grad), (1, key_grad)):
        scale = inverse[:, column : column + 1]
        hat = raw[:, column * part : (column + 1) * part] * scale
        out[:, column * part : (column + 1) * part] = (
            scale * (grad[...] - hat * inner[:, column : column + 1])
        ).astype(bf16)
    out[:, 2 * part :] = value_grad[...]


def qkv_back(query_grad, key_grad, value_grad, qkv, inverse, inner):
    length, part = query_grad.shape
    rows = math.gcd(length, 256)

    def spec(width):
        return pl.BlockSpec((rows, width), lambda i: (i, 0))

    return pl.pallas_call(
        qkv_back_body,
        grid=(length // rows,),
        in_specs=[spec(part)] * 3 + [spec(2 * part), spec(2), spec(2)],
        out_specs=spec(3 * part),
        out_shape=jax.ShapeDtypeStruct((length, 3 * part), bf16),
        compiler_params=pltpu.CompilerParams(vmem_limit_bytes=40 * 1024 * 1024),
        cost_estimate=pl.CostEstimate(
            flops=8 * length * part, bytes_accessed=24 * length * part, transcendentals=0
        ),
    )(query_grad, key_grad, value_grad, qkv, inverse, inner)


def attn_grad_body(token, grad_qkv, attended, grad_branch, gain, out):
    wide, part = grad_qkv.shape[1], grad_branch.shape[1]
    out[:, :wide] = dot(token[...], grad_qkv[...], 1, 0).astype(bf16)
    out[:, wide : wide + part] = dot(attended[...], grad_branch[...], 1, 0).astype(bf16)
    gains = jnp.concatenate(
        [gain[...], jnp.zeros((GAIN_COLS - gain.shape[0], gain.shape[1]), f32)], axis=0
    )
    out[:, wide + part :] = jnp.transpose(gains).astype(bf16)


def attn_grad(token, grad_qkv, attended, grad_branch, gain):
    width, length = token.shape
    rows = math.gcd(width, 512)
    columns = grad_qkv.shape[1] + grad_branch.shape[1] + GAIN_COLS

    def row_spec(wide):
        return pl.BlockSpec((rows, wide), lambda i: (i, 0))

    def whole(array):
        return pl.BlockSpec(array.shape, lambda i: (0, 0))

    return pl.pallas_call(
        attn_grad_body,
        grid=(width // rows,),
        in_specs=[
            row_spec(length),
            whole(grad_qkv),
            row_spec(length),
            whole(grad_branch),
            pl.BlockSpec((gain.shape[0], rows), lambda i: (0, i)),
        ],
        out_specs=row_spec(columns),
        out_shape=jax.ShapeDtypeStruct((width, columns), bf16),
        compiler_params=pltpu.CompilerParams(vmem_limit_bytes=48 * 1024 * 1024),
        cost_estimate=pl.CostEstimate(
            flops=2 * width * length * columns,
            bytes_accessed=6 * width * length,
            transcendentals=0,
        ),
    )(token, grad_qkv, attended, grad_branch, gain)


def token_grad_body(place, grad_qkv, weight, grad_hidden, out):
    own = (pl.program_id(0) == place[0]).astype(f32)
    out[...] = (dot(grad_qkv[...], weight[...], 1, 1) + own * grad_hidden[...]).astype(bf16)


def token_grad(place, grad_qkv, weight, grad_hidden):
    length, wide = grad_qkv.shape
    width, part = weight.shape[0], grad_hidden.shape[1]
    return pl.pallas_call(
        token_grad_body,
        grid_spec=pltpu.PrefetchScalarGridSpec(
            num_scalar_prefetch=1,
            grid=(width // part,),
            in_specs=[
                pl.BlockSpec((length, wide), lambda j, place: (0, 0)),
                pl.BlockSpec((part, wide), lambda j, place: (j, 0)),
                pl.BlockSpec((length, part), lambda j, place: (0, 0)),
            ],
            out_specs=pl.BlockSpec((length, part), lambda j, place: (0, j)),
        ),
        out_shape=jax.ShapeDtypeStruct((length, width), bf16),
        compiler_params=pltpu.CompilerParams(vmem_limit_bytes=48 * 1024 * 1024),
        cost_estimate=pl.CostEstimate(
            flops=2 * width * length * wide, bytes_accessed=8 * width * length, transcendentals=0
        ),
    )(place, grad_qkv, weight, grad_hidden)


def gate_up_body(hidden, weight, both, activ):
    value = dot(hidden[...], weight[...], 1, 0)
    gate, up = value[:, :TILE], value[:, TILE:]
    sigmoid = jax.nn.sigmoid(gate)
    silu = gate * sigmoid
    activ[...] = (silu * up).astype(bf16)
    both[:, :TILE] = up * sigmoid * (1.0 + gate * (1.0 - sigmoid))
    both[:, TILE:] = silu


def gate_up_back_body(grad_mlp, weight, both, out):
    grad = dot(grad_mlp[...], weight[...], 1, 0)
    for start in (0, TILE):
        out[:, start : start + TILE] = (grad * both[:, start : start + TILE]).astype(bf16)


def gate_up_kernels(length, width, wide):
    params = pltpu.CompilerParams(vmem_limit_bytes=48 * 1024 * 1024)
    rows_spec = pl.BlockSpec((length, width), lambda j: (0, 0))

    def columns(rows, size):
        return pl.BlockSpec((rows, size), lambda j: (0, j))

    def forward(hidden, weight):
        return pl.pallas_call(
            gate_up_body,
            grid=(wide // TILE,),
            in_specs=[rows_spec, columns(width, 2 * TILE)],
            out_specs=[columns(length, 2 * TILE), columns(length, TILE)],
            out_shape=[
                jax.ShapeDtypeStruct((length, 2 * wide), f32),
                jax.ShapeDtypeStruct((length, wide), bf16),
            ],
            compiler_params=params,
            cost_estimate=pl.CostEstimate(
                flops=4 * length * width * wide,
                bytes_accessed=10 * length * wide + 4 * width * wide,
                transcendentals=0,
            ),
        )(hidden, weight)

    def backward(grad_mlp, weight, both):
        return pl.pallas_call(
            gate_up_back_body,
            grid=(wide // TILE,),
            in_specs=[rows_spec, columns(width, TILE), columns(length, 2 * TILE)],
            out_specs=columns(length, 2 * TILE),
            out_shape=jax.ShapeDtypeStruct((length, 2 * wide), bf16),
            compiler_params=params,
            cost_estimate=pl.CostEstimate(
                flops=2 * length * width * wide,
                bytes_accessed=12 * length * wide + 2 * width * wide,
                transcendentals=0,
            ),
        )(grad_mlp, weight, both)

    return forward, backward


FSDP, DP = ("y", "x"), ("z", "core")


def order_body(values, other, out):
    pass


def order(values, other):
    anywhere = pl.BlockSpec(memory_space=pl.ANY)
    return pl.pallas_call(
        order_body,
        in_specs=[anywhere, anywhere],
        out_specs=anywhere,
        out_shape=jax.ShapeDtypeStruct(values.shape, values.dtype),
        input_output_aliases={0: 0},
    )(values, other)


class Plane:
    def __init__(self, count):
        self.count = count
        self.square = count == 4
        self.place = lax.axis_index(FSDP)

    def swap(self, values, bit):
        return lax.ppermute(values, FSDP, [(i, i ^ bit) for i in range(self.count)])

    def gather(self, block, axis):
        if not self.square:
            return lax.all_gather(block, FSDP, axis=axis, tiled=True)
        other = 1 - axis
        size, cut = block.shape[axis], block.shape[other] // 2
        by_x, by_y = self.swap(block, 1), self.swap(block, 2)
        low = self.swap(lax.slice_in_dim(by_x, 0, cut, axis=other), 2)
        high = self.swap(lax.slice_in_dim(by_y, cut, 2 * cut, axis=other), 1)
        shape = list(block.shape)
        shape[axis] = size * 4
        out = jnp.zeros(shape, block.dtype)
        for part, bit, offset in ((block, 0, 0), (by_x, 1, 0), (by_y, 2, 0), (low, 3, 0), (high, 3, cut)):
            start = [0, 0]
            start[axis] = (self.place ^ bit) * size
            start[other] = offset
            out = lax.dynamic_update_slice(out, part, start)
        return out

    def scatter(self, partial, axis):
        if not self.square:
            total = lax.psum_scatter(partial, FSDP, scatter_dimension=axis, tiled=True)
            return total.astype(f32)
        other = 1 - axis
        size, cut = partial.shape[axis] // 4, partial.shape[other] // 2
        place = self.place

        def piece(bit, offset):
            start = [0, 0]
            start[axis] = (place ^ bit) * size
            start[other] = offset
            extent = [0, 0]
            extent[axis] = size
            extent[other] = cut
            return lax.dynamic_slice(partial, start, extent)

        halves = []
        for offset, first, second in ((0, 1, 2), (cut, 2, 1)):
            relay = self.swap(piece(3, offset), first)
            mine = self.swap(piece(first, offset), first)
            relay = (piece(second, offset).astype(f32) + relay.astype(f32)).astype(bf16)
            halves.append(
                piece(0, offset).astype(f32) + mine.astype(f32) + self.swap(relay, second).astype(f32)
            )
        return jnp.concatenate(halves, axis=other)

    def total(self, values):
        if not self.square:
            return lax.psum(values, FSDP)
        return values + self.swap(values, 1) + self.swap(values, 2) + self.swap(values, 3)

    def gather_small(self, values):
        if not self.square:
            return lax.all_gather(values, FSDP, axis=0, tiled=True)
        parts = [values] + [self.swap(values, bit) for bit in (1, 2, 3)]
        return jnp.concatenate(
            [
                lax.select_n(self.place ^ j, *parts)
                for j in range(4)
            ],
            axis=0,
        )


def per_device(
    tokens,
    positions,
    cotangent,
    w_attn,
    w_gate_up,
    w_down,
    gains,
    m_attn,
    v_attn,
    m_gate_up,
    v_gate_up,
    m_down,
    v_down,
    m_gains,
    v_gains,
):
    rows, width = tokens.shape
    owned = w_attn.shape[0]
    hidden = w_down.shape[1]
    count = lax.axis_size(FSDP)
    plane = Plane(count)
    place = plane.place
    length = rows * count
    part = width // count
    heads = part // HEAD_DIM
    wide = hidden // count
    scale = 1.0 / math.sqrt(HEAD_DIM)

    def spread(weight, groups, extra=None, tile=0):
        block = spread_kernel(weight, groups, count, extra, tile)
        return lax.all_to_all(block, FSDP, 0, 0, tiled=True)

    gain_block = jnp.pad(gains, ((0, 0), (0, GAIN_COLS - gains.shape[1])))
    attn_all = lax.all_gather(spread(w_attn, 4, gain_block), DP, axis=0, tiled=True)
    gate_up_all = lax.all_gather(spread(w_gate_up, 2, tile=TILE), DP, axis=0, tiled=True)
    down_all = lax.all_gather(spread(w_down, 1), DP, axis=0, tiled=True)
    qkv_weight = attn_all[:, : 3 * part]
    out_weight = attn_all[:, 3 * part : 4 * part]
    gain_values = attn_all[:, 4 * part : 4 * part + 4].astype(f32)
    gain_part = lax.dynamic_slice_in_dim(gain_values, place * part, part, 0)

    token_full = plane.gather(tokens, 0)
    position_full = plane.gather_small(positions)
    cot_part = lax.all_to_all(
        cotangent.reshape(rows, count, part).transpose(1, 0, 2).reshape(count * rows, part),
        FSDP,
        0,
        0,
        tiled=True,
    ).astype(f32)

    half_dim = HEAD_DIM // 2
    frequency = jnp.exp(
        jnp.arange(half_dim, dtype=f32) * (-2.0 * math.log(rope_base) / HEAD_DIM)
    )
    angles = position_full.astype(f32)[:, None] * frequency[None, :]
    cosine, sine = jnp.cos(angles), jnp.sin(angles)
    cosine = jnp.concatenate([cosine, cosine], axis=1)
    sine = jnp.concatenate([-sine, sine], axis=1)
    first_key = (jnp.arange(length, dtype=jnp.int32) - position_full)[:, None]
    gain_rows = jnp.pad(jnp.transpose(gain_part), ((0, 4), (0, 0)))
    attend, attend_back = attend_kernels(length, heads)

    qkv = mm(token_full, qkv_weight, ((1,), (0,)))
    query_raw, key_raw = qkv[:, :part], qkv[:, part : 2 * part]
    squares = plane.total(
        jnp.stack([jnp.sum(query_raw * query_raw, axis=1), jnp.sum(key_raw * key_raw, axis=1)])
    )
    inverse = jnp.transpose(lax.rsqrt(squares / width + norm_eps))
    tables = (inverse, gain_rows, cosine, sine, first_key)
    query, key, value, attended_low, lse = attend(qkv, *tables)
    attended_full = plane.gather(attended_low, 1)

    branch = mm(attended_full, out_weight, ((1,), (0,)))
    branch_inv = lax.rsqrt(plane.total(jnp.sum(branch * branch, axis=1)) / width + norm_eps)[:, None]
    branch_hat = branch * branch_inv
    token_part = lax.dynamic_slice_in_dim(token_full, place * part, part, 1).astype(f32)
    hidden_low = (token_part + branch_hat * gain_part[None, :, 2]).astype(bf16)
    hidden_full = plane.gather(hidden_low, 1)

    copies, core = lax.axis_size("z"), lax.axis_index("core")
    share = width // (2 * copies)

    def side(index):
        return jnp.concatenate(
            [
                lax.dynamic_slice_in_dim(hidden_full, (2 * z + index) * share, share, 1)
                for z in range(copies)
            ],
            axis=1,
        )

    other_side, own_side = side(1 - core), side(core)
    hidden_full = order(order(hidden_full, other_side), own_side)
    gate_up, gate_up_back = gate_up_kernels(length, width, wide)
    both, activ = gate_up(hidden_full, gate_up_all)
    mlp = plane.scatter(mm(activ, down_all, ((1,), (1,))).astype(bf16), 0)
    mlp_inv = lax.rsqrt(jnp.mean(mlp * mlp, axis=1, keepdims=True) + norm_eps)
    mlp_hat = mlp * mlp_inv
    hidden_rows = lax.dynamic_slice_in_dim(hidden_full, place * rows, rows, 0).astype(f32)
    output = (hidden_rows + mlp_hat * gain_values[None, :, 3]).astype(bf16)

    grad_out = cotangent.astype(f32)
    scaled = grad_out * gain_values[None, :, 3]
    grad_mlp = mlp_inv * (scaled - mlp_hat * jnp.mean(scaled * mlp_hat, axis=1, keepdims=True))
    grad_gain_mlp = jnp.sum(grad_out * mlp_hat, axis=0)
    grad_mlp_full = with_layout_constraint(
        plane.gather(grad_mlp.astype(bf16), 0), Layout(major_to_minor=(0, 1))
    )

    def reduced(partial, axes, wait=()):
        mine = lax.psum_scatter(partial, axes, scatter_dimension=0, tiled=True)
        for other in wait:
            mine = order(mine, other)
        return mine, lax.all_to_all(mine, FSDP, 0, 0, tiled=True)

    down_mine, down_part = reduced(mm(grad_mlp_full, activ, ((0,), (0,))).astype(bf16), DP)
    grad_gate_up_low = gate_up_back(grad_mlp_full, down_all, both)

    send = mm(other_side, grad_gate_up_low, ((0,), (0,))).astype(bf16)
    got = lax.ppermute(send, "core", [(0, 1), (1, 0)])
    late = order(grad_gate_up_low, send)
    keep = mm(own_side, late, ((0,), (0,))).astype(bf16)
    late = order(late, keep)
    grad_hidden = cot_part + plane.scatter(
        mm(late, gate_up_all, ((1,), (1,))).astype(bf16), 1
    )
    gate_up_partial = (keep.astype(f32) + got.astype(f32)).astype(bf16)
    gate_up_mine, gate_up_part = reduced(gate_up_partial, "z")

    scaled = grad_hidden * gain_part[None, :, 2]
    grad_gain_attn = jnp.sum(grad_hidden * branch_hat, axis=0)
    inner = plane.total(jnp.sum(scaled * branch_hat, axis=1))[:, None] / width
    grad_branch = (branch_inv * (scaled - branch_hat * inner)).astype(bf16)
    grad_branch = order(grad_branch, down_mine)
    grad_att = plane.scatter(mm(grad_branch, out_weight, ((1,), (1,))).astype(bf16), 1)
    query_grad, key_grad, value_grad, gain_grad, inner = attend_back(
        query, key, value, attended_low, grad_att, lse, qkv, *tables
    )
    inner = jnp.transpose(plane.total(jnp.transpose(inner[:, :2])) / width)
    grad_qkv_low = qkv_back(query_grad, key_grad, value_grad, qkv, inverse, inner)

    own_gains = jnp.concatenate([gain_grad[:2], grad_gain_attn[None], jnp.zeros((5, part), f32)])
    gain_rows = jnp.pad(grad_gain_mlp[None], ((3, 4), (0, 0)))
    gain_rows = lax.dynamic_update_slice(
        gain_rows,
        own_gains + lax.dynamic_slice_in_dim(gain_rows, place * part, part, 1),
        (0, place * part),
    )
    lefts = (jnp.transpose(token_full), grad_qkv_low, jnp.transpose(attended_full), grad_branch)
    attn_partial = attn_grad(*lefts, gain_rows)
    attn_partial = order(attn_partial, gate_up_mine)
    back = token_grad(
        jnp.full((1,), place), order(grad_qkv_low, attn_partial), attn_all, grad_hidden
    )
    grad_down, new_down, new_m_down, new_v_down = adamw_kernel(
        down_part, w_down, m_down, v_down, 1, count
    )
    grad_gate_up, new_gate_up, new_m_gate_up, new_v_gate_up = adamw_kernel(
        gate_up_part, w_gate_up, m_gate_up, v_gate_up, 2, count, TILE
    )
    _, attn_part = reduced(attn_partial, DP, (new_down, new_gate_up))
    grad_gains = jnp.sum(
        attn_part[:, 4 * part : 4 * part + 4].reshape(count, owned, 4).astype(f32), axis=0
    )

    grad_tokens = plane.scatter(back, 0)
    grad_attn, new_attn, new_m_attn, new_v_attn = adamw_kernel(
        attn_part, w_attn, m_attn, v_attn, 4, count
    )
    new_gains, new_m_gains, new_v_gains = adamw_step(
        gains, grad_gains, m_gains, v_gains, 0.0, gain_rate
    )
    return (
        output,
        grad_tokens,
        grad_attn,
        grad_gate_up,
        grad_down,
        grad_gains,
        new_attn,
        new_gate_up,
        new_down,
        new_gains,
        new_m_attn,
        new_v_attn,
        new_m_gate_up,
        new_v_gate_up,
        new_m_down,
        new_v_down,
        new_m_gains,
        new_v_gains,
    )


def solution(mesh):
    copies, places = mesh.devices.shape
    mesh = Mesh(mesh.devices.reshape(copies // 2, 2, 2, places // 2), DP + FSDP)
    matrix, vector = P(DP + FSDP, None), P(DP + FSDP)
    in_specs = (matrix, vector) + (matrix,) * 13
    return jax.shard_map(
        per_device, mesh=mesh, in_specs=in_specs, out_specs=(matrix,) * 18, check_vma=False
    )
```

time: 1010 us -> 841 us (0.83)
  Pallas kernels: 0 us -> 129 us
  waiting for transfers between devices: 425 us -> 311 us
  matrix products: 205 us -> 95.8 us
  other arithmetic: 101 us -> 49.9 us
  local copies, waits for them, and re-layouts: 126 us -> 91.9 us
  blocking collectives: 48.7 us -> 63 us
    reduce_scatter x3, waiting for transfers between devices: 133 us -> 0.01 us  [reduced(): mine = lax.psum_scatter(partial, axes, scatter_dimension=0, tiled=True)]
    pallas_call x0 -> x22, Pallas kernels: none -> 129 us  [the longest x3 25 us: adamw_kernel(): pl.pallas_call(functools.partial(adamw_body, tile), grid=(count, groups),...]
    dot_general x12 -> x8, matrix products: 160 us -> 95.8 us  [mm(): lax.dot_general(left, right, (dims, ((), ())), preferred_element_type=f32)]
    ppermute x55 -> x56, waiting for transfers between devices: 204 us -> 259 us  [the longest x55 257 us: swap(): return lax.ppermute(values, FSDP, [(i, i ^ bit) for i in range(self.count)])]
    dot_general x6 -> x0, matrix products: 45.1 us -> none  [the longest x1 12.4 us: per_device(): jnp.einsum('hqk,khd->qhd', weights.astype(bf16), value, preferred_element...]
    convert_element_type x8 -> x0, local copies, waits for them, and re-layouts: 31.4 us -> none  [the longest x4 22.1 us: reduced(): return got.reshape(count, owned, groups, columns).transpose(1, 2, 0, 3).r...]
    sub x4 -> x1, other arithmetic: 25.1 us -> 0.6 us  [adamw_step(): weight * (1.0 - rate_value * decay_coef) - rate_value * step_ratio]
    all_to_all x4 -> x3, waiting for transfers between devices: 30.6 us -> 7.04 us  [reduced(): return (mine, lax.all_to_all(mine, FSDP, 0, 0, tiled=True))]
  transfers between devices with their start and end apart: 66 -> 66, of which waited for: 46 -> 42; matrix products, arithmetic and copies ran while one was open for 34% -> 20% of each run, Pallas kernels for 0% -> 14%
where the time goes in v2:
time: 841 us; the launch traced here: 834 us
  waiting for transfers between devices  311 us (37%)
  Pallas kernels  129 us (15%)
  matrix products  95.8 us (11%)
  local copies, waits for them, and re-layouts  91.9 us (11%)
  starting transfers between devices  78.7 us (9%)
  blocking collectives  63 us (7%)
  other arithmetic  49.9 us (6%)
  between operations  15.5 us (2%)
    ppermute x55, waiting for transfers between devices, swap(): return lax.ppermute(values, FSDP, [(i, i ^ bit) for i in range(self.count)])  257 us
    dot_general x8, matrix products, mm(): lax.dot_general(left, right, (dims, ((), ())), preferred_element_type=f32)  95.8 us
    all_to_all x3, blocking collectives, spread(): return lax.all_to_all(block, FSDP, 0, 0, tiled=True)  63 us
    ppermute x55, starting transfers between devices, swap(): return lax.ppermute(values, FSDP, [(i, i ^ bit) for i in range(self.count)])  62.4 us
    unnamed x125, local copies, waits for them, and re-layouts  37.4 us
    all_gather x1, waiting for transfers between devices, per_device(): down_all = lax.all_gather(spread(w_down, 1), DP, axis=0, tiled=True)  37.2 us
    pallas_call x3, Pallas kernels, adamw_kernel(): pl.pallas_call(functools.partial(adamw_body, tile), grid=(count, groups),...  25 us
    pallas_call x1, Pallas kernels, forward(): pl.pallas_call(gate_up_body, grid=(wide // TILE,), in_specs=[rows_spec, c...  24.8 us
  transfers between devices with their start and end apart: 66, of which 42 were waited for; matrix products, arithmetic and copies ran while one was open for 20% of the time, Pallas kernels for 14%

profile of v2, /device:TPU:0, one launch (start us, length us, event | category | flops | bytes accessed | tf_op | source)
XLA Modules:
  0.0 834.3 jit_solution(14705068153426350142)
XLA Ops:
  10.0 20.1 %all_to_all.75 = bf16[4,64,2176]{2,1,0:T(8,128)(2,1)} all-to-all(bf16[4,64,2176]{2,1,0:T(8,128)(2,1)S(1)} %bitcast.60), channel_id=1, replica_groups=mesh['z'=4,'core'=2,'y'=2,'x'=2] {'y','x'}, dimensions={0} | all-to-all | bytes 2228224 | tf_op jit(solution)/shard_map/all_to_all | solution.py:542
  33.0 27.6 %all_to_all.76 = bf16[4,64,4096]{2,1,0:T(8,128)(2,1)} all-to-all(bf16[4,64,4096]{2,1,0:T(8,128)(2,1)S(1)} %bitcast.57), channel_id=1, replica_groups=mesh['z'=4,'core'=2,'y'=2,'x'=2] {'y','x'}, dimensions={0} | all-to-all | bytes 4194304 | tf_op jit(solution)/shard_map/all_to_all | solution.py:542
  61.1 15.3 %all_to_all.77 = bf16[4,64,2048]{2,1,0:T(8,128)(2,1)} all-to-all(bf16[4,64,2048]{2,1,0:T(8,128)(2,1)S(1)} %bitcast.62), channel_id=1, replica_groups=mesh['z'=4,'core'=2,'y'=2,'x'=2] {'y','x'}, dimensions={0} | all-to-all | bytes 2097152 | tf_op jit(solution)/shard_map/all_to_all | solution.py:542
  85.0 13.1 %collective-permute-done.7 = s32[256]{0:T(256)S(1)} collective-permute-done((s32[256]{0:T(256)S(1)}, s32[256]{0:T(256)S(1)}, u32[]{:S(2)}, u32[]{:S(2)}) %collective-permute-start.7) | collective-permute-done | bytes 1056 | tf_op jit(solution)/shard_map/ppermute | solution.py:446
  116.2 10.2 %fusion.refs_0_.refs_1_.refs_2_.refs_6_.refs_7_.raw = f32[1024,1536]{1,0:T(8,128)S(1)} fusion(bf16[1024,2048]{1,0:T(8,128)(2,1)} %constant_dynamic-update-slice_fusion.19, bf16[2048,2176]{1,0:T(8,128)(2,1)} %all-gather.4.cloned.1.call-done.weight), kind=kOutput, calls=%fused_computation.4 | convolution fusion | flops 6442450944 | bytes 16777216 | tf_op jit(solution)/shard_map/dot_general | solution.py:33
  136.6 20.6 %collective-permute-done.5 = f32[2,1024]{0,1:T(8,128)S(1)} collective-permute-done((f32[2,1024]{0,1:T(8,128)S(1)}, f32[2,1024]{0,1:T(8,128)S(1)}, u32[]{:S(2)}, u32[]{:S(2)}) %collective-permute-start.5) | collective-permute-done | bytes 8224 | tf_op jit(solution)/shard_map/ppermute | solution.py:446
  158.3 17.7 %shard_map.287 = (bf16[1024,512]{1,0:T(8,128)(2,1)S(1)}, bf16[1024,512]{1,0:T(8,128)(2,1)S(1)}, bf16[1024,512]{1,0:T(8,128)(2,1)S(1)}, bf16[1024,512]{1,0:T(8,128)(2,1)}, f32[4,1024,1]{2,1,0:T(8,128)}) custom-call(f32[1024,1536]{1,0:T(8,128)} %copy-done.27, f32[1024,1536]{1,0:T(8,128)} %copy-done.27, f32[1024,1536]{1,0:T(8,128)} %copy-done.27, ...), custom_call_target="tpu_custom_call" | custom-call | flops 2147483648 | bytes 10485760 | tf_op jit(solution)/shard_map/pallas_call | solution.py:222
  180.0 22.4 %collective-permute-done.10 = bf16[1024,512]{1,0:T(8,128)(2,1)S(1)} collective-permute-done((bf16[1024,512]{1,0:T(8,128)(2,1)}, bf16[1024,512]{1,0:T(8,128)(2,1)S(1)}, u32[]{:S(2)}, u32[]{:S(2)}) %collective-permute-start.10) | collective-permute-done | bytes 1048608 | tf_op jit(solution)/shard_map/ppermute | solution.py:446
  209.2 6.7 collective-permute-done.12
  218.3 6.9 multiply_reduce_fusion.3
  239.4 20.3 %collective-permute-done.17 = bf16[1024,512]{1,0:T(8,128)(2,1)S(1)} collective-permute-done((bf16[1024,512]{1,0:T(8,128)(2,1)S(1)}, bf16[1024,512]{1,0:T(8,128)(2,1)S(1)}, u32[]{:S(2)}, u32[]{:S(2)}) %collective-permute-start.17) | collective-permute-done | bytes 1048608 | tf_op jit(solution)/shard_map/ppermute | solution.py:446
  285.4 24.8 %shard_map.291 = (f32[1024,4096]{1,0:T(8,128)}, bf16[1024,2048]{1,0:T(8,128)(2,1)S(1)}) custom-call(bf16[1024,2048]{1,0:T(8,128)(2,1)} %shard_map.289.hidden, bf16[2048,4096]{1,0:T(8,128)(2,1)} %all-gather.6.cloned.1.call-done.weight), custom_call_target="tpu_custom_call" | custom-call | flops 17179869184 | bytes 37748736 | tf_op jit(solution)/shard_map/pallas_call | solution.py:386
  312.2 37.2 %all-gather.8.cloned.1.call-done.weight = bf16[2048,2048]{1,0:T(8,128)(2,1)} async-done(((bf16[256,2048]{1,0:T(8,128)(2,1)}), bf16[2048,2048]{1,0:T(8,128)(2,1)}) %all-gather.8.cloned.1.call-update) | async-done | bytes 8388624 | tf_op jit(solution)/shard_map/all_gather | solution.py:547
  349.4 13.0 %convolution_convert_fusion.5 = bf16[1024,2048]{1,0:T(8,128)(2,1)S(1)} fusion(bf16[1024,2048]{1,0:T(8,128)(2,1)} %copy-done.25, bf16[2048,2048]{1,0:T(8,128)(2,1)} %all-gather.8.cloned.1.call-done.weight), kind=kOutput, calls=%fused_computation.8 | convolution fusion | flops 8592031744 | bytes 16777216 | tf_op jit(solution)/shard_map/dot_general | solution.py:33
  366.2 11.2 %collective-permute-done.22 = bf16[256,1024]{1,0:T(8,128)(2,1)S(1)} collective-permute-done((bf16[256,1024]{1,0:T(8,128)(2,1)S(1)}, bf16[256,1024]{1,0:T(8,128)(2,1)S(1)}, u32[]{:S(2)}, u32[]{:S(2)}) %collective-permute-start.22) | collective-permute-done | bytes 524320 | tf_op jit(solution)/shard_map/ppermute | solution.py:446
  379.8 8.3 collective-permute-done.21
  388.0 4.6 collective-permute-done.23
  395.3 6.3 collective-permute-done.24
  410.2 19.0 %collective-permute-done.27 = bf16[256,2048]{1,0:T(8,128)(2,1)S(1)} collective-permute-done((bf16[256,2048]{1,0:T(8,128)(2,1)S(1)}, bf16[256,2048]{1,0:T(8,128)(2,1)S(1)}, u32[]{:S(2)}, u32[]{:S(2)}) %collective-permute-start.27) | collective-permute-done | bytes 1048608 | tf_op jit(solution)/shard_map/ppermute | solution.py:446
  433.4 8.2 collective-permute-done.29
  442.3 11.4 %convolution_convert_fusion = bf16[2048,2048]{1,0:T(8,128)(2,1)} fusion(bf16[1024,2048]{1,0:T(8,128)(2,1)S(1)} %constant_dynamic-update-slice_fusion.18.grad_mlp, bf16[1024,2048]{1,0:T(8,128)(2,1)S(1)} %copy-done.26), kind=kOutput, calls=%fused_computation.1 | convolution fusion | flops 8594128896 | bytes 16777216 | tf_op jit(solution)/shard_map/dot_general | solution.py:33
  458.0 16.7 %shard_map.293.values = bf16[1024,4096]{1,0:T(8,128)(2,1)} custom-call(bf16[1024,2048]{1,0:T(8,128)(2,1)S(1)} %copy-done.5, bf16[2048,2048]{1,0:T(8,128)(2,1)} %all-gather.8.cloned.1.call-done.weight, f32[1024,4096]{1,0:T(8,128)} %get-tuple-element.47.both), custom_call_target="tpu_custom_call" | custom-call | flops 8589934592 | bytes 33554432 | tf_op jit(solution)/shard_map/pallas_call | solution.py:404
  474.7 15.0 %convolution_convert_fusion.2.other = bf16[1024,4096]{1,0:T(8,128)(2,1)} fusion(bf16[1024,4096]{1,0:T(8,128)(2,1)} %shard_map.293.values, bf16[1024,256]{1,0:T(8,128)(2,1)S(1)} %copy-done.44, bf16[1024,256]{1,0:T(8,128)(2,1)S(1)} %copy-done.46, bf16[1024,256]{1,0:T(8,128)(2,1)S(1)} %copy-done.48, bf16[1024,256]{1,0:T(8,128)(2,1)S(1)} %copy-done.50), kind=kOutput, calls=%fused_computation.3 | convolution fusion | flops 8602517504 | bytes 18874368 | tf_op jit(solution)/shard_map/dot_general | solution.py:33
  489.7 11.8 %convolution_convert_fusion.1.other = bf16[1024,4096]{1,0:T(8,128)(2,1)S(1)} fusion(bf16[1024,4096]{1,0:T(8,128)(2,1)} %shard_map.294.values, bf16[1024,256]{1,0:T(8,128)(2,1)} %get-tuple-element.141, bf16[1024,256]{1,0:T(8,128)(2,1)} %get-tuple-element.142, bf16[1024,256]{1,0:T(8,128)(2,1)} %get-tuple-element.143, bf16[1024,256]{1,0:T(8,128)(2,1)S(1)} %get-tuple-element.140), kind=kOutput, calls=%fused_computation.2 | convolution fusion | flops 8602517504 | bytes 18874368 | tf_op jit(solution)/shard_map/dot_general | solution.py:33
  504.7 8.5 %add_convert_fusion = bf16[1024,4096]{1,0:T(8,128)(2,1)} fusion(bf16[1024,4096]{1,0:T(8,128)(2,1)} %collective-permute-done.49, bf16[1024,4096]{1,0:T(8,128)(2,1)S(1)} %convolution_convert_fusion.1.other), kind=kLoop, calls=%fused_computation | loop fusion | flops 16777216 | bytes 25165824 | tf_op jit(solution)/shard_map/convert_element_type | solution.py:639
  513.2 23.1 %convolution_convert_fusion.3 = bf16[1024,2048]{1,0:T(8,128)(2,1)S(1)} fusion(bf16[1024,4096]{1,0:T(8,128)(2,1)} %shard_map.295, bf16[2048,4096]{1,0:T(8,128)(2,1)} %all-gather.6.cloned.1.call-done.weight), kind=kOutput, calls=%fused_computation.6 | convolution fusion | flops 17181966336 | bytes 29360128 | tf_op jit(solution)/shard_map/dot_general | solution.py:33
  540.1 11.4 %collective-permute-done.32 = bf16[512,512]{1,0:T(8,128)(2,1)S(1)} collective-permute-done((bf16[512,512]{1,0:T(8,128)(2,1)S(1)}, bf16[512,512]{1,0:T(8,128)(2,1)S(1)}, u32[]{:S(2)}, u32[]{:S(2)}) %collective-permute-start.32) | collective-permute-done | bytes 524320 | tf_op jit(solution)/shard_map/ppermute | solution.py:446
  553.7 8.6 %collective-permute-done.31 = bf16[512,512]{1,0:T(8,128)(2,1)S(1)} collective-permute-done((bf16[512,512]{1,0:T(8,128)(2,1)S(1)}, bf16[512,512]{1,0:T(8,128)(2,1)S(1)}, u32[]{:S(2)}, u32[]{:S(2)}) %collective-permute-start.31) | collective-permute-done | bytes 524320 | tf_op jit(solution)/shard_map/ppermute | solution.py:446
  573.6 5.9 collective-permute-done.34
  585.9 4.7 all-to-all-done.3
  603.7 4.3 convolution_convert_fusion.4
  611.8 11.4 %collective-permute-done.41 = bf16[512,512]{1,0:T(8,128)(2,1)S(1)} collective-permute-done((bf16[512,512]{1,0:T(8,128)(2,1)S(1)}, bf16[512,512]{1,0:T(8,128)(2,1)S(1)}, u32[]{:S(2)}, u32[]{:S(2)}) %collective-permute-start.41) | collective-permute-done | bytes 524320 | tf_op jit(solution)/shard_map/ppermute | solution.py:446
  628.8 7.6 collective-permute-done.42
  639.2 6.6 copy.92.token
  645.8 6.4 copy.93.attended
  656.7 16.4 %shard_map.297 = (f32[1024,512]{1,0:T(8,128)}, f32[1024,512]{1,0:T(8,128)}, bf16[1024,512]{1,0:T(8,128)(2,1)S(1)}, f32[8,512]{1,0:T(8,128)S(1)}, f32[1024,128]{1,0:T(8,128)S(1)}) custom-call(bf16[1024,512]{1,0:T(8,128)(2,1)S(1)} %get-tuple-element.44.refs_0_, bf16[1024,512]{1,0:T(8,128)(2,1)S(1)} %copy-done.23, bf16[1024,512]{1,0:T(8,128)(2,1)} %copy-done.24, ...), custom_call_target="tpu_custom_call" | custom-call | flops 5368709120 | bytes 15728640 | tf_op jit(solution)/shard_map/pallas_call | solution.py:235
  676.7 5.6 collective-permute-done.46
  682.3 6.5 collective-permute-done.47
  694.1 13.5 %shard_map.299.values = bf16[2048,2176]{1,0:T(8,128)(2,1)} custom-call(bf16[2048,1024]{1,0:T(8,128)(2,1)} %copy.92.token, bf16[1024,1536]{1,0:T(8,128)(2,1)S(1)} %shard_map.298.grad_qkv.values, bf16[2048,1024]{1,0:T(8,128)(2,1)} %copy.93.attended, bf16[1024,512]{1,0:T(8,128)(2,1)S(1)} %copy-done.15, f32[8,2048]{1,0:T(8,128)S(1)} %fusion.16.gain), custom_call_target="tpu_custom_call" | custom-call | flops 9126805504 | bytes 12582912 | tf_op jit(solution)/shard_map/pallas_call | solution.py:313
  714.8 9.7 %shard_map.302 = bf16[1024,2048]{1,0:T(8,128)(2,1)} custom-call(s32[1]{0:T(128)} %bitcast.14.place, bf16[1024,1536]{1,0:T(8,128)(2,1)S(1)} %copy-done.7, bf16[2048,2176]{1,0:T(8,128)(2,1)} %all-gather.4.cloned.1.call-done.weight, f32[1024,512]{1,0:T(8,128)S(1)} %copy-done.13), custom_call_target="tpu_custom_call" | custom-call | flops 6442450944 | bytes 16777216 | tf_op jit(solution)/shard_map/pallas_call | solution.py:342
  729.3 4.6 all-to-all-start.5
  737.4 5.2 collective-permute-done.51
  746.1 19.4 %collective-permute-done.50 = bf16[256,1024]{1,0:T(8,128)(2,1)S(1)} collective-permute-done((bf16[256,1024]{1,0:T(8,128)(2,1)}, bf16[256,1024]{1,0:T(8,128)(2,1)S(1)}, u32[]{:S(2)}, u32[]{:S(2)}) %collective-permute-start.50) | collective-permute-done | bytes 524320 | tf_op jit(solution)/shard_map/ppermute | solution.py:446
  765.8 8.4 %collective-permute-done.52 = bf16[256,1024]{1,0:T(8,128)(2,1)S(1)} collective-permute-done((bf16[256,1024]{1,0:T(8,128)(2,1)S(1)}, bf16[256,1024]{1,0:T(8,128)(2,1)S(1)}, u32[]{:S(2)}, u32[]{:S(2)}) %collective-permute-start.52) | collective-permute-done | bytes 524320 | tf_op jit(solution)/shard_map/ppermute | solution.py:446
  778.5 4.9 shard_map.303
  788.0 12.6 %shard_map.305 = (f32[64,16384]{1,0:T(8,128)}, f32[64,16384]{1,0:T(8,128)}, f32[64,16384]{1,0:T(8,128)}, f32[64,16384]{1,0:T(8,128)}) custom-call(bf16[256,4096]{1,0:T(8,128)(2,1)} %bitcast.26.refs_0_, f32[64,16384]{1,0:T(8,128)S(1)} %copy-done.3, f32[64,16384]{1,0:T(8,128)S(1)} %copy-done.14, f32[64,16384]{1,0:T(8,128)} %refs_3_.6), custom_call_target="tpu_custom_call" | custom-call | flops 12582912 | bytes 31457280 | tf_op jit(solution)/shard_map/pallas_call | solution.py:108
  808.6 7.0 all-to-all-done.6
  818.9 7.5 shard_map.307
  (344 shorter events, 230.5 us)
Async XLA Ops:
  7.2 109.0 %all-gather.4.cloned.1.call-start = ((), (), s32[]{:S(2)}) async-start(), calls=%async_computation.10 | async-start | bytes 10027008 | tf_op jit(solution)/shard_map/all_gather | solution.py:545
  30.1 255.3 %all-gather.6.cloned.1.call-start = ((), (), s32[]{:S(2)}) async-start(), calls=%async_computation.11 | async-start | bytes 18874368 | tf_op jit(solution)/shard_map/all_gather | solution.py:546
  60.7 288.7 %all-gather.8.cloned.1.call-start = ((), (), s32[]{:S(2)}) async-start(), calls=%async_computation.12 | async-start | bytes 9437184 | tf_op jit(solution)/shard_map/all_gather | solution.py:547
  76.4 527.3 %reduce-scatter.4.cloned.1.call-start = ((), (), s32[]{:S(2)}) async-start(), calls=%async_computation.13 | async-start | bytes 9437184 | tf_op jit(solution)/shard_map/reduce_scatter | solution.py:623
  76.5 24.6 %collective-permute-start = (bf16[256,2048]{1,0:T(8,128)(2,1)}, bf16[256,2048]{1,0:T(8,128)(2,1)S(1)}, u32[]{:S(2)}, u32[]{:S(2)}) collective-permute-start(bf16[256,2048]{1,0:T(8,128)(2,1)} %param.15), channel_id=1, source_target_pairs={{0,1},{1,0},{2,3},{3,2},{4,5},{5,4},{6,7},{7,6},{8,9},{9,8},{10,11... | collective-permute-start | bytes 3145736 | tf_op jit(solution)/shard_map/ppermute | solution.py:446
  77.8 24.4 %collective-permute-start.1 = (bf16[256,2048]{1,0:T(8,128)(2,1)}, bf16[256,2048]{1,0:T(8,128)(2,1)}, u32[]{:S(2)}, u32[]{:S(2)}) collective-permute-start(bf16[256,2048]{1,0:T(8,128)(2,1)} %param.15), channel_id=1, source_target_pairs={{0,2},{1,3},{2,0},{3,1},{4,6},{5,7},{6,4},{7,5},{8,10},{9,11},{10,... | collective-permute-start | bytes 3145736 | tf_op jit(solution)/shard_map/ppermute | solution.py:446
  77.9 20.1 %collective-permute-start.7 = (s32[256]{0:T(256)S(1)}, s32[256]{0:T(256)S(1)}, u32[]{:S(2)}, u32[]{:S(2)}) collective-permute-start(s32[256]{0:T(256)S(1)} %copy-done.60), channel_id=1, source_target_pairs={{0,1},{1,0},{2,3},{3,2},{4,5},{5,4},{6,7},{7,6},{8,9},{9,8},{10,11... | collective-permute-start | bytes 3080 | tf_op jit(solution)/shard_map/ppermute | solution.py:446
  79.8 18.9 %collective-permute-start.8 = (s32[256]{0:T(256)S(1)}, s32[256]{0:T(256)S(1)}, u32[]{:S(2)}, u32[]{:S(2)}) collective-permute-start(s32[256]{0:T(256)S(1)} %copy-done.60), channel_id=1, source_target_pairs={{0,2},{1,3},{2,0},{3,1},{4,6},{5,7},{6,4},{7,5},{8,10},{9,11},{10,... | collective-permute-start | bytes 3080 | tf_op jit(solution)/shard_map/ppermute | solution.py:446
  80.6 18.3 %collective-permute-start.9 = (s32[256]{0:T(256)S(1)}, s32[256]{0:T(256)S(1)}, u32[]{:S(2)}, u32[]{:S(2)}) collective-permute-start(s32[256]{0:T(256)S(1)} %copy-done.60), channel_id=1, source_target_pairs={{0,3},{1,2},{2,1},{3,0},{4,7},{5,6},{6,5},{7,4},{8,11},{9,10},{10,... | collective-permute-start | bytes 3080 | tf_op jit(solution)/shard_map/ppermute | solution.py:446
  132.1 25.1 %collective-permute-start.5 = (f32[2,1024]{0,1:T(8,128)S(1)}, f32[2,1024]{0,1:T(8,128)S(1)}, u32[]{:S(2)}, u32[]{:S(2)}) collective-permute-start(f32[2,1024]{0,1:T(8,128)S(1)} %copy.84), channel_id=1, source_target_pairs={{0,2},{1,3},{2,0},{3,1},{4,6},{5,7},{6,4},{7,5},{8,10},{9,11},{10,... | collective-permute-start | bytes 24584 | tf_op jit(solution)/shard_map/ppermute | solution.py:446
  133.6 23.5 %collective-permute-start.6 = (f32[2,1024]{0,1:T(8,128)S(1)}, f32[2,1024]{0,1:T(8,128)}, u32[]{:S(2)}, u32[]{:S(2)}) collective-permute-start(f32[2,1024]{0,1:T(8,128)S(1)} %copy.84), channel_id=1, source_target_pairs={{0,3},{1,2},{2,1},{3,0},{4,7},{5,6},{6,5},{7,4},{8,11},{9,10},{10,... | collective-permute-start | bytes 24584 | tf_op jit(solution)/shard_map/ppermute | solution.py:446
  178.0 24.5 %collective-permute-start.10 = (bf16[1024,512]{1,0:T(8,128)(2,1)}, bf16[1024,512]{1,0:T(8,128)(2,1)S(1)}, u32[]{:S(2)}, u32[]{:S(2)}) collective-permute-start(bf16[1024,512]{1,0:T(8,128)(2,1)} %get-tuple-element.42.refs_3_), channel_id=1, source_target_pairs={{0,1},{1,0},{2,3},{3,2},{4,5},{5,4},{6,7},{7,6},{8,9},{9,8},{10,11... | collective-permute-start | bytes 3145736 | tf_op jit(solution)/shard_map/ppermute | solution.py:446
  178.5 26.5 %collective-permute-start.11 = (bf16[1024,512]{1,0:T(8,128)(2,1)}, bf16[1024,512]{1,0:T(8,128)(2,1)}, u32[]{:S(2)}, u32[]{:S(2)}) collective-permute-start(bf16[1024,512]{1,0:T(8,128)(2,1)} %get-tuple-element.42.refs_3_), channel_id=1, source_target_pairs={{0,2},{1,3},{2,0},{3,1},{4,6},{5,7},{6,4},{7,5},{8,10},{9,11},{10,... | collective-permute-start | bytes 3145736 | tf_op jit(solution)/shard_map/ppermute | solution.py:446
  238.2 21.5 %collective-permute-start.17 = (bf16[1024,512]{1,0:T(8,128)(2,1)S(1)}, bf16[1024,512]{1,0:T(8,128)(2,1)S(1)}, u32[]{:S(2)}, u32[]{:S(2)}) collective-permute-start(bf16[1024,512]{1,0:T(8,128)(2,1)S(1)} %get-tuple-element.115), channel_id=1, source_target_pairs={{0,1},{1,0},{2,3},{3,2},{4,5},{5,4},{6,7},{7,6},{8,9},{9,8},{10,11... | collective-permute-start | bytes 3145736 | tf_op jit(solution)/shard_map/ppermute | solution.py:446
  238.9 22.4 %collective-permute-start.18 = (bf16[1024,512]{1,0:T(8,128)(2,1)S(1)}, bf16[1024,512]{1,0:T(8,128)(2,1)S(1)}, u32[]{:S(2)}, u32[]{:S(2)}) collective-permute-start(bf16[1024,512]{1,0:T(8,128)(2,1)S(1)} %get-tuple-element.115), channel_id=1, source_target_pairs={{0,2},{1,3},{2,0},{3,1},{4,6},{5,7},{6,4},{7,5},{8,10},{9,11},{10,... | collective-permute-start | bytes 3145736 | tf_op jit(solution)/shard_map/ppermute | solution.py:446
  362.6 14.8 %collective-permute-start.22 = (bf16[256,1024]{1,0:T(8,128)(2,1)S(1)}, bf16[256,1024]{1,0:T(8,128)(2,1)S(1)}, u32[]{:S(2)}, u32[]{:S(2)}) collective-permute-start(bf16[256,1024]{1,0:T(8,128)(2,1)S(1)} %get-tuple-element.139), channel_id=1, source_target_pairs={{0,1},{1,0},{2,3},{3,2},{4,5},{5,4},{6,7},{7,6},{8,9},{9,8},{10,11... | collective-permute-start | bytes 1572872 | tf_op jit(solution)/shard_map/ppermute | solution.py:446
  364.2 23.8 %collective-permute-start.21 = (bf16[256,1024]{1,0:T(8,128)(2,1)S(1)}, bf16[256,1024]{1,0:T(8,128)(2,1)S(1)}, u32[]{:S(2)}, u32[]{:S(2)}) collective-permute-start(bf16[256,1024]{1,0:T(8,128)(2,1)S(1)} %get-tuple-element.136), channel_id=1, source_target_pairs={{0,1},{1,0},{2,3},{3,2},{4,5},{5,4},{6,7},{7,6},{8,9},{9,8},{10,11... | collective-permute-start | bytes 1572872 | tf_op jit(solution)/shard_map/ppermute | solution.py:446
  364.7 23.3 %collective-permute-start.25 = (bf16[256,1024]{1,0:T(8,128)(2,1)S(1)}, bf16[256,1024]{1,0:T(8,128)(2,1)S(1)}, u32[]{:S(2)}, u32[]{:S(2)}) collective-permute-start(bf16[256,1024]{1,0:T(8,128)(2,1)S(1)} %get-tuple-element.137), channel_id=1, source_target_pairs={{0,2},{1,3},{2,0},{3,1},{4,6},{5,7},{6,4},{7,5},{8,10},{9,11},{10,... | collective-permute-start | bytes 1572872 | tf_op jit(solution)/shard_map/ppermute | solution.py:446
  377.7 14.9 %collective-permute-start.23 = (bf16[256,1024]{1,0:T(8,128)(2,1)S(1)}, bf16[256,1024]{1,0:T(8,128)(2,1)S(1)}, u32[]{:S(2)}, u32[]{:S(2)}) collective-permute-start(bf16[256,1024]{1,0:T(8,128)(2,1)S(1)} %add_convert_fusion.10), channel_id=1, source_target_pairs={{0,2},{1,3},{2,0},{3,1},{4,6},{5,7},{6,4},{7,5},{8,10},{9,11},{10,... | collective-permute-start | bytes 1572872 | tf_op jit(solution)/shard_map/ppermute | solution.py:446
  379.2 22.3 %collective-permute-start.24 = (bf16[256,1024]{1,0:T(8,128)(2,1)S(1)}, bf16[256,1024]{1,0:T(8,128)(2,1)S(1)}, u32[]{:S(2)}, u32[]{:S(2)}) collective-permute-start(bf16[256,1024]{1,0:T(8,128)(2,1)S(1)} %get-tuple-element.138), channel_id=1, source_target_pairs={{0,2},{1,3},{2,0},{3,1},{4,6},{5,7},{6,4},{7,5},{8,10},{9,11},{10,... | collective-permute-start | bytes 1572872 | tf_op jit(solution)/shard_map/ppermute | solution.py:446
  407.2 22.0 %collective-permute-start.27 = (bf16[256,2048]{1,0:T(8,128)(2,1)S(1)}, bf16[256,2048]{1,0:T(8,128)(2,1)S(1)}, u32[]{:S(2)}, u32[]{:S(2)}) collective-permute-start(bf16[256,2048]{1,0:T(8,128)(2,1)S(1)} %get-tuple-element.113), channel_id=1, source_target_pairs={{0,1},{1,0},{2,3},{3,2},{4,5},{5,4},{6,7},{7,6},{8,9},{9,8},{10,11... | collective-permute-start | bytes 3145736 | tf_op jit(solution)/shard_map/ppermute | solution.py:446
  408.7 24.2 %collective-permute-start.28 = (bf16[256,2048]{1,0:T(8,128)(2,1)S(1)}, bf16[256,2048]{1,0:T(8,128)(2,1)S(1)}, u32[]{:S(2)}, u32[]{:S(2)}) collective-permute-start(bf16[256,2048]{1,0:T(8,128)(2,1)S(1)} %get-tuple-element.113), channel_id=1, source_target_pairs={{0,2},{1,3},{2,0},{3,1},{4,6},{5,7},{6,4},{7,5},{8,10},{9,11},{10,... | collective-permute-start | bytes 3145736 | tf_op jit(solution)/shard_map/ppermute | solution.py:446
  455.7 251.9 %reduce-scatter.6.cloned.1.call-start = ((), (), s32[]{:S(2)}) async-start(), calls=%async_computation.14 | async-start | bytes 10485760 | tf_op jit(solution)/shard_map/reduce_scatter | solution.py:623
  489.7 13.5 %collective-permute-start.49 = (bf16[1024,4096]{1,0:T(8,128)(2,1)}, bf16[1024,4096]{1,0:T(8,128)(2,1)}, u32[]{:S(2)}, u32[]{:S(2)}) collective-permute-start(bf16[1024,4096]{1,0:T(8,128)(2,1)} %convolution_convert_fusion.2.other), channel_id=1, source_target_pairs={{0,4},{4,0},{1,5},{5,1},{2,6},{6,2},{3,7},{7,3},{8,12},{12,8},{9,1... | collective-permute-start | bytes 25165832 | tf_op jit(solution)/shard_map/ppermute | solution.py:632
  536.7 14.8 %collective-permute-start.32 = (bf16[512,512]{1,0:T(8,128)(2,1)S(1)}, bf16[512,512]{1,0:T(8,128)(2,1)S(1)}, u32[]{:S(2)}, u32[]{:S(2)}) collective-permute-start(bf16[512,512]{1,0:T(8,128)(2,1)S(1)} %get-tuple-element.133), channel_id=1, source_target_pairs={{0,1},{1,0},{2,3},{3,2},{4,5},{5,4},{6,7},{7,6},{8,9},{9,8},{10,11... | collective-permute-start | bytes 1572872 | tf_op jit(solution)/shard_map/ppermute | solution.py:446
  536.7 25.6 %collective-permute-start.31 = (bf16[512,512]{1,0:T(8,128)(2,1)S(1)}, bf16[512,512]{1,0:T(8,128)(2,1)S(1)}, u32[]{:S(2)}, u32[]{:S(2)}) collective-permute-start(bf16[512,512]{1,0:T(8,128)(2,1)S(1)} %get-tuple-element.130), channel_id=1, source_target_pairs={{0,1},{1,0},{2,3},{3,2},{4,5},{5,4},{6,7},{7,6},{8,9},{9,8},{10,11... | collective-permute-start | bytes 1572872 | tf_op jit(solution)/shard_map/ppermute | solution.py:446
  538.8 23.6 %collective-permute-start.35 = (bf16[512,512]{1,0:T(8,128)(2,1)S(1)}, bf16[512,512]{1,0:T(8,128)(2,1)S(1)}, u32[]{:S(2)}, u32[]{:S(2)}) collective-permute-start(bf16[512,512]{1,0:T(8,128)(2,1)S(1)} %get-tuple-element.131), channel_id=1, source_target_pairs={{0,2},{1,3},{2,0},{3,1},{4,6},{5,7},{6,4},{7,5},{8,10},{9,11},{10,... | collective-permute-start | bytes 1572872 | tf_op jit(solution)/shard_map/ppermute | solution.py:446
  551.6 14.9 %collective-permute-start.33 = (bf16[512,512]{1,0:T(8,128)(2,1)S(1)}, bf16[512,512]{1,0:T(8,128)(2,1)S(1)}, u32[]{:S(2)}, u32[]{:S(2)}) collective-permute-start(bf16[512,512]{1,0:T(8,128)(2,1)S(1)} %add_convert_fusion.8), channel_id=1, source_target_pairs={{0,2},{1,3},{2,0},{3,1},{4,6},{5,7},{6,4},{7,5},{8,10},{9,11},{10,... | collective-permute-start | bytes 1572872 | tf_op jit(solution)/shard_map/ppermute | solution.py:446
  553.0 26.5 %collective-permute-start.34 = (bf16[512,512]{1,0:T(8,128)(2,1)S(1)}, bf16[512,512]{1,0:T(8,128)(2,1)}, u32[]{:S(2)}, u32[]{:S(2)}) collective-permute-start(bf16[512,512]{1,0:T(8,128)(2,1)S(1)} %get-tuple-element.132), channel_id=1, source_target_pairs={{0,2},{1,3},{2,0},{3,1},{4,6},{5,7},{6,4},{7,5},{8,10},{9,11},{10,... | collective-permute-start | bytes 1572872 | tf_op jit(solution)/shard_map/ppermute | solution.py:446
  568.1 15.2 %collective-permute-start.36 = (bf16[512,512]{1,0:T(8,128)(2,1)}, bf16[512,512]{1,0:T(8,128)(2,1)}, u32[]{:S(2)}, u32[]{:S(2)}) collective-permute-start(bf16[512,512]{1,0:T(8,128)(2,1)} %get-tuple-element.129), channel_id=1, source_target_pairs={{0,1},{1,0},{2,3},{3,2},{4,5},{5,4},{6,7},{7,6},{8,9},{9,8},{10,11... | collective-permute-start | bytes 1572872 | tf_op jit(solution)/shard_map/ppermute | solution.py:446
  569.2 21.3 %all-to-all-start.3 = ((bf16[4,256,512]{2,1,0:T(8,128)(2,1)}), bf16[4,256,512]{2,1,0:T(8,128)(2,1)}, u32[]{:S(2)}, u32[]{:S(2)}) async-start(bf16[4,256,512]{2,1,0:T(8,128)(2,1)} %bitcast.70), calls=%async_computation.3 | async-start | bytes 2097152 | tf_op jit(solution)/shard_map/all_to_all | solution.py:555
  573.5 227.0 %reduce-scatter.8.cloned.1.call-start = ((), (), s32[]{:S(2)}) async-start(), calls=%async_computation.15 | async-start | bytes 10027008 | tf_op jit(solution)/shard_map/reduce_scatter | solution.py:623
  608.3 14.9 %collective-permute-start.41 = (bf16[512,512]{1,0:T(8,128)(2,1)S(1)}, bf16[512,512]{1,0:T(8,128)(2,1)S(1)}, u32[]{:S(2)}, u32[]{:S(2)}) collective-permute-start(bf16[512,512]{1,0:T(8,128)(2,1)S(1)} %get-tuple-element.127), channel_id=1, source_target_pairs={{0,1},{1,0},{2,3},{3,2},{4,5},{5,4},{6,7},{7,6},{8,9},{9,8},{10,11... | collective-permute-start | bytes 1572872 | tf_op jit(solution)/shard_map/ppermute | solution.py:446
  609.5 19.3 %collective-permute-start.40 = (bf16[512,512]{1,0:T(8,128)(2,1)S(1)}, bf16[512,512]{1,0:T(8,128)(2,1)S(1)}, u32[]{:S(2)}, u32[]{:S(2)}) collective-permute-start(bf16[512,512]{1,0:T(8,128)(2,1)S(1)} %get-tuple-element.124), channel_id=1, source_target_pairs={{0,1},{1,0},{2,3},{3,2},{4,5},{5,4},{6,7},{7,6},{8,9},{9,8},{10,11... | collective-permute-start | bytes 1572872 | tf_op jit(solution)/shard_map/ppermute | solution.py:446
  610.4 18.4 %collective-permute-start.44 = (bf16[512,512]{1,0:T(8,128)(2,1)S(1)}, bf16[512,512]{1,0:T(8,128)(2,1)S(1)}, u32[]{:S(2)}, u32[]{:S(2)}) collective-permute-start(bf16[512,512]{1,0:T(8,128)(2,1)S(1)} %get-tuple-element.125), channel_id=1, source_target_pairs={{0,2},{1,3},{2,0},{3,1},{4,6},{5,7},{6,4},{7,5},{8,10},{9,11},{10,... | collective-permute-start | bytes 1572872 | tf_op jit(solution)/shard_map/ppermute | solution.py:446
  624.8 27.4 %collective-permute-start.43 = (bf16[512,512]{1,0:T(8,128)(2,1)S(1)}, bf16[512,512]{1,0:T(8,128)(2,1)}, u32[]{:S(2)}, u32[]{:S(2)}) collective-permute-start(bf16[512,512]{1,0:T(8,128)(2,1)S(1)} %get-tuple-element.126), channel_id=1, source_target_pairs={{0,2},{1,3},{2,0},{3,1},{4,6},{5,7},{6,4},{7,5},{8,10},{9,11},{10,... | collective-permute-start | bytes 1572872 | tf_op jit(solution)/shard_map/ppermute | solution.py:446
  638.0 14.3 %collective-permute-start.45 = (bf16[512,512]{1,0:T(8,128)(2,1)}, bf16[512,512]{1,0:T(8,128)(2,1)}, u32[]{:S(2)}, u32[]{:S(2)}) collective-permute-start(bf16[512,512]{1,0:T(8,128)(2,1)} %get-tuple-element.123), channel_id=1, source_target_pairs={{0,1},{1,0},{2,3},{3,2},{4,5},{5,4},{6,7},{7,6},{8,9},{9,8},{10,11... | collective-permute-start | bytes 1572872 | tf_op jit(solution)/shard_map/ppermute | solution.py:446
  674.0 14.8 %collective-permute-start.47 = (f32[2,1024]{0,1:T(8,128)S(1)}, f32[2,1024]{0,1:T(8,128)S(1)}, u32[]{:S(2)}, u32[]{:S(2)}) collective-permute-start(f32[2,1024]{0,1:T(8,128)S(1)} %slice_bitcast_fusion), channel_id=1, source_target_pairs={{0,2},{1,3},{2,0},{3,1},{4,6},{5,7},{6,4},{7,5},{8,10},{9,11},{10,... | collective-permute-start | bytes 24584 | tf_op jit(solution)/shard_map/ppermute | solution.py:446
  675.4 13.4 %collective-permute-start.48 = (f32[2,1024]{0,1:T(8,128)S(1)}, f32[2,1024]{0,1:T(8,128)S(1)}, u32[]{:S(2)}, u32[]{:S(2)}) collective-permute-start(f32[2,1024]{0,1:T(8,128)S(1)} %slice_bitcast_fusion), channel_id=1, source_target_pairs={{0,3},{1,2},{2,1},{3,0},{4,7},{5,6},{6,5},{7,4},{8,11},{9,10},{10,... | collective-permute-start | bytes 24584 | tf_op jit(solution)/shard_map/ppermute | solution.py:446
  707.6 21.7 %all-to-all-start.4 = ((bf16[4,64,2048]{2,1,0:T(8,128)(2,1)}), bf16[4,64,2048]{2,1,0:T(8,128)(2,1)S(1)}, u32[]{:S(2)}, u32[]{:S(2)}) async-start(bf16[4,64,2048]{2,1,0:T(8,128)(2,1)} %bitcast.23), calls=%async_computation.7 | async-start | bytes 2097152 | tf_op jit(solution)/shard_map/all_to_all | solution.py:626
  727.4 15.2 %collective-permute-start.51 = (bf16[256,1024]{1,0:T(8,128)(2,1)}, bf16[256,1024]{1,0:T(8,128)(2,1)}, u32[]{:S(2)}, u32[]{:S(2)}) collective-permute-start(bf16[256,1024]{1,0:T(8,128)(2,1)} %get-tuple-element.121), channel_id=1, source_target_pairs={{0,1},{1,0},{2,3},{3,2},{4,5},{5,4},{6,7},{7,6},{8,9},{9,8},{10,11... | collective-permute-start | bytes 1572872 | tf_op jit(solution)/shard_map/ppermute | solution.py:446
  729.3 54.1 %all-to-all-start.5 = ((bf16[4,64,4096]{2,1,0:T(8,128)(2,1)}), bf16[4,64,4096]{2,1,0:T(8,128)(2,1)}, u32[]{:S(2)}, u32[]{:S(2)}) async-start(bf16[4,64,4096]{2,1,0:T(8,128)(2,1)} %bitcast.66), calls=%async_computation.8 | async-start | bytes 4194304 | tf_op jit(solution)/shard_map/all_to_all | solution.py:626
  734.0 31.6 %collective-permute-start.50 = (bf16[256,1024]{1,0:T(8,128)(2,1)}, bf16[256,1024]{1,0:T(8,128)(2,1)S(1)}, u32[]{:S(2)}, u32[]{:S(2)}) collective-permute-start(bf16[256,1024]{1,0:T(8,128)(2,1)} %get-tuple-element.118), channel_id=1, source_target_pairs={{0,1},{1,0},{2,3},{3,2},{4,5},{5,4},{6,7},{7,6},{8,9},{9,8},{10,11... | collective-permute-start | bytes 1572872 | tf_op jit(solution)/shard_map/ppermute | solution.py:446
  735.9 29.9 %collective-permute-start.54 = (bf16[256,1024]{1,0:T(8,128)(2,1)}, bf16[256,1024]{1,0:T(8,128)(2,1)S(1)}, u32[]{:S(2)}, u32[]{:S(2)}) collective-permute-start(bf16[256,1024]{1,0:T(8,128)(2,1)} %get-tuple-element.119), channel_id=1, source_target_pairs={{0,2},{1,3},{2,0},{3,1},{4,6},{5,7},{6,4},{7,5},{8,10},{9,11},{10,... | collective-permute-start | bytes 1572872 | tf_op jit(solution)/shard_map/ppermute | solution.py:446
  744.0 30.2 %collective-permute-start.52 = (bf16[256,1024]{1,0:T(8,128)(2,1)S(1)}, bf16[256,1024]{1,0:T(8,128)(2,1)S(1)}, u32[]{:S(2)}, u32[]{:S(2)}) collective-permute-start(bf16[256,1024]{1,0:T(8,128)(2,1)S(1)} %add_convert_fusion.4), channel_id=1, source_target_pairs={{0,2},{1,3},{2,0},{3,1},{4,6},{5,7},{6,4},{7,5},{8,10},{9,11},{10,... | collective-permute-start | bytes 1572872 | tf_op jit(solution)/shard_map/ppermute | solution.py:446
  746.0 58.2 %collective-permute-start.53 = (bf16[256,1024]{1,0:T(8,128)(2,1)}, bf16[256,1024]{1,0:T(8,128)(2,1)}, u32[]{:S(2)}, u32[]{:S(2)}) collective-permute-start(bf16[256,1024]{1,0:T(8,128)(2,1)} %get-tuple-element.120), channel_id=1, source_target_pairs={{0,2},{1,3},{2,0},{3,1},{4,6},{5,7},{6,4},{7,5},{8,10},{9,11},{10,... | collective-permute-start | bytes 1572872 | tf_op jit(solution)/shard_map/ppermute | solution.py:446
  777.1 27.2 %collective-permute-start.55 = (bf16[256,1024]{1,0:T(8,128)(2,1)}, bf16[256,1024]{1,0:T(8,128)(2,1)}, u32[]{:S(2)}, u32[]{:S(2)}) collective-permute-start(bf16[256,1024]{1,0:T(8,128)(2,1)} %get-tuple-element.117), channel_id=1, source_target_pairs={{0,1},{1,0},{2,3},{3,2},{4,5},{5,4},{6,7},{7,6},{8,9},{9,8},{10,11... | collective-permute-start | bytes 1572872 | tf_op jit(solution)/shard_map/ppermute | solution.py:446
  800.5 15.1 %all-to-all-start.6 = ((bf16[4,64,2176]{2,1,0:T(8,128)(2,1)}), bf16[4,64,2176]{2,1,0:T(8,128)(2,1)S(1)}, u32[]{:S(2)}, u32[]{:S(2)}) async-start(bf16[4,64,2176]{2,1,0:T(8,128)(2,1)} %bitcast.64), calls=%async_computation.9 | async-start | bytes 2228224 | tf_op jit(solution)/shard_map/all_to_all | solution.py:626
  (79 other events, 872.6 us)
Sparse Core Ops, SparseCore 0:
  30.3 85.9 all-gather.3
  117.8 149.5 all-gather.5
  269.1 80.2 all-gather.7
  455.8 87.1 reduce-scatter.3
  545.3 142.8 reduce-scatter.5
  707.7 91.6 reduce-scatter.7

commit v3 on v2

--- a/solution.py
+++ b/solution.py
@@ -25,8 +25,8 @@
 neg_large = -1e30
 bf16 = jnp.bfloat16
 f32 = jnp.float32
-GAIN_COLS = 128
 TILE = 512
+ALL_VMEM = 60 * 1024 * 1024
 
 
 def mm(left, right, dims):
@@ -58,7 +58,7 @@
         start += ref.shape[1]
 
 
-def spread_kernel(weight, groups, count, extra, tile):
+def spread_kernel(weight, groups, count, tile):
     owned, columns = weight.shape
     size = columns // (groups * count)
     specs = [
@@ -66,10 +66,6 @@
     ]
     operands = [weight] * groups
     wide = groups * size
-    if extra is not None:
-        specs.append(pl.BlockSpec(extra.shape, lambda f: (0, 0)))
-        operands.append(extra)
-        wide += extra.shape[1]
     return pl.pallas_call(
         functools.partial(spread_body, tile),
         grid=(count,),
@@ -159,8 +155,8 @@
     query, key, value, attended, grad_att, lse = refs[:6]
     query_in, key_in, inverse, gain, cosine, sine, first = refs[6:13]
     query_grad, key_grad, value_grad, gain_grad, inner = refs[13:18]
-    grad_low, key_sum, value_sum = refs[18:]
-    grad_low[...] = grad_att[...].astype(bf16)
+    key_sum, value_sum = refs[18:]
+    grad_low = grad_att
     delta = jnp.sum(
         grad_low[...].astype(f32) * attended[...].astype(f32), axis=1, keepdims=True
     )
@@ -245,7 +241,6 @@
                 jax.ShapeDtypeStruct((length, HEAD_DIM), f32),
             ],
             scratch_shapes=[
-                pltpu.VMEM((length, HEAD_DIM), bf16),
                 pltpu.VMEM((length, HEAD_DIM), f32),
                 pltpu.VMEM((length, HEAD_DIM), f32),
             ],
@@ -282,27 +277,30 @@
         in_specs=[spec(part)] * 3 + [spec(2 * part), spec(2), spec(2)],
         out_specs=spec(3 * part),
         out_shape=jax.ShapeDtypeStruct((length, 3 * part), bf16),
-        compiler_params=pltpu.CompilerParams(vmem_limit_bytes=40 * 1024 * 1024),
+        compiler_params=pltpu.CompilerParams(vmem_limit_bytes=ALL_VMEM),
         cost_estimate=pl.CostEstimate(
             flops=8 * length * part, bytes_accessed=24 * length * part, transcendentals=0
         ),
     )(query_grad, key_grad, value_grad, qkv, inverse, inner)
 
 
-def attn_grad_body(token, grad_qkv, attended, grad_branch, gain, out):
-    wide, part = grad_qkv.shape[1], grad_branch.shape[1]
-    out[:, :wide] = dot(token[...], grad_qkv[...], 1, 0).astype(bf16)
-    out[:, wide : wide + part] = dot(attended[...], grad_branch[...], 1, 0).astype(bf16)
-    gains = jnp.concatenate(
-        [gain[...], jnp.zeros((GAIN_COLS - gain.shape[0], gain.shape[1]), f32)], axis=0
-    )
-    out[:, wide + part :] = jnp.transpose(gains).astype(bf16)
-
-
-def attn_grad(token, grad_qkv, attended, grad_branch, gain):
+def attn_grad_body(token, grad_qkv, attended, grad_branch, *rest):
+    out = rest[-1]
+    wide = grad_qkv.shape[1]
+    for low, high, left, right in (
+        (0, wide, token, grad_qkv),
+        (wide, out.shape[1], attended, grad_branch),
+    ):
+        value = dot(left[...], right[...], 1, 0)
+        if len(rest) > 1:
+            value = value + rest[0][:, low:high].astype(f32)
+        out[:, low:high] = value.astype(bf16)
+
+
+def attn_grad(token, grad_qkv, attended, grad_branch, *other):
     width, length = token.shape
     rows = math.gcd(width, 512)
-    columns = grad_qkv.shape[1] + grad_branch.shape[1] + GAIN_COLS
+    columns = grad_qkv.shape[1] + grad_branch.shape[1]
 
     def row_spec(wide):
         return pl.BlockSpec((rows, wide), lambda i: (i, 0))
@@ -313,13 +311,8 @@
     return pl.pallas_call(
         attn_grad_body,
         grid=(width // rows,),
-        in_specs=[
-            row_spec(length),
-            whole(grad_qkv),
-            row_spec(length),
-            whole(grad_branch),
-            pl.BlockSpec((gain.shape[0], rows), lambda i: (0, i)),
-        ],
+        in_specs=[row_spec(length), whole(grad_qkv), row_spec(length), whole(grad_branch)]
+        + [row_spec(columns)] * len(other),
         out_specs=row_spec(columns),
         out_shape=jax.ShapeDtypeStruct((width, columns), bf16),
         compiler_params=pltpu.CompilerParams(vmem_limit_bytes=48 * 1024 * 1024),
@@ -328,7 +321,7 @@
             bytes_accessed=6 * width * length,
             transcendentals=0,
         ),
-    )(token, grad_qkv, attended, grad_branch, gain)
+    )(token, grad_qkv, attended, grad_branch, *other)
 
 
 def token_grad_body(place, grad_qkv, weight, grad_hidden, out):
@@ -359,6 +352,35 @@
     )(place, grad_qkv, weight, grad_hidden)
 
 
+def half_grad_body(left, right, *rest):
+    value = dot(left[...], right[...], 1, 0)
+    if len(rest) > 1:
+        value = value + rest[0][...].astype(f32)
+    rest[-1][...] = value.astype(bf16)
+
+
+def half_grad(left, right, *other):
+    rows, length = left.shape
+    columns = right.shape[1]
+    size = math.gcd(columns, 512)
+    spec = pl.BlockSpec((rows, size), lambda j: (0, j))
+    return pl.pallas_call(
+        half_grad_body,
+        grid=(columns // size,),
+        in_specs=[
+            pl.BlockSpec((rows, length), lambda j: (0, 0)),
+            pl.BlockSpec((length, size), lambda j: (0, j)),
+        ]
+        + [spec] * len(other),
+        out_specs=spec,
+        out_shape=jax.ShapeDtypeStruct((rows, columns), bf16),
+        compiler_params=pltpu.CompilerParams(vmem_limit_bytes=48 * 1024 * 1024),
+        cost_estimate=pl.CostEstimate(
+            flops=2 * rows * length * columns, bytes_accessed=4 * rows * columns, transcendentals=0
+        ),
+    )(left, right, *other)
+
+
 def gate_up_body(hidden, weight, both, activ):
     value = dot(hidden[...], weight[...], 1, 0)
     gate, up = value[:, :TILE], value[:, TILE:]
@@ -407,7 +429,7 @@
             in_specs=[rows_spec, columns(width, TILE), columns(length, 2 * TILE)],
             out_specs=columns(length, 2 * TILE),
             out_shape=jax.ShapeDtypeStruct((length, 2 * wide), bf16),
-            compiler_params=params,
+            compiler_params=pltpu.CompilerParams(vmem_limit_bytes=ALL_VMEM),
             cost_estimate=pl.CostEstimate(
                 flops=2 * length * width * wide,
                 bytes_accessed=12 * length * wide + 2 * width * wide,
@@ -434,6 +456,39 @@
         out_shape=jax.ShapeDtypeStruct(values.shape, values.dtype),
         input_output_aliases={0: 0},
     )(values, other)
+
+
+def zero_after(other):
+    first = other[(slice(0, 1),) * other.ndim].astype(f32).reshape(())
+    return jnp.minimum(jnp.abs(first), 0.0).astype(jnp.int32)
+
+
+class Copies:
+    def __init__(self):
+        self.count = lax.axis_size("z")
+
+    def swap(self, values):
+        return lax.ppermute(values, "core", [(0, 1), (1, 0)])
+
+    def along(self, values):
+        return [values] + [
+            lax.ppermute(values, "z", [(i, (i + step) % self.count) for i in range(self.count)])
+            for step in range(1, self.count)
+        ]
+
+    def gather(self, values):
+        core, place = lax.axis_index("core"), lax.axis_index("z")
+        other = self.swap(values)
+        both = jnp.concatenate(
+            [lax.select_n(core, values, other), lax.select_n(core, other, values)]
+        )
+        parts = self.along(both)
+        return jnp.concatenate(
+            [lax.select_n((place - z) % self.count, *parts) for z in range(self.count)]
+        )
+
+    def total(self, values):
+        return sum(self.along(values + self.swap(values)))
 
 
 class Plane:
@@ -463,7 +518,7 @@
             out = lax.dynamic_update_slice(out, part, start)
         return out
 
-    def scatter(self, partial, axis):
+    def scatter(self, partial, axis, kind=f32, last=(0, 0)):
         if not self.square:
             total = lax.psum_scatter(partial, FSDP, scatter_dimension=axis, tiled=True)
             return total.astype(f32)
@@ -471,9 +526,9 @@
         size, cut = partial.shape[axis] // 4, partial.shape[other] // 2
         place = self.place
 
-        def piece(bit, offset):
+        def piece(bit, offset, zero=0):
             start = [0, 0]
-            start[axis] = (place ^ bit) * size
+            start[axis] = (place ^ bit) * size + zero
             start[other] = offset
             extent = [0, 0]
             extent[axis] = size
@@ -481,14 +536,14 @@
             return lax.dynamic_slice(partial, start, extent)
 
         halves = []
-        for offset, first, second in ((0, 1, 2), (cut, 2, 1)):
+        for (offset, first, second), zero in zip(((0, 1, 2), (cut, 2, 1)), last):
             relay = self.swap(piece(3, offset), first)
             mine = self.swap(piece(first, offset), first)
             relay = (piece(second, offset).astype(f32) + relay.astype(f32)).astype(bf16)
             halves.append(
-                piece(0, offset).astype(f32) + mine.astype(f32) + self.swap(relay, second).astype(f32)
+                piece(0, offset, zero).astype(f32) + mine.astype(f32) + self.swap(relay, second).astype(f32)
             )
-        return jnp.concatenate(halves, axis=other)
+        return jnp.concatenate([half.astype(kind) for half in halves], axis=other)
 
     def total(self, values):
         if not self.square:
@@ -537,17 +592,19 @@
     wide = hidden // count
     scale = 1.0 / math.sqrt(HEAD_DIM)
 
-    def spread(weight, groups, extra=None, tile=0):
-        block = spread_kernel(weight, groups, count, extra, tile)
+    def spread(weight, groups, tile=0):
+        block = spread_kernel(weight, groups, count, tile)
         return lax.all_to_all(block, FSDP, 0, 0, tiled=True)
 
-    gain_block = jnp.pad(gains, ((0, 0), (0, GAIN_COLS - gains.shape[1])))
-    attn_all = lax.all_gather(spread(w_attn, 4, gain_block), DP, axis=0, tiled=True)
+    attn_all = lax.all_gather(spread(w_attn, 4), DP, axis=0, tiled=True)
     gate_up_all = lax.all_gather(spread(w_gate_up, 2, tile=TILE), DP, axis=0, tiled=True)
     down_all = lax.all_gather(spread(w_down, 1), DP, axis=0, tiled=True)
     qkv_weight = attn_all[:, : 3 * part]
     out_weight = attn_all[:, 3 * part : 4 * part]
-    gain_values = attn_all[:, 4 * part : 4 * part + 4].astype(f32)
+    copies = Copies()
+    gain_low = lax.reduce_precision(gains, exponent_bits=8, mantissa_bits=7)
+    gain_values = copies.gather(plane.gather_small(jnp.transpose(gain_low).reshape(-1)))
+    gain_values = jnp.transpose(gain_values.reshape(-1, 4, owned), (0, 2, 1)).reshape(width, 4)
     gain_part = lax.dynamic_slice_in_dim(gain_values, place * part, part, 0)
 
     token_full = plane.gather(tokens, 0)
@@ -575,9 +632,9 @@
     qkv = mm(token_full, qkv_weight, ((1,), (0,)))
     query_raw, key_raw = qkv[:, :part], qkv[:, part : 2 * part]
     squares = plane.total(
-        jnp.stack([jnp.sum(query_raw * query_raw, axis=1), jnp.sum(key_raw * key_raw, axis=1)])
-    )
-    inverse = jnp.transpose(lax.rsqrt(squares / width + norm_eps))
+        jnp.concatenate([jnp.sum(query_raw * query_raw, axis=1), jnp.sum(key_raw * key_raw, axis=1)])
+    )
+    inverse = jnp.transpose(lax.rsqrt(squares / width + norm_eps).reshape(2, length))
     tables = (inverse, gain_rows, cosine, sine, first_key)
     query, key, value, attended_low, lse = attend(qkv, *tables)
     attended_full = plane.gather(attended_low, 1)
@@ -589,20 +646,27 @@
     hidden_low = (token_part + branch_hat * gain_part[None, :, 2]).astype(bf16)
     hidden_full = plane.gather(hidden_low, 1)
 
-    copies, core = lax.axis_size("z"), lax.axis_index("core")
-    share = width // (2 * copies)
-
-    def side(index):
-        return jnp.concatenate(
-            [
-                lax.dynamic_slice_in_dim(hidden_full, (2 * z + index) * share, share, 1)
-                for z in range(copies)
-            ],
-            axis=1,
-        )
-
-    other_side, own_side = side(1 - core), side(core)
-    hidden_full = order(order(hidden_full, other_side), own_side)
+    core = lax.axis_index("core")
+    share = width // (2 * copies.count)
+
+    def sides(array):
+        return [
+            jnp.transpose(
+                jnp.concatenate(
+                    [
+                        lax.dynamic_slice_in_dim(array, (2 * z + index) * share, share, 1)
+                        for z in range(copies.count)
+                    ],
+                    axis=1,
+                )
+            )
+            for index in (1 - core, core)
+        ]
+
+    other_side, own_side = sides(hidden_full)
+    token_turned, attended_turned = jnp.transpose(token_full), jnp.transpose(attended_full)
+    for early in (other_side, own_side, token_turned, attended_turned, cot_part):
+        hidden_full = order(hidden_full, early)
     gate_up, gate_up_back = gate_up_kernels(length, width, wide)
     both, activ = gate_up(hidden_full, gate_up_all)
     mlp = plane.scatter(mm(activ, down_all, ((1,), (1,))).astype(bf16), 0)
@@ -619,65 +683,63 @@
         plane.gather(grad_mlp.astype(bf16), 0), Layout(major_to_minor=(0, 1))
     )
 
-    def reduced(partial, axes, wait=()):
-        mine = lax.psum_scatter(partial, axes, scatter_dimension=0, tiled=True)
+    def exchanged(mine, *wait):
         for other in wait:
             mine = order(mine, other)
-        return mine, lax.all_to_all(mine, FSDP, 0, 0, tiled=True)
-
-    down_mine, down_part = reduced(mm(grad_mlp_full, activ, ((0,), (0,))).astype(bf16), DP)
+        return lax.all_to_all(mine, FSDP, 0, 0, tiled=True)
+
+    down_partial = mm(grad_mlp_full, activ, ((0,), (0,))).astype(bf16)
+    down_mine = lax.psum_scatter(down_partial, DP, scatter_dimension=0, tiled=True)
     grad_gate_up_low = gate_up_back(grad_mlp_full, down_all, both)
 
-    send = mm(other_side, grad_gate_up_low, ((0,), (0,))).astype(bf16)
-    got = lax.ppermute(send, "core", [(0, 1), (1, 0)])
+    send = half_grad(other_side, grad_gate_up_low)
+    got = copies.swap(send)
     late = order(grad_gate_up_low, send)
-    keep = mm(own_side, late, ((0,), (0,))).astype(bf16)
-    late = order(late, keep)
-    grad_hidden = cot_part + plane.scatter(
-        mm(late, gate_up_all, ((1,), (1,))).astype(bf16), 1
-    )
-    gate_up_partial = (keep.astype(f32) + got.astype(f32)).astype(bf16)
-    gate_up_mine, gate_up_part = reduced(gate_up_partial, "z")
+    hidden_partial = mm(late, gate_up_all, ((1,), (1,))).astype(bf16)
+    grad_hidden = cot_part + plane.scatter(hidden_partial, 1)
+    gate_up_partial = half_grad(order(own_side, hidden_partial), late, got)
+    gate_up_mine = lax.psum_scatter(gate_up_partial, "z", scatter_dimension=0, tiled=True)
 
     scaled = grad_hidden * gain_part[None, :, 2]
     grad_gain_attn = jnp.sum(grad_hidden * branch_hat, axis=0)
     inner = plane.total(jnp.sum(scaled * branch_hat, axis=1))[:, None] / width
     grad_branch = (branch_inv * (scaled - branch_hat * inner)).astype(bf16)
     grad_branch = order(grad_branch, down_mine)
-    grad_att = plane.scatter(mm(grad_branch, out_weight, ((1,), (1,))).astype(bf16), 1)
+    grad_att = plane.scatter(
+        mm(grad_branch, out_weight, ((1,), (1,))).astype(bf16), 1, bf16
+    )
     query_grad, key_grad, value_grad, gain_grad, inner = attend_back(
         query, key, value, attended_low, grad_att, lse, qkv, *tables
     )
-    inner = jnp.transpose(plane.total(jnp.transpose(inner[:, :2])) / width)
+    inner = plane.total(jnp.concatenate([inner[:, 0], inner[:, 1]])) / width
+    inner = jnp.transpose(inner.reshape(2, length))
     grad_qkv_low = qkv_back(query_grad, key_grad, value_grad, qkv, inverse, inner)
 
-    own_gains = jnp.concatenate([gain_grad[:2], grad_gain_attn[None], jnp.zeros((5, part), f32)])
-    gain_rows = jnp.pad(grad_gain_mlp[None], ((3, 4), (0, 0)))
-    gain_rows = lax.dynamic_update_slice(
-        gain_rows,
-        own_gains + lax.dynamic_slice_in_dim(gain_rows, place * part, part, 1),
-        (0, place * part),
-    )
-    lefts = (jnp.transpose(token_full), grad_qkv_low, jnp.transpose(attended_full), grad_branch)
-    attn_partial = attn_grad(*lefts, gain_rows)
-    attn_partial = order(attn_partial, gate_up_mine)
-    back = token_grad(
-        jnp.full((1,), place), order(grad_qkv_low, attn_partial), attn_all, grad_hidden
+    own_gains = jnp.stack([gain_grad[0], gain_grad[1], grad_gain_attn])
+    gain_sums = jnp.concatenate([jnp.zeros((3, width), f32), grad_gain_mlp[None]])
+    gain_sums = lax.dynamic_update_slice(gain_sums, own_gains, (0, place * part)).reshape(-1)
+    gain_sums = plane.total(copies.total(gain_sums)).reshape(4, width)
+    owner = lax.axis_index(DP + FSDP)
+    grad_gains = jnp.transpose(lax.dynamic_slice_in_dim(gain_sums, owner * owned, owned, 1))
+    attn_partial = attn_grad(token_turned, grad_qkv_low, attended_turned, grad_branch)
+    late = order(grad_qkv_low, attn_partial)
+    back = token_grad(jnp.full((1,), place), late, attn_all, grad_hidden)
+    attn_partial = order(order(attn_partial, back), gate_up_mine)
+    attn_mine = lax.psum_scatter(attn_partial, DP, scatter_dimension=0, tiled=True)
+    gate_up_part = exchanged(gate_up_mine, attn_partial)
+    grad_tokens = plane.scatter(
+        back, 0, last=(zero_after(gate_up_part), zero_after(grad_gains))
     )
     grad_down, new_down, new_m_down, new_v_down = adamw_kernel(
-        down_part, w_down, m_down, v_down, 1, count
-    )
+        exchanged(down_mine, attn_partial), w_down, m_down, v_down, 1, count
+    )
+    attn_mine = order(order(attn_mine, grad_tokens), new_down)
+    attn_part = exchanged(attn_mine)
     grad_gate_up, new_gate_up, new_m_gate_up, new_v_gate_up = adamw_kernel(
-        gate_up_part, w_gate_up, m_gate_up, v_gate_up, 2, count, TILE
-    )
-    _, attn_part = reduced(attn_partial, DP, (new_down, new_gate_up))
-    grad_gains = jnp.sum(
-        attn_part[:, 4 * part : 4 * part + 4].reshape(count, owned, 4).astype(f32), axis=0
-    )
-
-    grad_tokens = plane.scatter(back, 0)
+        order(gate_up_part, attn_mine), w_gate_up, m_gate_up, v_gate_up, 2, count, TILE
+    )
     grad_attn, new_attn, new_m_attn, new_v_attn = adamw_kernel(
-        attn_part, w_attn, m_attn, v_attn, 4, count
+        order(attn_part, new_gate_up), w_attn, m_attn, v_attn, 4, count
     )
     new_gains, new_m_gains, new_v_gains = adamw_step(
         gains, grad_gains, m_gains, v_gains, 0.0, gain_rate

time: 841 us -> 829 us (0.986)
  Pallas kernels: 129 us -> 159 us
  matrix products: 95.8 us -> 69.4 us
  other arithmetic: 49.9 us -> 28.1 us
  waiting for transfers between devices: 311 us -> 296 us
  starting transfers between devices: 78.7 us -> 92.9 us
    pallas_call x0 -> x2, Pallas kernels: none -> 28.7 us  [half_grad(): pl.pallas_call(half_grad_body, grid=(columns // size,), in_specs=[pl.Bloc...]
    dot_general x8 -> x6, matrix products: 95.8 us -> 69.4 us  [mm(): lax.dot_general(left, right, (dims, ((), ())), preferred_element_type=f32)]
    ppermute x1 -> x9, starting transfers between devices: 0.01 us -> 10.1 us  [the longest x6 10 us: along(): lax.ppermute(values, 'z', [(i, (i + step) % self.count) for i in range(se...]
    all_gather x1, waiting for transfers between devices: 37.2 us -> 28.2 us  [per_device(): down_all = lax.all_gather(spread(w_down, 1), DP, axis=0, tiled=True)]
    ppermute x55 -> x61, starting transfers between devices: 62.4 us -> 67.9 us  [swap(): return lax.ppermute(values, FSDP, [(i, i ^ bit) for i in range(self.count)])]
    ppermute x55 -> x61, waiting for transfers between devices: 257 us -> 252 us  [swap(): return lax.ppermute(values, FSDP, [(i, i ^ bit) for i in range(self.count)])]
    unnamed x125 -> x127, local copies, waits for them, and re-layouts: 37.4 us -> 36.7 us
  transfers between devices with their start and end apart: 66 -> 80, of which waited for: 42 -> 48; matrix products, arithmetic and copies ran while one was open for 20% -> 16% of each run, Pallas kernels for 14% -> 18%
where the time goes in v3:
time: 829 us; the launch traced here: 822 us
  waiting for transfers between devices  296 us (36%)
  Pallas kernels  159 us (19%)
  local copies, waits for them, and re-layouts  98.1 us (12%)
  starting transfers between devices  92.9 us (11%)
  matrix products  69.4 us (8%)
  blocking collectives  61.6 us (7%)
  other arithmetic  28.1 us (3%)
  between operations  16.8 us (2%)
    ppermute x61, waiting for transfers between devices, swap(): return lax.ppermute(values, FSDP, [(i, i ^ bit) for i in range(self.count)])  252 us
    dot_general x6, matrix products, mm(): lax.dot_general(left, right, (dims, ((), ())), preferred_element_type=f32)  69.4 us
    ppermute x61, starting transfers between devices, swap(): return lax.ppermute(values, FSDP, [(i, i ^ bit) for i in range(self.count)])  67.9 us
    all_to_all x3, blocking collectives, spread(): return lax.all_to_all(block, FSDP, 0, 0, tiled=True)  61.6 us
    unnamed x127, local copies, waits for them, and re-layouts  36.7 us
    pallas_call x2, Pallas kernels, half_grad(): pl.pallas_call(half_grad_body, grid=(columns // size,), in_specs=[pl.Bloc...  28.7 us
    all_gather x1, waiting for transfers between devices, per_device(): down_all = lax.all_gather(spread(w_down, 1), DP, axis=0, tiled=True)  28.2 us
    pallas_call x1, Pallas kernels, forward(): pl.pallas_call(gate_up_body, grid=(wide // TILE,), in_specs=[rows_spec, c...  24.8 us
  transfers between devices with their start and end apart: 80, of which 48 were waited for; matrix products, arithmetic and copies ran while one was open for 16% of the time, Pallas kernels for 18%

profile of v3, /device:TPU:0, one launch (start us, length us, event | category | flops | bytes accessed | tf_op | source)
XLA Modules:
  0.0 822.5 jit_solution(12722930082324314973)
XLA Ops:
  9.2 19.2 %all_to_all.75 = bf16[4,64,2048]{2,1,0:T(8,128)(2,1)} all-to-all(bf16[4,64,2048]{2,1,0:T(8,128)(2,1)S(1)} %bitcast.76), channel_id=1, replica_groups=mesh['z'=4,'core'=2,'y'=2,'x'=2] {'y','x'}, dimensions={0} | all-to-all | bytes 2097152 | tf_op jit(solution)/shard_map/all_to_all | solution.py:597
  31.3 27.5 %all_to_all.76 = bf16[4,64,4096]{2,1,0:T(8,128)(2,1)} all-to-all(bf16[4,64,4096]{2,1,0:T(8,128)(2,1)S(1)} %bitcast.74), channel_id=1, replica_groups=mesh['z'=4,'core'=2,'y'=2,'x'=2] {'y','x'}, dimensions={0} | all-to-all | bytes 4194304 | tf_op jit(solution)/shard_map/all_to_all | solution.py:597
  59.2 14.9 %all_to_all.77 = bf16[4,64,2048]{2,1,0:T(8,128)(2,1)} all-to-all(bf16[4,64,2048]{2,1,0:T(8,128)(2,1)S(1)} %bitcast.77), channel_id=1, replica_groups=mesh['z'=4,'core'=2,'y'=2,'x'=2] {'y','x'}, dimensions={0} | all-to-all | bytes 2097152 | tf_op jit(solution)/shard_map/all_to_all | solution.py:597
  86.4 12.7 %collective-permute-done.15 = s32[256]{0:T(256)S(1)} collective-permute-done((s32[256]{0:T(256)S(1)}, s32[256]{0:T(256)S(1)}, u32[]{:S(2)}, u32[]{:S(2)}) %collective-permute-start.15) | collective-permute-done | bytes 1056 | tf_op jit(solution)/shard_map/ppermute | solution.py:501
  117.8 6.3 collective-permute-done.2
  126.9 10.0 %fusion.refs_0_.refs_1_.refs_2_.refs_6_.refs_7_.raw = f32[1024,1536]{1,0:T(8,128)S(1)} fusion(bf16[1024,2048]{1,0:T(8,128)(2,1)} %constant_dynamic-update-slice_fusion.19, bf16[2048,2048]{1,0:T(8,128)(2,1)} %all-gather.4.cloned.1.call-done.weight), kind=kOutput, calls=%fused_computation.1 | convolution fusion | flops 6442450944 | bytes 16777216 | tf_op jit(solution)/shard_map/dot_general | solution.py:33
  144.0 17.7 %shard_map.287 = (bf16[1024,512]{1,0:T(8,128)(2,1)S(1)}, bf16[1024,512]{1,0:T(8,128)(2,1)S(1)}, bf16[1024,512]{1,0:T(8,128)(2,1)S(1)}, bf16[1024,512]{1,0:T(8,128)(2,1)}, f32[4,1024,1]{2,1,0:T(8,128)}) custom-call(f32[1024,1536]{1,0:T(8,128)} %copy-done.37, f32[1024,1536]{1,0:T(8,128)} %copy-done.37, f32[1024,1536]{1,0:T(8,128)} %copy-done.37, ...), custom_call_target="tpu_custom_call" | custom-call | flops 2147483648 | bytes 10485760 | tf_op jit(solution)/shard_map/pallas_call | solution.py:218
  166.4 20.3 %collective-permute-done.17 = bf16[1024,512]{1,0:T(8,128)(2,1)S(1)} collective-permute-done((bf16[1024,512]{1,0:T(8,128)(2,1)}, bf16[1024,512]{1,0:T(8,128)(2,1)S(1)}, u32[]{:S(2)}, u32[]{:S(2)}) %collective-permute-start.17) | collective-permute-done | bytes 1048608 | tf_op jit(solution)/shard_map/ppermute | solution.py:501
  193.8 5.0 collective-permute-done.19
  200.0 6.9 multiply_reduce_fusion.3
  225.5 19.3 %collective-permute-done.24 = bf16[1024,512]{1,0:T(8,128)(2,1)S(1)} collective-permute-done((bf16[1024,512]{1,0:T(8,128)(2,1)}, bf16[1024,512]{1,0:T(8,128)(2,1)S(1)}, u32[]{:S(2)}, u32[]{:S(2)}) %collective-permute-start.24) | collective-permute-done | bytes 1048608 | tf_op jit(solution)/shard_map/ppermute | solution.py:501
  246.5 4.8 collective-permute-done.25
  258.7 6.4 copy.126.other.token
  265.1 6.5 copy.127.other.attended
  289.1 24.8 %shard_map.294 = (f32[1024,4096]{1,0:T(8,128)}, bf16[1024,2048]{1,0:T(8,128)(2,1)S(1)}) custom-call(bf16[1024,2048]{1,0:T(8,128)(2,1)} %shard_map.292.hidden, bf16[2048,4096]{1,0:T(8,128)(2,1)} %all-gather.6.cloned.1.call-done.weight), custom_call_target="tpu_custom_call" | custom-call | flops 17179869184 | bytes 37748736 | tf_op jit(solution)/shard_map/pallas_call | solution.py:408
  315.9 28.2 %all-gather.8.cloned.1.call-done.weight = bf16[2048,2048]{1,0:T(8,128)(2,1)} async-done(((bf16[256,2048]{1,0:T(8,128)(2,1)}), bf16[2048,2048]{1,0:T(8,128)(2,1)}) %all-gather.8.cloned.1.call-update) | async-done | bytes 8388624 | tf_op jit(solution)/shard_map/all_gather | solution.py:601
  344.1 13.0 %convolution_convert_fusion.3 = bf16[1024,2048]{1,0:T(8,128)(2,1)S(1)} fusion(bf16[1024,2048]{1,0:T(8,128)(2,1)} %copy-done.35, bf16[2048,2048]{1,0:T(8,128)(2,1)} %all-gather.8.cloned.1.call-done.weight), kind=kOutput, calls=%fused_computation.5 | convolution fusion | flops 8592031744 | bytes 16777216 | tf_op jit(solution)/shard_map/dot_general | solution.py:33
  361.0 11.2 %collective-permute-done.29 = bf16[256,1024]{1,0:T(8,128)(2,1)S(1)} collective-permute-done((bf16[256,1024]{1,0:T(8,128)(2,1)S(1)}, bf16[256,1024]{1,0:T(8,128)(2,1)S(1)}, u32[]{:S(2)}, u32[]{:S(2)}) %collective-permute-start.29) | collective-permute-done | bytes 524320 | tf_op jit(solution)/shard_map/ppermute | solution.py:501
  374.5 8.3 %collective-permute-done.28 = bf16[256,1024]{1,0:T(8,128)(2,1)S(1)} collective-permute-done((bf16[256,1024]{1,0:T(8,128)(2,1)S(1)}, bf16[256,1024]{1,0:T(8,128)(2,1)S(1)}, u32[]{:S(2)}, u32[]{:S(2)}) %collective-permute-start.28) | collective-permute-done | bytes 524320 | tf_op jit(solution)/shard_map/ppermute | solution.py:501
  382.7 4.6 collective-permute-done.30
  389.4 6.9 collective-permute-done.31
  405.5 18.9 %collective-permute-done.34 = bf16[256,2048]{1,0:T(8,128)(2,1)S(1)} collective-permute-done((bf16[256,2048]{1,0:T(8,128)(2,1)S(1)}, bf16[256,2048]{1,0:T(8,128)(2,1)S(1)}, u32[]{:S(2)}, u32[]{:S(2)}) %collective-permute-start.34) | collective-permute-done | bytes 1048608 | tf_op jit(solution)/shard_map/ppermute | solution.py:501
  428.8 8.1 collective-permute-done.36
  439.5 11.4 %convolution_convert_fusion = bf16[2048,2048]{1,0:T(8,128)(2,1)} fusion(bf16[1024,2048]{1,0:T(8,128)(2,1)S(1)} %constant_dynamic-update-slice_fusion.18.grad_mlp, bf16[1024,2048]{1,0:T(8,128)(2,1)S(1)} %copy-done.36), kind=kOutput, calls=%fused_computation | convolution fusion | flops 8594128896 | bytes 16777216 | tf_op jit(solution)/shard_map/dot_general | solution.py:33
  451.0 18.4 %shard_map.296.right.values = bf16[1024,4096]{1,0:T(8,128)(2,1)} custom-call(bf16[1024,2048]{1,0:T(8,128)(2,1)} %copy-done.40, bf16[2048,2048]{1,0:T(8,128)(2,1)} %all-gather.8.cloned.1.call-done.weight, f32[1024,4096]{1,0:T(8,128)} %get-tuple-element.47.both), custom_call_target="tpu_custom_call" | custom-call | flops 8589934592 | bytes 33554432 | tf_op jit(solution)/shard_map/pallas_call | solution.py:426
  469.4 13.6 %shard_map.297.other = bf16[1024,4096]{1,0:T(8,128)(2,1)} custom-call(bf16[1024,1024]{1,0:T(8,128)(2,1)S(1)} %copy-done.14, bf16[1024,4096]{1,0:T(8,128)(2,1)} %shard_map.296.right.values), custom_call_target="tpu_custom_call" | custom-call | flops 8589934592 | bytes 16777216 | tf_op jit(solution)/shard_map/pallas_call | solution.py:367
  483.0 23.9 %convolution_convert_fusion.1.other = bf16[1024,2048]{1,0:T(8,128)(2,1)} fusion(bf16[1024,4096]{1,0:T(8,128)(2,1)} %shard_map.298.right, bf16[2048,4096]{1,0:T(8,128)(2,1)} %all-gather.6.cloned.1.call-done.weight), kind=kOutput, calls=%fused_computation.3 | convolution fusion | flops 17181966336 | bytes 29360128 | tf_op jit(solution)/shard_map/dot_general | solution.py:33
  508.5 15.1 %shard_map.306 = bf16[1024,4096]{1,0:T(8,128)(2,1)} custom-call(bf16[1024,1024]{1,0:T(8,128)(2,1)S(1)} %copy-done.6, bf16[1024,4096]{1,0:T(8,128)(2,1)} %shard_map.298.right, bf16[1024,4096]{1,0:T(8,128)(2,1)} %collective-permute-done.56.rest_0_), custom_call_target="tpu_custom_call" | custom-call | flops 8589934592 | bytes 16777216 | tf_op jit(solution)/shard_map/pallas_call | solution.py:367
  529.2 11.2 %collective-permute-done.39 = bf16[512,512]{1,0:T(8,128)(2,1)S(1)} collective-permute-done((bf16[512,512]{1,0:T(8,128)(2,1)S(1)}, bf16[512,512]{1,0:T(8,128)(2,1)S(1)}, u32[]{:S(2)}, u32[]{:S(2)}) %collective-permute-start.39) | collective-permute-done | bytes 524320 | tf_op jit(solution)/shard_map/ppermute | solution.py:501
  542.7 8.5 %collective-permute-done.38 = bf16[512,512]{1,0:T(8,128)(2,1)S(1)} collective-permute-done((bf16[512,512]{1,0:T(8,128)(2,1)S(1)}, bf16[512,512]{1,0:T(8,128)(2,1)S(1)}, u32[]{:S(2)}, u32[]{:S(2)}) %collective-permute-start.38) | collective-permute-done | bytes 524320 | tf_op jit(solution)/shard_map/ppermute | solution.py:501
  551.2 4.3 collective-permute-done.40
  556.1 8.8 %collective-permute-done.41 = bf16[512,512]{1,0:T(8,128)(2,1)S(1)} collective-permute-done((bf16[512,512]{1,0:T(8,128)(2,1)S(1)}, bf16[512,512]{1,0:T(8,128)(2,1)S(1)}, u32[]{:S(2)}, u32[]{:S(2)}) %collective-permute-start.41) | collective-permute-done | bytes 524320 | tf_op jit(solution)/shard_map/ppermute | solution.py:501
  575.0 4.3 convolution_convert_fusion.2
  583.2 11.3 %collective-permute-done.48 = bf16[512,512]{1,0:T(8,128)(2,1)S(1)} collective-permute-done((bf16[512,512]{1,0:T(8,128)(2,1)S(1)}, bf16[512,512]{1,0:T(8,128)(2,1)S(1)}, u32[]{:S(2)}, u32[]{:S(2)}) %collective-permute-start.48) | collective-permute-done | bytes 524320 | tf_op jit(solution)/shard_map/ppermute | solution.py:501
  600.7 7.0 collective-permute-done.49
  609.3 4.0 collective-permute-done.50
  613.3 4.1 collective-permute-done.52
  618.7 16.4 %shard_map.300 = (f32[1024,512]{1,0:T(8,128)}, f32[1024,512]{1,0:T(8,128)}, bf16[1024,512]{1,0:T(8,128)(2,1)S(1)}, f32[8,512]{1,0:T(8,128)S(1)}, f32[1024,128]{1,0:T(8,128)S(1)}) custom-call(bf16[1024,512]{1,0:T(8,128)(2,1)S(1)} %copy-done.28, bf16[1024,512]{1,0:T(8,128)(2,1)S(1)} %copy-done.30, bf16[1024,512]{1,0:T(8,128)(2,1)} %copy-done.31, ...), custom_call_target="tpu_custom_call" | custom-call | flops 5368709120 | bytes 15728640 | tf_op jit(solution)/shard_map/pallas_call | solution.py:231
  643.4 6.4 shard_map.301.grad_qkv.values
  651.6 12.3 %shard_map.302.other.values = bf16[2048,2048]{1,0:T(8,128)(2,1)} custom-call(bf16[2048,1024]{1,0:T(8,128)(2,1)} %copy.126.other.token, bf16[1024,1536]{1,0:T(8,128)(2,1)S(1)} %copy-done.7, bf16[2048,1024]{1,0:T(8,128)(2,1)} %copy.127.other.attended, bf16[1024,512]{1,0:T(8,128)(2,1)S(1)} %copy-done.22), custom_call_target="tpu_custom_call" | custom-call | flops 8589934592 | bytes 12582912 | tf_op jit(solution)/shard_map/pallas_call | solution.py:311
  665.8 9.8 %shard_map.304.other = bf16[1024,2048]{1,0:T(8,128)(2,1)} custom-call(s32[1]{0:T(128)} %bitcast.22.place, bf16[1024,1536]{1,0:T(8,128)(2,1)S(1)} %copy-done.8, bf16[2048,2048]{1,0:T(8,128)(2,1)} %all-gather.4.cloned.1.call-done.weight, f32[1024,512]{1,0:T(8,128)S(1)} %get-tuple-element.149.grad_hidden), custom_call_target="tpu_custom_call" | custom-call | flops 6442450944 | bytes 16777216 | tf_op jit(solution)/shard_map/pallas_call | solution.py:335
  675.6 7.7 reduce-scatter.6.cloned.1.call-done.other.values
  693.8 30.8 %collective-permute-done.58 = bf16[256,1024]{1,0:T(8,128)(2,1)S(1)} collective-permute-done((bf16[256,1024]{1,0:T(8,128)(2,1)S(1)}, bf16[256,1024]{1,0:T(8,128)(2,1)S(1)}, u32[]{:S(2)}, u32[]{:S(2)}) %collective-permute-start.58) | collective-permute-done | bytes 524320 | tf_op jit(solution)/shard_map/ppermute | solution.py:501
  739.8 7.6 collective-permute-done.59
  754.4 9.2 %collective-permute-done.66 = f32[8192]{0:T(1024)S(1)} collective-permute-done((f32[8192]{0:T(1024)S(1)}, f32[8192]{0:T(1024)S(1)}, u32[]{:S(2)}, u32[]{:S(2)}) %collective-permute-start.66) | collective-permute-done | bytes 32800 | tf_op jit(solution)/shard_map/ppermute | solution.py:501
  769.8 4.9 shard_map.312
  790.7 10.9 %shard_map.315 = (f32[64,16384]{1,0:T(8,128)}, f32[64,16384]{1,0:T(8,128)}, f32[64,16384]{1,0:T(8,128)}, f32[64,16384]{1,0:T(8,128)}) custom-call(bf16[256,4096]{1,0:T(8,128)(2,1)S(1)} %copy-done.5, f32[64,16384]{1,0:T(8,128)S(1)} %copy-done.3, f32[64,16384]{1,0:T(8,128)S(1)} %copy-done.21, f32[64,16384]{1,0:T(8,128)} %refs_3_.6), custom_call_target="tpu_custom_call" | custom-call | flops 12582912 | bytes 31457280 | tf_op jit(solution)/shard_map/pallas_call | solution.py:104
  808.0 7.4 shard_map.317
  (407 shorter events, 234.8 us)
Async XLA Ops:
  7.2 119.7 %all-gather.4.cloned.1.call-start = ((), (), s32[]{:S(2)}) async-start(), calls=%async_computation.10 | async-start | bytes 9437184 | tf_op jit(solution)/shard_map/all_gather | solution.py:599
  28.5 260.7 %all-gather.6.cloned.1.call-start = ((), (), s32[]{:S(2)}) async-start(), calls=%async_computation.11 | async-start | bytes 18874368 | tf_op jit(solution)/shard_map/all_gather | solution.py:600
  58.8 285.3 %all-gather.8.cloned.1.call-start = ((), (), s32[]{:S(2)}) async-start(), calls=%async_computation.12 | async-start | bytes 9437184 | tf_op jit(solution)/shard_map/all_gather | solution.py:601
  77.8 33.3 %collective-permute-start = (bf16[256,2048]{1,0:T(8,128)(2,1)}, bf16[256,2048]{1,0:T(8,128)(2,1)S(1)}, u32[]{:S(2)}, u32[]{:S(2)}) collective-permute-start(bf16[256,2048]{1,0:T(8,128)(2,1)} %param.15), channel_id=1, source_target_pairs={{0,1},{1,0},{2,3},{3,2},{4,5},{5,4},{6,7},{7,6},{8,9},{9,8},{10,11... | collective-permute-start | bytes 3145736 | tf_op jit(solution)/shard_map/ppermute | solution.py:501
  78.7 33.2 %collective-permute-start.1 = (bf16[256,2048]{1,0:T(8,128)(2,1)}, bf16[256,2048]{1,0:T(8,128)(2,1)}, u32[]{:S(2)}, u32[]{:S(2)}) collective-permute-start(bf16[256,2048]{1,0:T(8,128)(2,1)} %param.15), channel_id=1, source_target_pairs={{0,2},{1,3},{2,0},{3,1},{4,6},{5,7},{6,4},{7,5},{8,10},{9,11},{10,... | collective-permute-start | bytes 3145736 | tf_op jit(solution)/shard_map/ppermute | solution.py:501
  82.8 16.2 %collective-permute-start.15 = (s32[256]{0:T(256)S(1)}, s32[256]{0:T(256)S(1)}, u32[]{:S(2)}, u32[]{:S(2)}) collective-permute-start(s32[256]{0:T(256)S(1)} %copy-done.59), channel_id=1, source_target_pairs={{0,2},{1,3},{2,0},{3,1},{4,6},{5,7},{6,4},{7,5},{8,10},{9,11},{10,... | collective-permute-start | bytes 3080 | tf_op jit(solution)/shard_map/ppermute | solution.py:501
  84.3 14.8 %collective-permute-start.16 = (s32[256]{0:T(256)S(1)}, s32[256]{0:T(256)S(1)}, u32[]{:S(2)}, u32[]{:S(2)}) collective-permute-start(s32[256]{0:T(256)S(1)} %copy-done.59), channel_id=1, source_target_pairs={{0,3},{1,2},{2,1},{3,0},{4,7},{5,6},{6,5},{7,4},{8,11},{9,10},{10,... | collective-permute-start | bytes 3080 | tf_op jit(solution)/shard_map/ppermute | solution.py:501
  85.8 13.3 %collective-permute-start.14 = (s32[256]{0:T(256)S(1)}, s32[256]{0:T(256)S(1)}, u32[]{:S(2)}, u32[]{:S(2)}) collective-permute-start(s32[256]{0:T(256)S(1)} %copy-done.59), channel_id=1, source_target_pairs={{0,1},{1,0},{2,3},{3,2},{4,5},{5,4},{6,7},{7,6},{8,9},{9,8},{10,11... | collective-permute-start | bytes 3080 | tf_op jit(solution)/shard_map/ppermute | solution.py:501
  111.1 13.1 %collective-permute-start.2 = (bf16[256,1024]{1,0:T(8,128)(2,1)S(1)}, bf16[256,1024]{1,0:T(8,128)(2,1)}, u32[]{:S(2)}, u32[]{:S(2)}) collective-permute-start(bf16[256,1024]{1,0:T(8,128)(2,1)S(1)} %slice.80), channel_id=1, source_target_pairs={{0,2},{1,3},{2,0},{3,1},{4,6},{5,7},{6,4},{7,5},{8,10},{9,11},{10,... | collective-permute-start | bytes 1572872 | tf_op jit(solution)/shard_map/ppermute | solution.py:501
  113.0 13.1 %collective-permute-start.3 = (bf16[256,1024]{1,0:T(8,128)(2,1)S(1)}, bf16[256,1024]{1,0:T(8,128)(2,1)S(1)}, u32[]{:S(2)}, u32[]{:S(2)}) collective-permute-start(bf16[256,1024]{1,0:T(8,128)(2,1)S(1)} %slice.81), channel_id=1, source_target_pairs={{0,1},{1,0},{2,3},{3,2},{4,5},{5,4},{6,7},{7,6},{8,9},{9,8},{10,11... | collective-permute-start | bytes 1572872 | tf_op jit(solution)/shard_map/ppermute | solution.py:501
  164.6 22.2 %collective-permute-start.17 = (bf16[1024,512]{1,0:T(8,128)(2,1)}, bf16[1024,512]{1,0:T(8,128)(2,1)S(1)}, u32[]{:S(2)}, u32[]{:S(2)}) collective-permute-start(bf16[1024,512]{1,0:T(8,128)(2,1)} %get-tuple-element.42.refs_3_), channel_id=1, source_target_pairs={{0,1},{1,0},{2,3},{3,2},{4,5},{5,4},{6,7},{7,6},{8,9},{9,8},{10,11... | collective-permute-start | bytes 3145736 | tf_op jit(solution)/shard_map/ppermute | solution.py:501
  165.4 24.0 %collective-permute-start.18 = (bf16[1024,512]{1,0:T(8,128)(2,1)}, bf16[1024,512]{1,0:T(8,128)(2,1)}, u32[]{:S(2)}, u32[]{:S(2)}) collective-permute-start(bf16[1024,512]{1,0:T(8,128)(2,1)} %get-tuple-element.42.refs_3_), channel_id=1, source_target_pairs={{0,2},{1,3},{2,0},{3,1},{4,6},{5,7},{6,4},{7,5},{8,10},{9,11},{10,... | collective-permute-start | bytes 3145736 | tf_op jit(solution)/shard_map/ppermute | solution.py:501
  218.5 26.3 %collective-permute-start.24 = (bf16[1024,512]{1,0:T(8,128)(2,1)}, bf16[1024,512]{1,0:T(8,128)(2,1)S(1)}, u32[]{:S(2)}, u32[]{:S(2)}) collective-permute-start(bf16[1024,512]{1,0:T(8,128)(2,1)} %get-tuple-element.153), channel_id=1, source_target_pairs={{0,1},{1,0},{2,3},{3,2},{4,5},{5,4},{6,7},{7,6},{8,9},{9,8},{10,11... | collective-permute-start | bytes 3145736 | tf_op jit(solution)/shard_map/ppermute | solution.py:501
  219.4 31.9 %collective-permute-start.25 = (bf16[1024,512]{1,0:T(8,128)(2,1)}, bf16[1024,512]{1,0:T(8,128)(2,1)}, u32[]{:S(2)}, u32[]{:S(2)}) collective-permute-start(bf16[1024,512]{1,0:T(8,128)(2,1)} %get-tuple-element.153), channel_id=1, source_target_pairs={{0,2},{1,3},{2,0},{3,1},{4,6},{5,7},{6,4},{7,5},{8,10},{9,11},{10,... | collective-permute-start | bytes 3145736 | tf_op jit(solution)/shard_map/ppermute | solution.py:501
  221.7 35.3 %all-to-all-start.1 = ((bf16[4,256,512]{2,1,0:T(8,128)(2,1)}), bf16[4,256,512]{2,1,0:T(8,128)(2,1)S(1)}, u32[]{:S(2)}, u32[]{:S(2)}) async-start(bf16[4,256,512]{2,1,0:T(8,128)(2,1)} %bitcast.67), calls=%async_computation.1 | async-start | bytes 2097152 | tf_op jit(solution)/shard_map/all_to_all | solution.py:612
  225.4 349.6 %reduce-scatter.4.cloned.1.call-start = ((), (), s32[]{:S(2)}) async-start(), calls=%async_computation.13 | async-start | bytes 9437184 | tf_op jit(solution)/shard_map/reduce_scatter | solution.py:692
  244.8 30.1 %collective-permute-start.26 = (bf16[512,512]{1,0:T(8,128)(2,1)S(1)}, bf16[512,512]{1,0:T(8,128)(2,1)}, u32[]{:S(2)}, u32[]{:S(2)}) collective-permute-start(bf16[512,512]{1,0:T(8,128)(2,1)S(1)} %slice.88), channel_id=1, source_target_pairs={{0,2},{1,3},{2,0},{3,1},{4,6},{5,7},{6,4},{7,5},{8,10},{9,11},{10,... | collective-permute-start | bytes 1572872 | tf_op jit(solution)/shard_map/ppermute | solution.py:501
  253.2 23.5 %collective-permute-start.27 = (bf16[512,512]{1,0:T(8,128)(2,1)}, bf16[512,512]{1,0:T(8,128)(2,1)}, u32[]{:S(2)}, u32[]{:S(2)}) collective-permute-start(bf16[512,512]{1,0:T(8,128)(2,1)} %slice.89), channel_id=1, source_target_pairs={{0,1},{1,0},{2,3},{3,2},{4,5},{5,4},{6,7},{7,6},{8,9},{9,8},{10,11... | collective-permute-start | bytes 1572872 | tf_op jit(solution)/shard_map/ppermute | solution.py:501
  357.4 14.8 %collective-permute-start.29 = (bf16[256,1024]{1,0:T(8,128)(2,1)S(1)}, bf16[256,1024]{1,0:T(8,128)(2,1)S(1)}, u32[]{:S(2)}, u32[]{:S(2)}) collective-permute-start(bf16[256,1024]{1,0:T(8,128)(2,1)S(1)} %get-tuple-element.177), channel_id=1, source_target_pairs={{0,1},{1,0},{2,3},{3,2},{4,5},{5,4},{6,7},{7,6},{8,9},{9,8},{10,11... | collective-permute-start | bytes 1572872 | tf_op jit(solution)/shard_map/ppermute | solution.py:501
  358.9 23.8 %collective-permute-start.28 = (bf16[256,1024]{1,0:T(8,128)(2,1)S(1)}, bf16[256,1024]{1,0:T(8,128)(2,1)S(1)}, u32[]{:S(2)}, u32[]{:S(2)}) collective-permute-start(bf16[256,1024]{1,0:T(8,128)(2,1)S(1)} %get-tuple-element.174), channel_id=1, source_target_pairs={{0,1},{1,0},{2,3},{3,2},{4,5},{5,4},{6,7},{7,6},{8,9},{9,8},{10,11... | collective-permute-start | bytes 1572872 | tf_op jit(solution)/shard_map/ppermute | solution.py:501
  359.4 23.3 %collective-permute-start.32 = (bf16[256,1024]{1,0:T(8,128)(2,1)S(1)}, bf16[256,1024]{1,0:T(8,128)(2,1)S(1)}, u32[]{:S(2)}, u32[]{:S(2)}) collective-permute-start(bf16[256,1024]{1,0:T(8,128)(2,1)S(1)} %get-tuple-element.175), channel_id=1, source_target_pairs={{0,2},{1,3},{2,0},{3,1},{4,6},{5,7},{6,4},{7,5},{8,10},{9,11},{10,... | collective-permute-start | bytes 1572872 | tf_op jit(solution)/shard_map/ppermute | solution.py:501
  372.4 14.9 %collective-permute-start.30 = (bf16[256,1024]{1,0:T(8,128)(2,1)S(1)}, bf16[256,1024]{1,0:T(8,128)(2,1)S(1)}, u32[]{:S(2)}, u32[]{:S(2)}) collective-permute-start(bf16[256,1024]{1,0:T(8,128)(2,1)S(1)} %add_convert_fusion.11), channel_id=1, source_target_pairs={{0,2},{1,3},{2,0},{3,1},{4,6},{5,7},{6,4},{7,5},{8,10},{9,11},{10,... | collective-permute-start | bytes 1572872 | tf_op jit(solution)/shard_map/ppermute | solution.py:501
  373.9 22.3 %collective-permute-start.31 = (bf16[256,1024]{1,0:T(8,128)(2,1)S(1)}, bf16[256,1024]{1,0:T(8,128)(2,1)S(1)}, u32[]{:S(2)}, u32[]{:S(2)}) collective-permute-start(bf16[256,1024]{1,0:T(8,128)(2,1)S(1)} %get-tuple-element.176), channel_id=1, source_target_pairs={{0,2},{1,3},{2,0},{3,1},{4,6},{5,7},{6,4},{7,5},{8,10},{9,11},{10,... | collective-permute-start | bytes 1572872 | tf_op jit(solution)/shard_map/ppermute | solution.py:501
  402.4 22.0 %collective-permute-start.34 = (bf16[256,2048]{1,0:T(8,128)(2,1)S(1)}, bf16[256,2048]{1,0:T(8,128)(2,1)S(1)}, u32[]{:S(2)}, u32[]{:S(2)}) collective-permute-start(bf16[256,2048]{1,0:T(8,128)(2,1)S(1)} %get-tuple-element.151), channel_id=1, source_target_pairs={{0,1},{1,0},{2,3},{3,2},{4,5},{5,4},{6,7},{7,6},{8,9},{9,8},{10,11... | collective-permute-start | bytes 3145736 | tf_op jit(solution)/shard_map/ppermute | solution.py:501
  404.0 24.2 %collective-permute-start.35 = (bf16[256,2048]{1,0:T(8,128)(2,1)S(1)}, bf16[256,2048]{1,0:T(8,128)(2,1)S(1)}, u32[]{:S(2)}, u32[]{:S(2)}) collective-permute-start(bf16[256,2048]{1,0:T(8,128)(2,1)S(1)} %get-tuple-element.151), channel_id=1, source_target_pairs={{0,2},{1,3},{2,0},{3,1},{4,6},{5,7},{6,4},{7,5},{8,10},{9,11},{10,... | collective-permute-start | bytes 3145736 | tf_op jit(solution)/shard_map/ppermute | solution.py:501
  450.9 232.4 %reduce-scatter.6.cloned.1.call-start = ((), (), s32[]{:S(2)}) async-start(), calls=%async_computation.14 | async-start | bytes 10485760 | tf_op jit(solution)/shard_map/reduce_scatter | solution.py:701
  483.0 23.9 %collective-permute-start.56 = (bf16[1024,4096]{1,0:T(8,128)(2,1)}, bf16[1024,4096]{1,0:T(8,128)(2,1)}, u32[]{:S(2)}, u32[]{:S(2)}) collective-permute-start(bf16[1024,4096]{1,0:T(8,128)(2,1)} %shard_map.297.other), channel_id=1, source_target_pairs={{0,4},{4,0},{1,5},{5,1},{2,6},{6,2},{3,7},{7,3},{8,12},{12,8},{9,1... | collective-permute-start | bytes 25165832 | tf_op jit(solution)/shard_map/ppermute | solution.py:471
  523.7 254.3 %reduce-scatter.8.cloned.1.call-start = ((), (), s32[]{:S(2)}) async-start(), calls=%async_computation.15 | async-start | bytes 9437184 | tf_op jit(solution)/shard_map/reduce_scatter | solution.py:728
  525.6 14.8 %collective-permute-start.39 = (bf16[512,512]{1,0:T(8,128)(2,1)S(1)}, bf16[512,512]{1,0:T(8,128)(2,1)S(1)}, u32[]{:S(2)}, u32[]{:S(2)}) collective-permute-start(bf16[512,512]{1,0:T(8,128)(2,1)S(1)} %get-tuple-element.171), channel_id=1, source_target_pairs={{0,1},{1,0},{2,3},{3,2},{4,5},{5,4},{6,7},{7,6},{8,9},{9,8},{10,11... | collective-permute-start | bytes 1572872 | tf_op jit(solution)/shard_map/ppermute | solution.py:501
  525.7 25.5 %collective-permute-start.38 = (bf16[512,512]{1,0:T(8,128)(2,1)S(1)}, bf16[512,512]{1,0:T(8,128)(2,1)S(1)}, u32[]{:S(2)}, u32[]{:S(2)}) collective-permute-start(bf16[512,512]{1,0:T(8,128)(2,1)S(1)} %get-tuple-element.168), channel_id=1, source_target_pairs={{0,1},{1,0},{2,3},{3,2},{4,5},{5,4},{6,7},{7,6},{8,9},{9,8},{10,11... | collective-permute-start | bytes 1572872 | tf_op jit(solution)/shard_map/ppermute | solution.py:501
  527.7 23.5 %collective-permute-start.42 = (bf16[512,512]{1,0:T(8,128)(2,1)S(1)}, bf16[512,512]{1,0:T(8,128)(2,1)S(1)}, u32[]{:S(2)}, u32[]{:S(2)}) collective-permute-start(bf16[512,512]{1,0:T(8,128)(2,1)S(1)} %get-tuple-element.169), channel_id=1, source_target_pairs={{0,2},{1,3},{2,0},{3,1},{4,6},{5,7},{6,4},{7,5},{8,10},{9,11},{10,... | collective-permute-start | bytes 1572872 | tf_op jit(solution)/shard_map/ppermute | solution.py:501
  540.6 14.9 %collective-permute-start.40 = (bf16[512,512]{1,0:T(8,128)(2,1)S(1)}, bf16[512,512]{1,0:T(8,128)(2,1)S(1)}, u32[]{:S(2)}, u32[]{:S(2)}) collective-permute-start(bf16[512,512]{1,0:T(8,128)(2,1)S(1)} %add_convert_fusion.9), channel_id=1, source_target_pairs={{0,2},{1,3},{2,0},{3,1},{4,6},{5,7},{6,4},{7,5},{8,10},{9,11},{10,... | collective-permute-start | bytes 1572872 | tf_op jit(solution)/shard_map/ppermute | solution.py:501
  542.1 22.9 %collective-permute-start.41 = (bf16[512,512]{1,0:T(8,128)(2,1)S(1)}, bf16[512,512]{1,0:T(8,128)(2,1)S(1)}, u32[]{:S(2)}, u32[]{:S(2)}) collective-permute-start(bf16[512,512]{1,0:T(8,128)(2,1)S(1)} %get-tuple-element.170), channel_id=1, source_target_pairs={{0,2},{1,3},{2,0},{3,1},{4,6},{5,7},{6,4},{7,5},{8,10},{9,11},{10,... | collective-permute-start | bytes 1572872 | tf_op jit(solution)/shard_map/ppermute | solution.py:501
  579.6 14.9 %collective-permute-start.48 = (bf16[512,512]{1,0:T(8,128)(2,1)S(1)}, bf16[512,512]{1,0:T(8,128)(2,1)S(1)}, u32[]{:S(2)}, u32[]{:S(2)}) collective-permute-start(bf16[512,512]{1,0:T(8,128)(2,1)S(1)} %get-tuple-element.165), channel_id=1, source_target_pairs={{0,1},{1,0},{2,3},{3,2},{4,5},{5,4},{6,7},{7,6},{8,9},{9,8},{10,11... | collective-permute-start | bytes 1572872 | tf_op jit(solution)/shard_map/ppermute | solution.py:501
  580.7 20.0 %collective-permute-start.47 = (bf16[512,512]{1,0:T(8,128)(2,1)S(1)}, bf16[512,512]{1,0:T(8,128)(2,1)S(1)}, u32[]{:S(2)}, u32[]{:S(2)}) collective-permute-start(bf16[512,512]{1,0:T(8,128)(2,1)S(1)} %get-tuple-element.162), channel_id=1, source_target_pairs={{0,1},{1,0},{2,3},{3,2},{4,5},{5,4},{6,7},{7,6},{8,9},{9,8},{10,11... | collective-permute-start | bytes 1572872 | tf_op jit(solution)/shard_map/ppermute | solution.py:501
  581.6 19.0 %collective-permute-start.51 = (bf16[512,512]{1,0:T(8,128)(2,1)S(1)}, bf16[512,512]{1,0:T(8,128)(2,1)S(1)}, u32[]{:S(2)}, u32[]{:S(2)}) collective-permute-start(bf16[512,512]{1,0:T(8,128)(2,1)S(1)} %get-tuple-element.163), channel_id=1, source_target_pairs={{0,2},{1,3},{2,0},{3,1},{4,6},{5,7},{6,4},{7,5},{8,10},{9,11},{10,... | collective-permute-start | bytes 1572872 | tf_op jit(solution)/shard_map/ppermute | solution.py:501
  596.3 17.0 %collective-permute-start.50 = (bf16[512,512]{1,0:T(8,128)(2,1)S(1)}, bf16[512,512]{1,0:T(8,128)(2,1)S(1)}, u32[]{:S(2)}, u32[]{:S(2)}) collective-permute-start(bf16[512,512]{1,0:T(8,128)(2,1)S(1)} %get-tuple-element.164), channel_id=1, source_target_pairs={{0,2},{1,3},{2,0},{3,1},{4,6},{5,7},{6,4},{7,5},{8,10},{9,11},{10,... | collective-permute-start | bytes 1572872 | tf_op jit(solution)/shard_map/ppermute | solution.py:501
  683.4 49.5 %all-to-all-start.4 = ((bf16[4,64,4096]{2,1,0:T(8,128)(2,1)}), bf16[4,64,4096]{2,1,0:T(8,128)(2,1)S(1)}, u32[]{:S(2)}, u32[]{:S(2)}) async-start(bf16[4,64,4096]{2,1,0:T(8,128)(2,1)} %bitcast.78), calls=%async_computation.6 | async-start | bytes 4194304 | tf_op jit(solution)/shard_map/all_to_all | solution.py:689
  689.7 34.8 %collective-permute-start.58 = (bf16[256,1024]{1,0:T(8,128)(2,1)S(1)}, bf16[256,1024]{1,0:T(8,128)(2,1)S(1)}, u32[]{:S(2)}, u32[]{:S(2)}) collective-permute-start(bf16[256,1024]{1,0:T(8,128)(2,1)S(1)} %get-tuple-element.159), channel_id=1, source_target_pairs={{0,1},{1,0},{2,3},{3,2},{4,5},{5,4},{6,7},{7,6},{8,9},{9,8},{10,11... | collective-permute-start | bytes 1572872 | tf_op jit(solution)/shard_map/ppermute | solution.py:501
  691.8 45.9 %collective-permute-start.57 = (bf16[256,1024]{1,0:T(8,128)(2,1)}, bf16[256,1024]{1,0:T(8,128)(2,1)}, u32[]{:S(2)}, u32[]{:S(2)}) collective-permute-start(bf16[256,1024]{1,0:T(8,128)(2,1)} %get-tuple-element.156), channel_id=1, source_target_pairs={{0,1},{1,0},{2,3},{3,2},{4,5},{5,4},{6,7},{7,6},{8,9},{9,8},{10,11... | collective-permute-start | bytes 1572872 | tf_op jit(solution)/shard_map/ppermute | solution.py:501
  691.8 46.1 %collective-permute-start.68 = (bf16[256,1024]{1,0:T(8,128)(2,1)}, bf16[256,1024]{1,0:T(8,128)(2,1)}, u32[]{:S(2)}, u32[]{:S(2)}) collective-permute-start(bf16[256,1024]{1,0:T(8,128)(2,1)} %get-tuple-element.157), channel_id=1, source_target_pairs={{0,2},{1,3},{2,0},{3,1},{4,6},{5,7},{6,4},{7,5},{8,10},{9,11},{10,... | collective-permute-start | bytes 1572872 | tf_op jit(solution)/shard_map/ppermute | solution.py:501
  726.6 20.8 %collective-permute-start.59 = (bf16[256,1024]{1,0:T(8,128)(2,1)}, bf16[256,1024]{1,0:T(8,128)(2,1)}, u32[]{:S(2)}, u32[]{:S(2)}) collective-permute-start(bf16[256,1024]{1,0:T(8,128)(2,1)} %add_convert_fusion.3), channel_id=1, source_target_pairs={{0,2},{1,3},{2,0},{3,1},{4,6},{5,7},{6,4},{7,5},{8,10},{9,11},{10,... | collective-permute-start | bytes 1572872 | tf_op jit(solution)/shard_map/ppermute | solution.py:501
  728.7 46.0 %collective-permute-start.67 = (bf16[256,1024]{1,0:T(8,128)(2,1)}, bf16[256,1024]{1,0:T(8,128)(2,1)}, u32[]{:S(2)}, u32[]{:S(2)}) collective-permute-start(bf16[256,1024]{1,0:T(8,128)(2,1)} %get-tuple-element.158), channel_id=1, source_target_pairs={{0,2},{1,3},{2,0},{3,1},{4,6},{5,7},{6,4},{7,5},{8,10},{9,11},{10,... | collective-permute-start | bytes 1572872 | tf_op jit(solution)/shard_map/ppermute | solution.py:501
  729.9 20.8 %collective-permute-start.63 = (f32[8192]{0:T(1024)S(1)}, f32[8192]{0:T(1024)S(1)}, u32[]{:S(2)}, u32[]{:S(2)}) collective-permute-start(f32[8192]{0:T(1024)S(1)} %add.410), channel_id=1, source_target_pairs={{0,24},{8,0},{16,8},{24,16},{1,25},{9,1},{17,9},{25,17},{2,26},{10... | collective-permute-start | bytes 98312 | tf_op jit(solution)/shard_map/ppermute | solution.py:475
  732.9 32.0 %all-to-all-start.5 = ((bf16[4,64,2048]{2,1,0:T(8,128)(2,1)}), bf16[4,64,2048]{2,1,0:T(8,128)(2,1)S(1)}, u32[]{:S(2)}, u32[]{:S(2)}) async-start(bf16[4,64,2048]{2,1,0:T(8,128)(2,1)} %bitcast.82), calls=%async_computation.8 | async-start | bytes 2097152 | tf_op jit(solution)/shard_map/all_to_all | solution.py:689
  737.6 13.1 %collective-permute-start.62 = (f32[8192]{0:T(1024)S(1)}, f32[8192]{0:T(1024)S(1)}, u32[]{:S(2)}, u32[]{:S(2)}) collective-permute-start(f32[8192]{0:T(1024)S(1)} %add.410), channel_id=1, source_target_pairs={{0,16},{8,24},{16,0},{24,8},{1,17},{9,25},{17,1},{25,9},{2,18},{10... | collective-permute-start | bytes 98312 | tf_op jit(solution)/shard_map/ppermute | solution.py:475
  750.7 24.0 %collective-permute-start.69 = (bf16[256,1024]{1,0:T(8,128)(2,1)}, bf16[256,1024]{1,0:T(8,128)(2,1)}, u32[]{:S(2)}, u32[]{:S(2)}) collective-permute-start(bf16[256,1024]{1,0:T(8,128)(2,1)} %get-tuple-element.155), channel_id=1, source_target_pairs={{0,1},{1,0},{2,3},{3,2},{4,5},{5,4},{6,7},{7,6},{8,9},{9,8},{10,11... | collective-permute-start | bytes 1572872 | tf_op jit(solution)/shard_map/ppermute | solution.py:501
  778.0 23.7 %all-to-all-start.6 = ((bf16[4,64,2048]{2,1,0:T(8,128)(2,1)}), bf16[4,64,2048]{2,1,0:T(8,128)(2,1)S(1)}, u32[]{:S(2)}, u32[]{:S(2)}) async-start(bf16[4,64,2048]{2,1,0:T(8,128)(2,1)} %bitcast.80), calls=%async_computation.9 | async-start | bytes 2097152 | tf_op jit(solution)/shard_map/all_to_all | solution.py:689
  (92 other events, 1524.7 us)
Sparse Core Ops, SparseCore 0:
  28.6 82.2 all-gather.3
  112.5 149.6 all-gather.5
  263.8 80.2 all-gather.7
  451.1 87.1 reduce-scatter.3
  540.5 142.8 reduce-scatter.5
  685.5 92.4 reduce-scatter.7

commit v4 on v3

--- a/solution.py
+++ b/solution.py
@@ -315,7 +315,7 @@
         + [row_spec(columns)] * len(other),
         out_specs=row_spec(columns),
         out_shape=jax.ShapeDtypeStruct((width, columns), bf16),
-        compiler_params=pltpu.CompilerParams(vmem_limit_bytes=48 * 1024 * 1024),
+        compiler_params=pltpu.CompilerParams(vmem_limit_bytes=ALL_VMEM),
         cost_estimate=pl.CostEstimate(
             flops=2 * width * length * columns,
             bytes_accessed=6 * width * length,
@@ -345,7 +345,7 @@
             out_specs=pl.BlockSpec((length, part), lambda j, place: (0, j)),
         ),
         out_shape=jax.ShapeDtypeStruct((length, width), bf16),
-        compiler_params=pltpu.CompilerParams(vmem_limit_bytes=48 * 1024 * 1024),
+        compiler_params=pltpu.CompilerParams(vmem_limit_bytes=ALL_VMEM),
         cost_estimate=pl.CostEstimate(
             flops=2 * width * length * wide, bytes_accessed=8 * width * length, transcendentals=0
         ),
@@ -500,7 +500,7 @@
     def swap(self, values, bit):
         return lax.ppermute(values, FSDP, [(i, i ^ bit) for i in range(self.count)])
 
-    def gather(self, block, axis):
+    def gather(self, block, axis, fill=0):
         if not self.square:
             return lax.all_gather(block, FSDP, axis=axis, tiled=True)
         other = 1 - axis
@@ -510,7 +510,7 @@
         high = self.swap(lax.slice_in_dim(by_y, cut, 2 * cut, axis=other), 1)
         shape = list(block.shape)
         shape[axis] = size * 4
-        out = jnp.zeros(shape, block.dtype)
+        out = jnp.full(shape, fill, block.dtype)
         for part, bit, offset in ((block, 0, 0), (by_x, 1, 0), (by_y, 2, 0), (low, 3, 0), (high, 3, cut)):
             start = [0, 0]
             start[axis] = (self.place ^ bit) * size
@@ -518,7 +518,7 @@
             out = lax.dynamic_update_slice(out, part, start)
         return out
 
-    def scatter(self, partial, axis, kind=f32, last=(0, 0)):
+    def scatter(self, partial, axis, kind=f32, hop=0, last=(0, 0)):
         if not self.square:
             total = lax.psum_scatter(partial, FSDP, scatter_dimension=axis, tiled=True)
             return total.astype(f32)
@@ -539,7 +539,7 @@
         for (offset, first, second), zero in zip(((0, 1, 2), (cut, 2, 1)), last):
             relay = self.swap(piece(3, offset), first)
             mine = self.swap(piece(first, offset), first)
-            relay = (piece(second, offset).astype(f32) + relay.astype(f32)).astype(bf16)
+            relay = (piece(second, offset, hop).astype(f32) + relay.astype(f32)).astype(bf16)
             halves.append(
                 piece(0, offset, zero).astype(f32) + mine.astype(f32) + self.swap(relay, second).astype(f32)
             )
@@ -637,14 +637,14 @@
     inverse = jnp.transpose(lax.rsqrt(squares / width + norm_eps).reshape(2, length))
     tables = (inverse, gain_rows, cosine, sine, first_key)
     query, key, value, attended_low, lse = attend(qkv, *tables)
-    attended_full = plane.gather(attended_low, 1)
+    attended_full = plane.gather(attended_low, 1, 1)
 
     branch = mm(attended_full, out_weight, ((1,), (0,)))
     branch_inv = lax.rsqrt(plane.total(jnp.sum(branch * branch, axis=1)) / width + norm_eps)[:, None]
     branch_hat = branch * branch_inv
     token_part = lax.dynamic_slice_in_dim(token_full, place * part, part, 1).astype(f32)
     hidden_low = (token_part + branch_hat * gain_part[None, :, 2]).astype(bf16)
-    hidden_full = plane.gather(hidden_low, 1)
+    hidden_full = plane.gather(hidden_low, 1, 2)
 
     core = lax.axis_index("core")
     share = width // (2 * copies.count)
@@ -664,8 +664,8 @@
         ]
 
     other_side, own_side = sides(hidden_full)
-    token_turned, attended_turned = jnp.transpose(token_full), jnp.transpose(attended_full)
-    for early in (other_side, own_side, token_turned, attended_turned, cot_part):
+    token_sides, attended_sides = sides(token_full), sides(attended_full)
+    for early in (other_side, own_side, *token_sides, *attended_sides, cot_part):
         hidden_full = order(hidden_full, early)
     gate_up, gate_up_back = gate_up_kernels(length, width, wide)
     both, activ = gate_up(hidden_full, gate_up_all)
@@ -679,8 +679,9 @@
     scaled = grad_out * gain_values[None, :, 3]
     grad_mlp = mlp_inv * (scaled - mlp_hat * jnp.mean(scaled * mlp_hat, axis=1, keepdims=True))
     grad_gain_mlp = jnp.sum(grad_out * mlp_hat, axis=0)
+    by_rows = Layout(major_to_minor=(0, 1))
     grad_mlp_full = with_layout_constraint(
-        plane.gather(grad_mlp.astype(bf16), 0), Layout(major_to_minor=(0, 1))
+        plane.gather(with_layout_constraint(grad_mlp.astype(bf16), by_rows), 0, 3), by_rows
     )
 
     def exchanged(mine, *wait):
@@ -697,7 +698,7 @@
     late = order(grad_gate_up_low, send)
     hidden_partial = mm(late, gate_up_all, ((1,), (1,))).astype(bf16)
     grad_hidden = cot_part + plane.scatter(hidden_partial, 1)
-    gate_up_partial = half_grad(order(own_side, hidden_partial), late, got)
+    gate_up_partial = half_grad(order(own_side, hidden_partial[:16, :128]), late, got)
     gate_up_mine = lax.psum_scatter(gate_up_partial, "z", scatter_dimension=0, tiled=True)
 
     scaled = grad_hidden * gain_part[None, :, 2]
@@ -721,17 +722,24 @@
     gain_sums = plane.total(copies.total(gain_sums)).reshape(4, width)
     owner = lax.axis_index(DP + FSDP)
     grad_gains = jnp.transpose(lax.dynamic_slice_in_dim(gain_sums, owner * owned, owned, 1))
-    attn_partial = attn_grad(token_turned, grad_qkv_low, attended_turned, grad_branch)
-    late = order(grad_qkv_low, attn_partial)
+    send = attn_grad(token_sides[0], grad_qkv_low, attended_sides[0], grad_branch)
+    got = copies.swap(send)
+    late = order(grad_qkv_low, send)
     back = token_grad(jnp.full((1,), place), late, attn_all, grad_hidden)
-    attn_partial = order(order(attn_partial, back), gate_up_mine)
-    attn_mine = lax.psum_scatter(attn_partial, DP, scatter_dimension=0, tiled=True)
+    late = order(late, back)
+    attn_partial = attn_grad(token_sides[1], late, attended_sides[1], grad_branch, got)
+    down_part = exchanged(down_mine, grad_qkv_low)
+    attn_partial = order(order(attn_partial, down_part), gate_up_mine)
+    attn_mine = lax.psum_scatter(attn_partial, "z", scatter_dimension=0, tiled=True)
     gate_up_part = exchanged(gate_up_mine, attn_partial)
+    grad_down, new_down, new_m_down, new_v_down = adamw_kernel(
+        order(down_part, attn_partial), w_down, m_down, v_down, 1, count
+    )
     grad_tokens = plane.scatter(
-        back, 0, last=(zero_after(gate_up_part), zero_after(grad_gains))
-    )
-    grad_down, new_down, new_m_down, new_v_down = adamw_kernel(
-        exchanged(down_mine, attn_partial), w_down, m_down, v_down, 1, count
+        back,
+        0,
+        hop=zero_after(new_down),
+        last=(zero_after(gate_up_part), zero_after(grad_gains)),
     )
     attn_mine = order(order(attn_mine, grad_tokens), new_down)
     attn_part = exchanged(attn_mine)

time: 829 us -> 819 us (0.988)
  waiting for transfers between devices: 296 us -> 271 us
    ppermute x61, waiting for transfers between devices: 252 us -> 231 us  [swap(): return lax.ppermute(values, FSDP, [(i, i ^ bit) for i in range(self.count)])]
    transpose x4 -> x0, local copies, waits for them, and re-layouts: 18 us -> none  [the longest x1 6.48 us: per_device(): jnp.transpose(attended_full)]
    all_gather x1, waiting for transfers between devices: 28.2 us -> 37.7 us  [per_device(): down_all = lax.all_gather(spread(w_down, 1), DP, axis=0, tiled=True)]
    dynamic_update_slice x18 -> x19, local copies, waits for them, and re-layouts: 17.3 us -> 24.4 us  [gather(): out = lax.dynamic_update_slice(out, part, start)]
    pallas_call x1 -> x2, Pallas kernels: 12.3 us -> 18.7 us  [attn_grad(): pl.pallas_call(attn_grad_body, grid=(width // rows,), in_specs=[row_spec(...]
    unnamed x127 -> x135, local copies, waits for them, and re-layouts: 36.7 us -> 42.5 us
  transfers between devices with their start and end apart: 80 -> 81, of which waited for: 48 -> 48; matrix products, arithmetic and copies ran while one was open for 16% -> 17% of each run, Pallas kernels for 18% -> 20%
where the time goes in v4:
time: 819 us; the launch traced here: 812 us
  waiting for transfers between devices  271 us (33%)
  Pallas kernels  167 us (20%)
  local copies, waits for them, and re-layouts  104 us (13%)
  starting transfers between devices  89.7 us (11%)
  matrix products  67.6 us (8%)
  blocking collectives  61.5 us (8%)
  other arithmetic  33 us (4%)
  between operations  17.6 us (2%)
    ppermute x61, waiting for transfers between devices, swap(): return lax.ppermute(values, FSDP, [(i, i ^ bit) for i in range(self.count)])  231 us
    dot_general x6, matrix products, mm(): lax.dot_general(left, right, (dims, ((), ())), preferred_element_type=f32)  67.6 us
    ppermute x61, starting transfers between devices, swap(): return lax.ppermute(values, FSDP, [(i, i ^ bit) for i in range(self.count)])  67 us
    all_to_all x3, blocking collectives, spread(): return lax.all_to_all(block, FSDP, 0, 0, tiled=True)  61.5 us
    unnamed x135, local copies, waits for them, and re-layouts  42.5 us
    all_gather x1, waiting for transfers between devices, per_device(): down_all = lax.all_gather(spread(w_down, 1), DP, axis=0, tiled=True)  37.7 us
    pallas_call x2, Pallas kernels, half_grad(): pl.pallas_call(half_grad_body, grid=(columns // size,), in_specs=[pl.Bloc...  28.6 us
    pallas_call x1, Pallas kernels, forward(): pl.pallas_call(gate_up_body, grid=(wide // TILE,), in_specs=[rows_spec, c...  24.7 us
  transfers between devices with their start and end apart: 81, of which 48 were waited for; matrix products, arithmetic and copies ran while one was open for 17% of the time, Pallas kernels for 20%

profile of v4, /device:TPU:0, one launch (start us, length us, event | category | flops | bytes accessed | tf_op | source)
XLA Modules:
  0.0 811.8 jit_solution(3233387070289551082)
XLA Ops:
  9.2 19.2 %all_to_all.75 = bf16[4,64,2048]{2,1,0:T(8,128)(2,1)} all-to-all(bf16[4,64,2048]{2,1,0:T(8,128)(2,1)S(1)} %bitcast.77), channel_id=1, replica_groups=mesh['z'=4,'core'=2,'y'=2,'x'=2] {'y','x'}, dimensions={0} | all-to-all | bytes 2097152 | tf_op jit(solution)/shard_map/all_to_all | solution.py:597
  31.3 27.5 %all_to_all.76 = bf16[4,64,4096]{2,1,0:T(8,128)(2,1)} all-to-all(bf16[4,64,4096]{2,1,0:T(8,128)(2,1)S(1)} %bitcast.76), channel_id=1, replica_groups=mesh['z'=4,'core'=2,'y'=2,'x'=2] {'y','x'}, dimensions={0} | all-to-all | bytes 4194304 | tf_op jit(solution)/shard_map/all_to_all | solution.py:597
  59.2 14.8 %all_to_all.77 = bf16[4,64,2048]{2,1,0:T(8,128)(2,1)} all-to-all(bf16[4,64,2048]{2,1,0:T(8,128)(2,1)S(1)} %bitcast.78), channel_id=1, replica_groups=mesh['z'=4,'core'=2,'y'=2,'x'=2] {'y','x'}, dimensions={0} | all-to-all | bytes 2097152 | tf_op jit(solution)/shard_map/all_to_all | solution.py:597
  84.2 12.3 %collective-permute-done.7 = f32[256]{0:T(256)S(1)} collective-permute-done((f32[256]{0:T(256)S(1)}, f32[256]{0:T(256)S(1)}, u32[]{:S(2)}, u32[]{:S(2)}) %collective-permute-start.7) | collective-permute-done | bytes 1056 | tf_op jit(solution)/shard_map/ppermute | solution.py:501
  128.0 10.6 %fusion.refs_0_.refs_1_.refs_2_.refs_6_.refs_7_.raw = f32[1024,1536]{1,0:T(8,128)S(1)} fusion(bf16[1024,2048]{0,1:T(8,128)(2,1)} %constant_dynamic-update-slice_fusion.19, bf16[2048,2048]{1,0:T(8,128)(2,1)} %all-gather.4.cloned.1.call-done.weight), kind=kOutput, calls=%fused_computation.1 | convolution fusion | flops 6442450944 | bytes 16777216 | tf_op jit(solution)/shard_map/dot_general | solution.py:33
  145.8 17.7 %shard_map.287 = (bf16[1024,512]{1,0:T(8,128)(2,1)S(1)}, bf16[1024,512]{1,0:T(8,128)(2,1)S(1)}, bf16[1024,512]{1,0:T(8,128)(2,1)S(1)}, bf16[1024,512]{1,0:T(8,128)(2,1)}, f32[4,1024,1]{2,1,0:T(8,128)}) custom-call(f32[1024,1536]{1,0:T(8,128)} %copy-done.36, f32[1024,1536]{1,0:T(8,128)} %copy-done.36, f32[1024,1536]{1,0:T(8,128)} %copy-done.36, ...), custom_call_target="tpu_custom_call" | custom-call | flops 2147483648 | bytes 10485760 | tf_op jit(solution)/shard_map/pallas_call | solution.py:218
  170.3 17.7 %collective-permute-done.17 = bf16[1024,512]{0,1:T(8,128)(2,1)S(1)} collective-permute-done((bf16[1024,512]{0,1:T(8,128)(2,1)S(1)}, bf16[1024,512]{0,1:T(8,128)(2,1)S(1)}, u32[]{:S(2)}, u32[]{:S(2)}) %collective-permute-start.17) | collective-permute-done | bytes 1048608 | tf_op jit(solution)/shard_map/ppermute | solution.py:501
  191.8 4.3 all-to-all-start.1
  201.7 6.5 collective-permute-done.19
  209.4 5.2 collective-permute-done.20
  214.7 5.5 multiply_reduce_fusion.3
  245.1 6.4 collective-permute-done.24
  266.9 6.7 copy.143.values
  279.5 24.7 %shard_map.296 = (f32[1024,4096]{1,0:T(8,128)}, bf16[1024,2048]{1,0:T(8,128)(2,1)S(1)}) custom-call(bf16[1024,2048]{1,0:T(8,128)(2,1)} %shard_map.294.hidden, bf16[2048,4096]{1,0:T(8,128)(2,1)} %all-gather.6.cloned.1.call-done.weight), custom_call_target="tpu_custom_call" | custom-call | flops 17179869184 | bytes 37748736 | tf_op jit(solution)/shard_map/pallas_call | solution.py:408
  306.1 37.7 %all-gather.8.cloned.1.call-done.weight = bf16[2048,2048]{1,0:T(8,128)(2,1)} async-done(((bf16[256,2048]{1,0:T(8,128)(2,1)}), bf16[2048,2048]{1,0:T(8,128)(2,1)}) %all-gather.8.cloned.1.call-update) | async-done | bytes 8388624 | tf_op jit(solution)/shard_map/all_gather | solution.py:601
  343.9 12.8 %convolution_convert_fusion.3 = bf16[1024,2048]{1,0:T(8,128)(2,1)S(1)} fusion(bf16[1024,2048]{1,0:T(8,128)(2,1)} %copy-done.34, bf16[2048,2048]{1,0:T(8,128)(2,1)} %all-gather.8.cloned.1.call-done.weight), kind=kOutput, calls=%fused_computation.5 | convolution fusion | flops 8592031744 | bytes 16777216 | tf_op jit(solution)/shard_map/dot_general | solution.py:33
  360.5 11.2 %collective-permute-done.29 = bf16[256,1024]{1,0:T(8,128)(2,1)S(1)} collective-permute-done((bf16[256,1024]{1,0:T(8,128)(2,1)S(1)}, bf16[256,1024]{1,0:T(8,128)(2,1)S(1)}, u32[]{:S(2)}, u32[]{:S(2)}) %collective-permute-start.29) | collective-permute-done | bytes 524320 | tf_op jit(solution)/shard_map/ppermute | solution.py:501
  374.0 8.2 %collective-permute-done.28 = bf16[256,1024]{1,0:T(8,128)(2,1)S(1)} collective-permute-done((bf16[256,1024]{1,0:T(8,128)(2,1)S(1)}, bf16[256,1024]{1,0:T(8,128)(2,1)S(1)}, u32[]{:S(2)}, u32[]{:S(2)}) %collective-permute-start.28) | collective-permute-done | bytes 524320 | tf_op jit(solution)/shard_map/ppermute | solution.py:501
  382.2 4.6 collective-permute-done.30
  388.9 6.9 collective-permute-done.31
  405.0 18.9 %collective-permute-done.34 = bf16[256,2048]{1,0:T(8,128)(2,1)S(1)} collective-permute-done((bf16[256,2048]{1,0:T(8,128)(2,1)S(1)}, bf16[256,2048]{1,0:T(8,128)(2,1)S(1)}, u32[]{:S(2)}, u32[]{:S(2)}) %collective-permute-start.34) | collective-permute-done | bytes 1048608 | tf_op jit(solution)/shard_map/ppermute | solution.py:501
  428.3 8.1 collective-permute-done.36
  439.1 11.4 %convolution_convert_fusion = bf16[2048,2048]{1,0:T(8,128)(2,1)} fusion(bf16[1024,2048]{1,0:T(8,128)(2,1)S(1)} %constant_dynamic-update-slice_fusion.18.grad_mlp, bf16[1024,2048]{1,0:T(8,128)(2,1)S(1)} %copy-done.35), kind=kOutput, calls=%fused_computation | convolution fusion | flops 8594128896 | bytes 16777216 | tf_op jit(solution)/shard_map/dot_general | solution.py:33
  450.6 18.9 %shard_map.298.right.values = bf16[1024,4096]{1,0:T(8,128)(2,1)} custom-call(bf16[1024,2048]{1,0:T(8,128)(2,1)} %copy-done.43, bf16[2048,2048]{1,0:T(8,128)(2,1)} %all-gather.8.cloned.1.call-done.weight, f32[1024,4096]{1,0:T(8,128)} %get-tuple-element.47.both), custom_call_target="tpu_custom_call" | custom-call | flops 8589934592 | bytes 33554432 | tf_op jit(solution)/shard_map/pallas_call | solution.py:426
  469.5 13.6 %shard_map.299.other = bf16[1024,4096]{1,0:T(8,128)(2,1)} custom-call(bf16[1024,1024]{1,0:T(8,128)(2,1)S(1)} %copy-done.14, bf16[1024,4096]{1,0:T(8,128)(2,1)} %shard_map.298.right.values), custom_call_target="tpu_custom_call" | custom-call | flops 8589934592 | bytes 16777216 | tf_op jit(solution)/shard_map/pallas_call | solution.py:367
  483.1 22.9 %convolution_convert_fusion.1 = bf16[1024,2048]{0,1:T(8,128)(2,1)S(1)} fusion(bf16[1024,4096]{1,0:T(8,128)(2,1)} %shard_map.300.right, bf16[2048,4096]{1,0:T(8,128)(2,1)} %all-gather.6.cloned.1.call-done.weight), kind=kOutput, calls=%fused_computation.3 | convolution fusion | flops 17181966336 | bytes 29360128 | tf_op jit(solution)/shard_map/dot_general | solution.py:33
  510.4 15.1 %shard_map.308 = bf16[1024,4096]{1,0:T(8,128)(2,1)} custom-call(bf16[1024,1024]{1,0:T(8,128)(2,1)S(1)} %copy-done.6, bf16[1024,4096]{1,0:T(8,128)(2,1)} %shard_map.300.right, bf16[1024,4096]{1,0:T(8,128)(2,1)} %collective-permute-done.56.rest_0_), custom_call_target="tpu_custom_call" | custom-call | flops 8589934592 | bytes 16777216 | tf_op jit(solution)/shard_map/pallas_call | solution.py:367
  530.8 11.2 %collective-permute-done.39 = bf16[512,512]{0,1:T(8,128)(2,1)S(1)} collective-permute-done((bf16[512,512]{0,1:T(8,128)(2,1)S(1)}, bf16[512,512]{0,1:T(8,128)(2,1)S(1)}, u32[]{:S(2)}, u32[]{:S(2)}) %collective-permute-start.39) | collective-permute-done | bytes 524320 | tf_op jit(solution)/shard_map/ppermute | solution.py:501
  544.3 8.7 %collective-permute-done.38 = bf16[512,512]{0,1:T(8,128)(2,1)S(1)} collective-permute-done((bf16[512,512]{0,1:T(8,128)(2,1)S(1)}, bf16[512,512]{0,1:T(8,128)(2,1)S(1)}, u32[]{:S(2)}, u32[]{:S(2)}) %collective-permute-start.38) | collective-permute-done | bytes 524320 | tf_op jit(solution)/shard_map/ppermute | solution.py:501
  553.0 4.2 collective-permute-done.40
  557.6 9.2 %collective-permute-done.41 = bf16[512,512]{0,1:T(8,128)(2,1)S(1)} collective-permute-done((bf16[512,512]{0,1:T(8,128)(2,1)S(1)}, bf16[512,512]{0,1:T(8,128)(2,1)S(1)}, u32[]{:S(2)}, u32[]{:S(2)}) %collective-permute-start.41) | collective-permute-done | bytes 524320 | tf_op jit(solution)/shard_map/ppermute | solution.py:501
  578.5 4.3 convolution_convert_fusion.2
  585.8 12.3 %collective-permute-done.48 = bf16[512,512]{1,0:T(8,128)(2,1)S(1)} collective-permute-done((bf16[512,512]{1,0:T(8,128)(2,1)S(1)}, bf16[512,512]{1,0:T(8,128)(2,1)S(1)}, u32[]{:S(2)}, u32[]{:S(2)}) %collective-permute-start.48) | collective-permute-done | bytes 524320 | tf_op jit(solution)/shard_map/ppermute | solution.py:501
  600.4 4.6 collective-permute-done.47
  605.0 6.3 collective-permute-done.49
  616.9 4.1 collective-permute-done.52
  622.3 16.2 %shard_map.302 = (f32[1024,512]{1,0:T(8,128)}, f32[1024,512]{1,0:T(8,128)}, bf16[1024,512]{1,0:T(8,128)(2,1)S(1)}, f32[8,512]{1,0:T(8,128)S(1)}, f32[1024,128]{1,0:T(8,128)S(1)}) custom-call(bf16[1024,512]{1,0:T(8,128)(2,1)S(1)} %copy-done.27, bf16[1024,512]{1,0:T(8,128)(2,1)S(1)} %copy-done.29, bf16[1024,512]{1,0:T(8,128)(2,1)} %copy-done.30, ...), custom_call_target="tpu_custom_call" | custom-call | flops 5368709120 | bytes 15728640 | tf_op jit(solution)/shard_map/pallas_call | solution.py:231
  646.8 6.2 shard_map.303.grad_qkv.values.other
  653.0 9.0 %shard_map.304.other = bf16[1024,2048]{1,0:T(8,128)(2,1)} custom-call(bf16[1024,1024]{1,0:T(8,128)(2,1)} %get-tuple-element.223.other.token, bf16[1024,1536]{1,0:T(8,128)(2,1)} %shard_map.303.grad_qkv.values.other, bf16[1024,1024]{1,0:T(8,128)(2,1)} %maximum_bitcast_fusion.4.other.attended, bf16[1024,512]{1,0:T(8,128)(2,1)} %shard_map.301.grad_branch), custom_call_target="tpu_custom_call" | custom-call | flops 4294967296 | bytes 6291456 | tf_op jit(solution)/shard_map/pallas_call | solution.py:311
  667.4 11.6 %shard_map.306.other = bf16[1024,2048]{1,0:T(8,128)(2,1)} custom-call(s32[1]{0:T(128)} %bitcast.24.place, bf16[1024,1536]{1,0:T(8,128)(2,1)} %shard_map.305.grad_qkv.values, bf16[2048,2048]{1,0:T(8,128)(2,1)} %all-gather.4.cloned.1.call-done.weight, f32[1024,512]{1,0:T(8,128)} %copy.150.grad_hidden), custom_call_target="tpu_custom_call" | custom-call | flops 6442450944 | bytes 16777216 | tf_op jit(solution)/shard_map/pallas_call | solution.py:335
  678.9 9.7 %shard_map.310.values = bf16[1024,2048]{1,0:T(8,128)(2,1)} custom-call(bf16[1024,1024]{1,0:T(8,128)(2,1)} %get-tuple-element.224.other.token, bf16[1024,1536]{1,0:T(8,128)(2,1)} %shard_map.309.grad_qkv, bf16[1024,1024]{1,0:T(8,128)(2,1)} %maximum_bitcast_fusion.5.other.attended, bf16[1024,512]{1,0:T(8,128)(2,1)} %shard_map.301.grad_branch, ...), custom_call_target="tpu_custom_call" | custom-call | flops 4294967296 | bytes 6291456 | tf_op jit(solution)/shard_map/pallas_call | solution.py:311
  689.7 4.1 all-to-all-start.5
  707.0 4.9 shard_map.316
  713.8 17.6 %collective-permute-done.59 = bf16[256,1024]{1,0:T(8,128)(2,1)} collective-permute-done((bf16[256,1024]{1,0:T(8,128)(2,1)}, bf16[256,1024]{1,0:T(8,128)(2,1)}, u32[]{:S(2)}, u32[]{:S(2)}) %collective-permute-start.59) | collective-permute-done | bytes 524320 | tf_op jit(solution)/shard_map/ppermute | solution.py:501
  742.4 6.4 collective-permute-done.60
  755.5 6.1 collective-permute-done.65
  780.0 10.9 %shard_map.320 = (f32[64,16384]{1,0:T(8,128)}, f32[64,16384]{1,0:T(8,128)}, f32[64,16384]{1,0:T(8,128)}, f32[64,16384]{1,0:T(8,128)}) custom-call(bf16[256,4096]{1,0:T(8,128)(2,1)S(1)} %copy-done.5, f32[64,16384]{1,0:T(8,128)S(1)} %copy-done.3, f32[64,16384]{1,0:T(8,128)S(1)} %copy-done.21, f32[64,16384]{1,0:T(8,128)} %refs_3_.6), custom_call_target="tpu_custom_call" | custom-call | flops 12582912 | bytes 31457280 | tf_op jit(solution)/shard_map/pallas_call | solution.py:104
  797.3 7.4 shard_map.322
  (430 shorter events, 249.6 us)
Async XLA Ops:
  7.2 120.8 %all-gather.4.cloned.1.call-start = ((), (), s32[]{:S(2)}) async-start(), calls=%async_computation.10 | async-start | bytes 9437184 | tf_op jit(solution)/shard_map/all_gather | solution.py:599
  28.5 251.0 %all-gather.6.cloned.1.call-start = ((), (), s32[]{:S(2)}) async-start(), calls=%async_computation.11 | async-start | bytes 18874368 | tf_op jit(solution)/shard_map/all_gather | solution.py:600
  58.8 285.0 %all-gather.8.cloned.1.call-start = ((), (), s32[]{:S(2)}) async-start(), calls=%async_computation.12 | async-start | bytes 9437184 | tf_op jit(solution)/shard_map/all_gather | solution.py:601
  75.5 38.3 %collective-permute-start = (bf16[256,2048]{0,1:T(8,128)(2,1)S(1)}, bf16[256,2048]{0,1:T(8,128)(2,1)}, u32[]{:S(2)}, u32[]{:S(2)}) collective-permute-start(bf16[256,2048]{0,1:T(8,128)(2,1)S(1)} %copy.134), channel_id=1, source_target_pairs={{0,1},{1,0},{2,3},{3,2},{4,5},{5,4},{6,7},{7,6},{8,9},{9,8},{10,11... | collective-permute-start | bytes 3145736 | tf_op jit(solution)/shard_map/ppermute | solution.py:501
  76.5 40.1 %collective-permute-start.1 = (bf16[256,2048]{0,1:T(8,128)(2,1)S(1)}, bf16[256,2048]{0,1:T(8,128)(2,1)}, u32[]{:S(2)}, u32[]{:S(2)}) collective-permute-start(bf16[256,2048]{0,1:T(8,128)(2,1)S(1)} %copy.134), channel_id=1, source_target_pairs={{0,2},{1,3},{2,0},{3,1},{4,6},{5,7},{6,4},{7,5},{8,10},{9,11},{10,... | collective-permute-start | bytes 3145736 | tf_op jit(solution)/shard_map/ppermute | solution.py:501
  77.2 19.4 %collective-permute-start.7 = (f32[256]{0:T(256)S(1)}, f32[256]{0:T(256)S(1)}, u32[]{:S(2)}, u32[]{:S(2)}) collective-permute-start(f32[256]{0:T(256)S(1)} %reshape.206), channel_id=1, source_target_pairs={{0,1},{1,0},{2,3},{3,2},{4,5},{5,4},{6,7},{7,6},{8,9},{9,8},{10,11... | collective-permute-start | bytes 3080 | tf_op jit(solution)/shard_map/ppermute | solution.py:501
  78.6 19.2 %collective-permute-start.8 = (f32[256]{0:T(256)S(1)}, f32[256]{0:T(256)S(1)}, u32[]{:S(2)}, u32[]{:S(2)}) collective-permute-start(f32[256]{0:T(256)S(1)} %reshape.206), channel_id=1, source_target_pairs={{0,2},{1,3},{2,0},{3,1},{4,6},{5,7},{6,4},{7,5},{8,10},{9,11},{10,... | collective-permute-start | bytes 3080 | tf_op jit(solution)/shard_map/ppermute | solution.py:501
  79.7 18.7 %collective-permute-start.9 = (f32[256]{0:T(256)S(1)}, f32[256]{0:T(256)S(1)}, u32[]{:S(2)}, u32[]{:S(2)}) collective-permute-start(f32[256]{0:T(256)S(1)} %reshape.206), channel_id=1, source_target_pairs={{0,3},{1,2},{2,1},{3,0},{4,7},{5,6},{6,5},{7,4},{8,11},{9,10},{10,... | collective-permute-start | bytes 3080 | tf_op jit(solution)/shard_map/ppermute | solution.py:501
  168.0 19.9 %collective-permute-start.17 = (bf16[1024,512]{0,1:T(8,128)(2,1)S(1)}, bf16[1024,512]{0,1:T(8,128)(2,1)S(1)}, u32[]{:S(2)}, u32[]{:S(2)}) collective-permute-start(bf16[1024,512]{0,1:T(8,128)(2,1)S(1)} %copy.140), channel_id=1, source_target_pairs={{0,1},{1,0},{2,3},{3,2},{4,5},{5,4},{6,7},{7,6},{8,9},{9,8},{10,11... | collective-permute-start | bytes 3145736 | tf_op jit(solution)/shard_map/ppermute | solution.py:501
  169.3 27.1 %collective-permute-start.18 = (bf16[1024,512]{0,1:T(8,128)(2,1)S(1)}, bf16[1024,512]{0,1:T(8,128)(2,1)}, u32[]{:S(2)}, u32[]{:S(2)}) collective-permute-start(bf16[1024,512]{0,1:T(8,128)(2,1)S(1)} %copy.140), channel_id=1, source_target_pairs={{0,2},{1,3},{2,0},{3,1},{4,6},{5,7},{6,4},{7,5},{8,10},{9,11},{10,... | collective-permute-start | bytes 3145736 | tf_op jit(solution)/shard_map/ppermute | solution.py:501
  189.7 18.5 %collective-permute-start.19 = (bf16[512,512]{0,1:T(8,128)(2,1)}, bf16[512,512]{0,1:T(8,128)(2,1)}, u32[]{:S(2)}, u32[]{:S(2)}) collective-permute-start(bf16[512,512]{0,1:T(8,128)(2,1)} %slice.93), channel_id=1, source_target_pairs={{0,2},{1,3},{2,0},{3,1},{4,6},{5,7},{6,4},{7,5},{8,10},{9,11},{10,... | collective-permute-start | bytes 1572872 | tf_op jit(solution)/shard_map/ppermute | solution.py:501
  191.8 42.7 %all-to-all-start.1 = ((bf16[4,256,512]{1,2,0:T(8,128)(2,1)}), bf16[4,256,512]{1,2,0:T(8,128)(2,1)}, u32[]{:S(2)}, u32[]{:S(2)}) async-start(bf16[4,256,512]{1,2,0:T(8,128)(2,1)} %bitcast.86), calls=%async_computation.1 | async-start | bytes 2097152 | tf_op jit(solution)/shard_map/all_to_all | solution.py:612
  196.1 382.5 %reduce-scatter.4.cloned.1.call-start = ((), (), s32[]{:S(2)}) async-start(), calls=%async_computation.13 | async-start | bytes 9437184 | tf_op jit(solution)/shard_map/reduce_scatter | solution.py:693
  197.5 17.2 %collective-permute-start.20 = (bf16[512,512]{0,1:T(8,128)(2,1)S(1)}, bf16[512,512]{0,1:T(8,128)(2,1)S(1)}, u32[]{:S(2)}, u32[]{:S(2)}) collective-permute-start(bf16[512,512]{0,1:T(8,128)(2,1)S(1)} %slice.94), channel_id=1, source_target_pairs={{0,1},{1,0},{2,3},{3,2},{4,5},{5,4},{6,7},{7,6},{8,9},{9,8},{10,11... | collective-permute-start | bytes 1572872 | tf_op jit(solution)/shard_map/ppermute | solution.py:501
  232.4 19.1 %collective-permute-start.24 = (bf16[1024,512]{0,1:T(8,128)(2,1)}, bf16[1024,512]{0,1:T(8,128)(2,1)}, u32[]{:S(2)}, u32[]{:S(2)}) collective-permute-start(bf16[1024,512]{0,1:T(8,128)(2,1)} %get-tuple-element.153), channel_id=1, source_target_pairs={{0,1},{1,0},{2,3},{3,2},{4,5},{5,4},{6,7},{7,6},{8,9},{9,8},{10,11... | collective-permute-start | bytes 3145736 | tf_op jit(solution)/shard_map/ppermute | solution.py:501
  234.0 21.8 %collective-permute-start.25 = (bf16[1024,512]{0,1:T(8,128)(2,1)}, bf16[1024,512]{0,1:T(8,128)(2,1)}, u32[]{:S(2)}, u32[]{:S(2)}) collective-permute-start(bf16[1024,512]{0,1:T(8,128)(2,1)} %get-tuple-element.153), channel_id=1, source_target_pairs={{0,2},{1,3},{2,0},{3,1},{4,6},{5,7},{6,4},{7,5},{8,10},{9,11},{10,... | collective-permute-start | bytes 3145736 | tf_op jit(solution)/shard_map/ppermute | solution.py:501
  356.9 14.8 %collective-permute-start.29 = (bf16[256,1024]{1,0:T(8,128)(2,1)S(1)}, bf16[256,1024]{1,0:T(8,128)(2,1)S(1)}, u32[]{:S(2)}, u32[]{:S(2)}) collective-permute-start(bf16[256,1024]{1,0:T(8,128)(2,1)S(1)} %get-tuple-element.177), channel_id=1, source_target_pairs={{0,1},{1,0},{2,3},{3,2},{4,5},{5,4},{6,7},{7,6},{8,9},{9,8},{10,11... | collective-permute-start | bytes 1572872 | tf_op jit(solution)/shard_map/ppermute | solution.py:501
  358.4 23.8 %collective-permute-start.28 = (bf16[256,1024]{1,0:T(8,128)(2,1)S(1)}, bf16[256,1024]{1,0:T(8,128)(2,1)S(1)}, u32[]{:S(2)}, u32[]{:S(2)}) collective-permute-start(bf16[256,1024]{1,0:T(8,128)(2,1)S(1)} %get-tuple-element.174), channel_id=1, source_target_pairs={{0,1},{1,0},{2,3},{3,2},{4,5},{5,4},{6,7},{7,6},{8,9},{9,8},{10,11... | collective-permute-start | bytes 1572872 | tf_op jit(solution)/shard_map/ppermute | solution.py:501
  359.0 23.3 %collective-permute-start.32 = (bf16[256,1024]{1,0:T(8,128)(2,1)S(1)}, bf16[256,1024]{1,0:T(8,128)(2,1)S(1)}, u32[]{:S(2)}, u32[]{:S(2)}) collective-permute-start(bf16[256,1024]{1,0:T(8,128)(2,1)S(1)} %get-tuple-element.175), channel_id=1, source_target_pairs={{0,2},{1,3},{2,0},{3,1},{4,6},{5,7},{6,4},{7,5},{8,10},{9,11},{10,... | collective-permute-start | bytes 1572872 | tf_op jit(solution)/shard_map/ppermute | solution.py:501
  371.9 14.9 %collective-permute-start.30 = (bf16[256,1024]{1,0:T(8,128)(2,1)S(1)}, bf16[256,1024]{1,0:T(8,128)(2,1)S(1)}, u32[]{:S(2)}, u32[]{:S(2)}) collective-permute-start(bf16[256,1024]{1,0:T(8,128)(2,1)S(1)} %add_convert_fusion.11), channel_id=1, source_target_pairs={{0,2},{1,3},{2,0},{3,1},{4,6},{5,7},{6,4},{7,5},{8,10},{9,11},{10,... | collective-permute-start | bytes 1572872 | tf_op jit(solution)/shard_map/ppermute | solution.py:501
  373.5 22.3 %collective-permute-start.31 = (bf16[256,1024]{1,0:T(8,128)(2,1)S(1)}, bf16[256,1024]{1,0:T(8,128)(2,1)S(1)}, u32[]{:S(2)}, u32[]{:S(2)}) collective-permute-start(bf16[256,1024]{1,0:T(8,128)(2,1)S(1)} %get-tuple-element.176), channel_id=1, source_target_pairs={{0,2},{1,3},{2,0},{3,1},{4,6},{5,7},{6,4},{7,5},{8,10},{9,11},{10,... | collective-permute-start | bytes 1572872 | tf_op jit(solution)/shard_map/ppermute | solution.py:501
  401.9 22.0 %collective-permute-start.34 = (bf16[256,2048]{1,0:T(8,128)(2,1)S(1)}, bf16[256,2048]{1,0:T(8,128)(2,1)S(1)}, u32[]{:S(2)}, u32[]{:S(2)}) collective-permute-start(bf16[256,2048]{1,0:T(8,128)(2,1)S(1)} %get-tuple-element.151), channel_id=1, source_target_pairs={{0,1},{1,0},{2,3},{3,2},{4,5},{5,4},{6,7},{7,6},{8,9},{9,8},{10,11... | collective-permute-start | bytes 3145736 | tf_op jit(solution)/shard_map/ppermute | solution.py:501
  403.5 24.2 %collective-permute-start.35 = (bf16[256,2048]{1,0:T(8,128)(2,1)S(1)}, bf16[256,2048]{1,0:T(8,128)(2,1)S(1)}, u32[]{:S(2)}, u32[]{:S(2)}) collective-permute-start(bf16[256,2048]{1,0:T(8,128)(2,1)S(1)} %get-tuple-element.151), channel_id=1, source_target_pairs={{0,2},{1,3},{2,0},{3,1},{4,6},{5,7},{6,4},{7,5},{8,10},{9,11},{10,... | collective-permute-start | bytes 3145736 | tf_op jit(solution)/shard_map/ppermute | solution.py:501
  424.0 12.4 %collective-permute-start.36 = (bf16[256,1024]{1,0:T(8,128)(2,1)S(1)}, bf16[256,1024]{1,0:T(8,128)(2,1)S(1)}, u32[]{:S(2)}, u32[]{:S(2)}) collective-permute-start(bf16[256,1024]{1,0:T(8,128)(2,1)S(1)} %slice.99), channel_id=1, source_target_pairs={{0,2},{1,3},{2,0},{3,1},{4,6},{5,7},{6,4},{7,5},{8,10},{9,11},{10,... | collective-permute-start | bytes 1572872 | tf_op jit(solution)/shard_map/ppermute | solution.py:501
  450.5 239.1 %reduce-scatter.6.cloned.1.call-start = ((), (), s32[]{:S(2)}) async-start(), calls=%async_computation.14 | async-start | bytes 10485760 | tf_op jit(solution)/shard_map/reduce_scatter | solution.py:702
  483.1 25.7 %collective-permute-start.56 = (bf16[1024,4096]{1,0:T(8,128)(2,1)}, bf16[1024,4096]{1,0:T(8,128)(2,1)}, u32[]{:S(2)}, u32[]{:S(2)}) collective-permute-start(bf16[1024,4096]{1,0:T(8,128)(2,1)} %shard_map.299.other), channel_id=1, source_target_pairs={{0,4},{4,0},{1,5},{5,1},{2,6},{6,2},{3,7},{7,3},{8,12},{12,8},{9,1... | collective-permute-start | bytes 25165832 | tf_op jit(solution)/shard_map/ppermute | solution.py:471
  527.3 14.8 %collective-permute-start.39 = (bf16[512,512]{0,1:T(8,128)(2,1)S(1)}, bf16[512,512]{0,1:T(8,128)(2,1)S(1)}, u32[]{:S(2)}, u32[]{:S(2)}) collective-permute-start(bf16[512,512]{0,1:T(8,128)(2,1)S(1)} %get-tuple-element.171), channel_id=1, source_target_pairs={{0,1},{1,0},{2,3},{3,2},{4,5},{5,4},{6,7},{7,6},{8,9},{9,8},{10,11... | collective-permute-start | bytes 1572872 | tf_op jit(solution)/shard_map/ppermute | solution.py:501
  527.4 25.6 %collective-permute-start.38 = (bf16[512,512]{0,1:T(8,128)(2,1)S(1)}, bf16[512,512]{0,1:T(8,128)(2,1)S(1)}, u32[]{:S(2)}, u32[]{:S(2)}) collective-permute-start(bf16[512,512]{0,1:T(8,128)(2,1)S(1)} %get-tuple-element.168), channel_id=1, source_target_pairs={{0,1},{1,0},{2,3},{3,2},{4,5},{5,4},{6,7},{7,6},{8,9},{9,8},{10,11... | collective-permute-start | bytes 1572872 | tf_op jit(solution)/shard_map/ppermute | solution.py:501
  529.4 23.6 %collective-permute-start.42 = (bf16[512,512]{0,1:T(8,128)(2,1)S(1)}, bf16[512,512]{0,1:T(8,128)(2,1)S(1)}, u32[]{:S(2)}, u32[]{:S(2)}) collective-permute-start(bf16[512,512]{0,1:T(8,128)(2,1)S(1)} %get-tuple-element.169), channel_id=1, source_target_pairs={{0,2},{1,3},{2,0},{3,1},{4,6},{5,7},{6,4},{7,5},{8,10},{9,11},{10,... | collective-permute-start | bytes 1572872 | tf_op jit(solution)/shard_map/ppermute | solution.py:501
  542.3 14.9 %collective-permute-start.40 = (bf16[512,512]{0,1:T(8,128)(2,1)S(1)}, bf16[512,512]{0,1:T(8,128)(2,1)S(1)}, u32[]{:S(2)}, u32[]{:S(2)}) collective-permute-start(bf16[512,512]{0,1:T(8,128)(2,1)S(1)} %add_convert_fusion.9), channel_id=1, source_target_pairs={{0,2},{1,3},{2,0},{3,1},{4,6},{5,7},{6,4},{7,5},{8,10},{9,11},{10,... | collective-permute-start | bytes 1572872 | tf_op jit(solution)/shard_map/ppermute | solution.py:501
  543.7 23.2 %collective-permute-start.41 = (bf16[512,512]{0,1:T(8,128)(2,1)S(1)}, bf16[512,512]{0,1:T(8,128)(2,1)S(1)}, u32[]{:S(2)}, u32[]{:S(2)}) collective-permute-start(bf16[512,512]{0,1:T(8,128)(2,1)S(1)} %get-tuple-element.170), channel_id=1, source_target_pairs={{0,2},{1,3},{2,0},{3,1},{4,6},{5,7},{6,4},{7,5},{8,10},{9,11},{10,... | collective-permute-start | bytes 1572872 | tf_op jit(solution)/shard_map/ppermute | solution.py:501
  583.2 14.9 %collective-permute-start.48 = (bf16[512,512]{1,0:T(8,128)(2,1)S(1)}, bf16[512,512]{1,0:T(8,128)(2,1)S(1)}, u32[]{:S(2)}, u32[]{:S(2)}) collective-permute-start(bf16[512,512]{1,0:T(8,128)(2,1)S(1)} %get-tuple-element.165), channel_id=1, source_target_pairs={{0,1},{1,0},{2,3},{3,2},{4,5},{5,4},{6,7},{7,6},{8,9},{9,8},{10,11... | collective-permute-start | bytes 1572872 | tf_op jit(solution)/shard_map/ppermute | solution.py:501
  584.3 20.6 %collective-permute-start.47 = (bf16[512,512]{1,0:T(8,128)(2,1)S(1)}, bf16[512,512]{1,0:T(8,128)(2,1)S(1)}, u32[]{:S(2)}, u32[]{:S(2)}) collective-permute-start(bf16[512,512]{1,0:T(8,128)(2,1)S(1)} %get-tuple-element.162), channel_id=1, source_target_pairs={{0,1},{1,0},{2,3},{3,2},{4,5},{5,4},{6,7},{7,6},{8,9},{9,8},{10,11... | collective-permute-start | bytes 1572872 | tf_op jit(solution)/shard_map/ppermute | solution.py:501
  585.2 19.7 %collective-permute-start.51 = (bf16[512,512]{1,0:T(8,128)(2,1)S(1)}, bf16[512,512]{1,0:T(8,128)(2,1)S(1)}, u32[]{:S(2)}, u32[]{:S(2)}) collective-permute-start(bf16[512,512]{1,0:T(8,128)(2,1)S(1)} %get-tuple-element.163), channel_id=1, source_target_pairs={{0,2},{1,3},{2,0},{3,1},{4,6},{5,7},{6,4},{7,5},{8,10},{9,11},{10,... | collective-permute-start | bytes 1572872 | tf_op jit(solution)/shard_map/ppermute | solution.py:501
  598.3 13.0 %collective-permute-start.49 = (bf16[512,512]{1,0:T(8,128)(2,1)S(1)}, bf16[512,512]{1,0:T(8,128)(2,1)S(1)}, u32[]{:S(2)}, u32[]{:S(2)}) collective-permute-start(bf16[512,512]{1,0:T(8,128)(2,1)S(1)} %add_convert_fusion.7), channel_id=1, source_target_pairs={{0,2},{1,3},{2,0},{3,1},{4,6},{5,7},{6,4},{7,5},{8,10},{9,11},{10,... | collective-permute-start | bytes 1572872 | tf_op jit(solution)/shard_map/ppermute | solution.py:501
  598.9 18.0 %collective-permute-start.50 = (bf16[512,512]{1,0:T(8,128)(2,1)S(1)}, bf16[512,512]{1,0:T(8,128)(2,1)S(1)}, u32[]{:S(2)}, u32[]{:S(2)}) collective-permute-start(bf16[512,512]{1,0:T(8,128)(2,1)S(1)} %get-tuple-element.164), channel_id=1, source_target_pairs={{0,2},{1,3},{2,0},{3,1},{4,6},{5,7},{6,4},{7,5},{8,10},{9,11},{10,... | collective-permute-start | bytes 1572872 | tf_op jit(solution)/shard_map/ppermute | solution.py:501
  661.9 17.0 %collective-permute-start.57 = (bf16[1024,2048]{1,0:T(8,128)(2,1)}, bf16[1024,2048]{1,0:T(8,128)(2,1)}, u32[]{:S(2)}, u32[]{:S(2)}) collective-permute-start(bf16[1024,2048]{1,0:T(8,128)(2,1)} %shard_map.304.other), channel_id=1, source_target_pairs={{0,4},{4,0},{1,5},{5,1},{2,6},{6,2},{3,7},{7,3},{8,12},{12,8},{9,1... | collective-permute-start | bytes 12582920 | tf_op jit(solution)/shard_map/ppermute | solution.py:471
  663.8 24.9 %all-to-all-start.4 = ((bf16[4,64,2048]{2,1,0:T(8,128)(2,1)}), bf16[4,64,2048]{2,1,0:T(8,128)(2,1)S(1)}, u32[]{:S(2)}, u32[]{:S(2)}) async-start(bf16[4,64,2048]{2,1,0:T(8,128)(2,1)} %bitcast.26), calls=%async_computation.6 | async-start | bytes 2097152 | tf_op jit(solution)/shard_map/all_to_all | solution.py:690
  667.3 100.1 %reduce-scatter.8.cloned.1.call-start = ((), (), s32[]{:S(2)}) async-start(), calls=%async_computation.15 | async-start | bytes 5242880 | tf_op jit(solution)/shard_map/reduce_scatter | solution.py:733
  689.7 47.2 %all-to-all-start.5 = ((bf16[4,64,4096]{2,1,0:T(8,128)(2,1)}), bf16[4,64,4096]{2,1,0:T(8,128)(2,1)S(1)}, u32[]{:S(2)}, u32[]{:S(2)}) async-start(bf16[4,64,4096]{2,1,0:T(8,128)(2,1)} %bitcast.81), calls=%async_computation.7 | async-start | bytes 4194304 | tf_op jit(solution)/shard_map/all_to_all | solution.py:690
  697.0 34.4 %collective-permute-start.59 = (bf16[256,1024]{1,0:T(8,128)(2,1)}, bf16[256,1024]{1,0:T(8,128)(2,1)}, u32[]{:S(2)}, u32[]{:S(2)}) collective-permute-start(bf16[256,1024]{1,0:T(8,128)(2,1)} %get-tuple-element.159), channel_id=1, source_target_pairs={{0,1},{1,0},{2,3},{3,2},{4,5},{5,4},{6,7},{7,6},{8,9},{9,8},{10,11... | collective-permute-start | bytes 1572872 | tf_op jit(solution)/shard_map/ppermute | solution.py:501
  699.0 42.6 %collective-permute-start.58 = (bf16[256,1024]{1,0:T(8,128)(2,1)}, bf16[256,1024]{1,0:T(8,128)(2,1)S(1)}, u32[]{:S(2)}, u32[]{:S(2)}) collective-permute-start(bf16[256,1024]{1,0:T(8,128)(2,1)} %get-tuple-element.156), channel_id=1, source_target_pairs={{0,1},{1,0},{2,3},{3,2},{4,5},{5,4},{6,7},{7,6},{8,9},{9,8},{10,11... | collective-permute-start | bytes 1572872 | tf_op jit(solution)/shard_map/ppermute | solution.py:501
  699.1 42.6 %collective-permute-start.69 = (bf16[256,1024]{1,0:T(8,128)(2,1)S(1)}, bf16[256,1024]{1,0:T(8,128)(2,1)}, u32[]{:S(2)}, u32[]{:S(2)}) collective-permute-start(bf16[256,1024]{1,0:T(8,128)(2,1)S(1)} %get-tuple-element.157), channel_id=1, source_target_pairs={{0,2},{1,3},{2,0},{3,1},{4,6},{5,7},{6,4},{7,5},{8,10},{9,11},{10,... | collective-permute-start | bytes 1572872 | tf_op jit(solution)/shard_map/ppermute | solution.py:501
  733.6 15.2 %collective-permute-start.60 = (bf16[256,1024]{1,0:T(8,128)(2,1)}, bf16[256,1024]{1,0:T(8,128)(2,1)}, u32[]{:S(2)}, u32[]{:S(2)}) collective-permute-start(bf16[256,1024]{1,0:T(8,128)(2,1)} %add_convert_fusion.3), channel_id=1, source_target_pairs={{0,2},{1,3},{2,0},{3,1},{4,6},{5,7},{6,4},{7,5},{8,10},{9,11},{10,... | collective-permute-start | bytes 1572872 | tf_op jit(solution)/shard_map/ppermute | solution.py:501
  735.7 28.5 %collective-permute-start.68 = (bf16[256,1024]{1,0:T(8,128)(2,1)}, bf16[256,1024]{1,0:T(8,128)(2,1)}, u32[]{:S(2)}, u32[]{:S(2)}) collective-permute-start(bf16[256,1024]{1,0:T(8,128)(2,1)} %get-tuple-element.158), channel_id=1, source_target_pairs={{0,2},{1,3},{2,0},{3,1},{4,6},{5,7},{6,4},{7,5},{8,10},{9,11},{10,... | collective-permute-start | bytes 1572872 | tf_op jit(solution)/shard_map/ppermute | solution.py:501
  736.9 14.9 %collective-permute-start.62 = (f32[8192]{0:T(1024)S(1)}, f32[8192]{0:T(1024)S(1)}, u32[]{:S(2)}, u32[]{:S(2)}) collective-permute-start(f32[8192]{0:T(1024)S(1)} %add.450), channel_id=1, source_target_pairs={{0,8},{8,16},{16,24},{24,0},{1,9},{9,17},{17,25},{25,1},{2,10},{10... | collective-permute-start | bytes 98312 | tf_op jit(solution)/shard_map/ppermute | solution.py:475
  751.9 12.4 %collective-permute-start.70 = (bf16[256,1024]{1,0:T(8,128)(2,1)}, bf16[256,1024]{1,0:T(8,128)(2,1)}, u32[]{:S(2)}, u32[]{:S(2)}) collective-permute-start(bf16[256,1024]{1,0:T(8,128)(2,1)} %get-tuple-element.155), channel_id=1, source_target_pairs={{0,1},{1,0},{2,3},{3,2},{4,5},{5,4},{6,7},{7,6},{8,9},{9,8},{10,11... | collective-permute-start | bytes 1572872 | tf_op jit(solution)/shard_map/ppermute | solution.py:501
  767.4 23.6 %all-to-all-start.6 = ((bf16[4,64,2048]{2,1,0:T(8,128)(2,1)}), bf16[4,64,2048]{2,1,0:T(8,128)(2,1)S(1)}, u32[]{:S(2)}, u32[]{:S(2)}) async-start(bf16[4,64,2048]{2,1,0:T(8,128)(2,1)} %bitcast.82), calls=%async_computation.9 | async-start | bytes 2097152 | tf_op jit(solution)/shard_map/all_to_all | solution.py:690
  (96 other events, 1495.1 us)
Sparse Core Ops, SparseCore 0:
  28.6 82.0 all-gather.3
  112.3 149.6 all-gather.5
  263.5 80.2 all-gather.7
  450.7 87.1 reduce-scatter.3
  540.1 142.8 reduce-scatter.5
  689.8 77.4 reduce-scatter.7

commit v5 on v4

--- a/solution.py
+++ b/solution.py
@@ -387,14 +387,16 @@
     sigmoid = jax.nn.sigmoid(gate)
     silu = gate * sigmoid
     activ[...] = (silu * up).astype(bf16)
-    both[:, :TILE] = up * sigmoid * (1.0 + gate * (1.0 - sigmoid))
-    both[:, TILE:] = silu
+    both[:, :TILE] = (up * sigmoid * (1.0 + gate * (1.0 - sigmoid))).astype(bf16)
+    both[:, TILE:] = silu.astype(bf16)
 
 
 def gate_up_back_body(grad_mlp, weight, both, out):
     grad = dot(grad_mlp[...], weight[...], 1, 0)
     for start in (0, TILE):
-        out[:, start : start + TILE] = (grad * both[:, start : start + TILE]).astype(bf16)
+        out[:, start : start + TILE] = (
+            grad * both[:, start : start + TILE].astype(f32)
+        ).astype(bf16)
 
 
 def gate_up_kernels(length, width, wide):
@@ -411,7 +413,7 @@
             in_specs=[rows_spec, columns(width, 2 * TILE)],
             out_specs=[columns(length, 2 * TILE), columns(length, TILE)],
             out_shape=[
-                jax.ShapeDtypeStruct((length, 2 * wide), f32),
+                jax.ShapeDtypeStruct((length, 2 * wide), bf16),
                 jax.ShapeDtypeStruct((length, wide), bf16),
             ],
             compiler_params=params,

time: 819 us -> 817 us (level)
  transfers between devices with their start and end apart: 81 -> 81, of which waited for: 48 -> 49; matrix products, arithmetic and copies ran while one was open for 17% -> 17% of each run, Pallas kernels for 20% -> 19%
where the time goes in v5:
time: 817 us; the launch traced here: 810 us
  waiting for transfers between devices  271 us (33%)
  Pallas kernels  165 us (20%)
  local copies, waits for them, and re-layouts  104 us (13%)
  starting transfers between devices  90.2 us (11%)
  matrix products  67.5 us (8%)
  blocking collectives  61.4 us (8%)
  other arithmetic  33 us (4%)
  between operations  17.6 us (2%)
    ppermute x61, waiting for transfers between devices, swap(): return lax.ppermute(values, FSDP, [(i, i ^ bit) for i in range(self.count)])  230 us
    dot_general x6, matrix products, mm(): lax.dot_general(left, right, (dims, ((), ())), preferred_element_type=f32)  67.5 us
    ppermute x61, starting transfers between devices, swap(): return lax.ppermute(values, FSDP, [(i, i ^ bit) for i in range(self.count)])  67.2 us
    all_to_all x3, blocking collectives, spread(): return lax.all_to_all(block, FSDP, 0, 0, tiled=True)  61.4 us
    unnamed x135, local copies, waits for them, and re-layouts  42.1 us
    all_gather x1, waiting for transfers between devices, per_device(): down_all = lax.all_gather(spread(w_down, 1), DP, axis=0, tiled=True)  38.4 us
    pallas_call x2, Pallas kernels, half_grad(): pl.pallas_call(half_grad_body, grid=(columns // size,), in_specs=[pl.Bloc...  28.7 us
    dynamic_update_slice x19, local copies, waits for them, and re-layouts, gather(): out = lax.dynamic_update_slice(out, part, start)  24.4 us
  transfers between devices with their start and end apart: 81, of which 49 were waited for; matrix products, arithmetic and copies ran while one was open for 17% of the time, Pallas kernels for 19%

profile of v5, /device:TPU:0, one launch (start us, length us, event | category | flops | bytes accessed | tf_op | source)
XLA Modules:
  0.0 810.2 jit_solution(6905979059428287493)
XLA Ops:
  9.2 19.2 %all_to_all.75 = bf16[4,64,2048]{2,1,0:T(8,128)(2,1)} all-to-all(bf16[4,64,2048]{2,1,0:T(8,128)(2,1)S(1)} %bitcast.77), channel_id=1, replica_groups=mesh['z'=4,'core'=2,'y'=2,'x'=2] {'y','x'}, dimensions={0} | all-to-all | bytes 2097152 | tf_op jit(solution)/shard_map/all_to_all | solution.py:599
  31.3 27.5 %all_to_all.76 = bf16[4,64,4096]{2,1,0:T(8,128)(2,1)} all-to-all(bf16[4,64,4096]{2,1,0:T(8,128)(2,1)S(1)} %bitcast.76), channel_id=1, replica_groups=mesh['z'=4,'core'=2,'y'=2,'x'=2] {'y','x'}, dimensions={0} | all-to-all | bytes 4194304 | tf_op jit(solution)/shard_map/all_to_all | solution.py:599
  59.2 14.7 %all_to_all.77 = bf16[4,64,2048]{2,1,0:T(8,128)(2,1)} all-to-all(bf16[4,64,2048]{2,1,0:T(8,128)(2,1)S(1)} %bitcast.78), channel_id=1, replica_groups=mesh['z'=4,'core'=2,'y'=2,'x'=2] {'y','x'}, dimensions={0} | all-to-all | bytes 2097152 | tf_op jit(solution)/shard_map/all_to_all | solution.py:599
  84.2 12.3 %collective-permute-done.7 = f32[256]{0:T(256)S(1)} collective-permute-done((f32[256]{0:T(256)S(1)}, f32[256]{0:T(256)S(1)}, u32[]{:S(2)}, u32[]{:S(2)}) %collective-permute-start.7) | collective-permute-done | bytes 1056 | tf_op jit(solution)/shard_map/ppermute | solution.py:503
  128.0 10.6 %fusion.refs_0_.refs_1_.refs_2_.refs_6_.refs_7_.raw = f32[1024,1536]{1,0:T(8,128)S(1)} fusion(bf16[1024,2048]{0,1:T(8,128)(2,1)} %constant_dynamic-update-slice_fusion.19, bf16[2048,2048]{1,0:T(8,128)(2,1)} %all-gather.4.cloned.1.call-done.weight), kind=kOutput, calls=%fused_computation.1 | convolution fusion | flops 6442450944 | bytes 16777216 | tf_op jit(solution)/shard_map/dot_general | solution.py:33
  145.8 17.7 %shard_map.287 = (bf16[1024,512]{1,0:T(8,128)(2,1)S(1)}, bf16[1024,512]{1,0:T(8,128)(2,1)S(1)}, bf16[1024,512]{1,0:T(8,128)(2,1)S(1)}, bf16[1024,512]{1,0:T(8,128)(2,1)}, f32[4,1024,1]{2,1,0:T(8,128)}) custom-call(f32[1024,1536]{1,0:T(8,128)} %copy-done.36, f32[1024,1536]{1,0:T(8,128)} %copy-done.36, f32[1024,1536]{1,0:T(8,128)} %copy-done.36, ...), custom_call_target="tpu_custom_call" | custom-call | flops 2147483648 | bytes 10485760 | tf_op jit(solution)/shard_map/pallas_call | solution.py:218
  170.2 17.7 %collective-permute-done.17 = bf16[1024,512]{0,1:T(8,128)(2,1)S(1)} collective-permute-done((bf16[1024,512]{0,1:T(8,128)(2,1)S(1)}, bf16[1024,512]{0,1:T(8,128)(2,1)S(1)}, u32[]{:S(2)}, u32[]{:S(2)}) %collective-permute-start.17) | collective-permute-done | bytes 1048608 | tf_op jit(solution)/shard_map/ppermute | solution.py:503
  191.7 4.3 all-to-all-start.1
  201.6 6.6 collective-permute-done.19
  209.3 5.1 collective-permute-done.20
  214.6 5.5 multiply_reduce_fusion.3
  245.0 6.4 collective-permute-done.24
  266.8 6.7 copy.143.values
  279.3 24.1 %shard_map.296 = (bf16[1024,4096]{1,0:T(8,128)(2,1)}, bf16[1024,2048]{1,0:T(8,128)(2,1)S(1)}) custom-call(bf16[1024,2048]{1,0:T(8,128)(2,1)} %shard_map.294.hidden, bf16[2048,4096]{1,0:T(8,128)(2,1)} %all-gather.6.cloned.1.call-done.weight), custom_call_target="tpu_custom_call" | custom-call | flops 17179869184 | bytes 37748736 | tf_op jit(solution)/shard_map/pallas_call | solution.py:410
  305.4 38.4 %all-gather.8.cloned.1.call-done.weight = bf16[2048,2048]{1,0:T(8,128)(2,1)} async-done(((bf16[256,2048]{1,0:T(8,128)(2,1)}), bf16[2048,2048]{1,0:T(8,128)(2,1)}) %all-gather.8.cloned.1.call-update) | async-done | bytes 8388624 | tf_op jit(solution)/shard_map/all_gather | solution.py:603
  343.9 12.8 %convolution_convert_fusion.3 = bf16[1024,2048]{1,0:T(8,128)(2,1)S(1)} fusion(bf16[1024,2048]{1,0:T(8,128)(2,1)} %copy-done.34, bf16[2048,2048]{1,0:T(8,128)(2,1)} %all-gather.8.cloned.1.call-done.weight), kind=kOutput, calls=%fused_computation.5 | convolution fusion | flops 8592031744 | bytes 16777216 | tf_op jit(solution)/shard_map/dot_general | solution.py:33
  360.5 11.2 %collective-permute-done.29 = bf16[256,1024]{1,0:T(8,128)(2,1)S(1)} collective-permute-done((bf16[256,1024]{1,0:T(8,128)(2,1)S(1)}, bf16[256,1024]{1,0:T(8,128)(2,1)S(1)}, u32[]{:S(2)}, u32[]{:S(2)}) %collective-permute-start.29) | collective-permute-done | bytes 524320 | tf_op jit(solution)/shard_map/ppermute | solution.py:503
  374.0 8.2 %collective-permute-done.28 = bf16[256,1024]{1,0:T(8,128)(2,1)S(1)} collective-permute-done((bf16[256,1024]{1,0:T(8,128)(2,1)S(1)}, bf16[256,1024]{1,0:T(8,128)(2,1)S(1)}, u32[]{:S(2)}, u32[]{:S(2)}) %collective-permute-start.28) | collective-permute-done | bytes 524320 | tf_op jit(solution)/shard_map/ppermute | solution.py:503
  382.2 4.6 collective-permute-done.30
  388.9 6.9 collective-permute-done.31
  405.0 18.9 %collective-permute-done.34 = bf16[256,2048]{1,0:T(8,128)(2,1)S(1)} collective-permute-done((bf16[256,2048]{1,0:T(8,128)(2,1)S(1)}, bf16[256,2048]{1,0:T(8,128)(2,1)S(1)}, u32[]{:S(2)}, u32[]{:S(2)}) %collective-permute-start.34) | collective-permute-done | bytes 1048608 | tf_op jit(solution)/shard_map/ppermute | solution.py:503
  428.3 8.1 %collective-permute-done.36 = bf16[256,1024]{1,0:T(8,128)(2,1)S(1)} collective-permute-done((bf16[256,1024]{1,0:T(8,128)(2,1)S(1)}, bf16[256,1024]{1,0:T(8,128)(2,1)S(1)}, u32[]{:S(2)}, u32[]{:S(2)}) %collective-permute-start.36) | collective-permute-done | bytes 524320 | tf_op jit(solution)/shard_map/ppermute | solution.py:503
  439.1 11.4 %convolution_convert_fusion = bf16[2048,2048]{1,0:T(8,128)(2,1)} fusion(bf16[1024,2048]{1,0:T(8,128)(2,1)S(1)} %constant_dynamic-update-slice_fusion.18.grad_mlp, bf16[1024,2048]{1,0:T(8,128)(2,1)S(1)} %copy-done.35), kind=kOutput, calls=%fused_computation | convolution fusion | flops 8594128896 | bytes 16777216 | tf_op jit(solution)/shard_map/dot_general | solution.py:33
  450.6 17.3 %shard_map.298.right.values = bf16[1024,4096]{1,0:T(8,128)(2,1)} custom-call(bf16[1024,2048]{1,0:T(8,128)(2,1)} %copy-done.49, bf16[2048,2048]{1,0:T(8,128)(2,1)} %all-gather.8.cloned.1.call-done.weight, bf16[1024,4096]{1,0:T(8,128)(2,1)} %get-tuple-element.47.both), custom_call_target="tpu_custom_call" | custom-call | flops 8589934592 | bytes 33554432 | tf_op jit(solution)/shard_map/pallas_call | solution.py:428
  467.9 13.6 %shard_map.299.other = bf16[1024,4096]{1,0:T(8,128)(2,1)} custom-call(bf16[1024,1024]{1,0:T(8,128)(2,1)S(1)} %copy-done.14, bf16[1024,4096]{1,0:T(8,128)(2,1)} %shard_map.298.right.values), custom_call_target="tpu_custom_call" | custom-call | flops 8589934592 | bytes 16777216 | tf_op jit(solution)/shard_map/pallas_call | solution.py:367
  481.5 22.9 %convolution_convert_fusion.1 = bf16[1024,2048]{0,1:T(8,128)(2,1)S(1)} fusion(bf16[1024,4096]{1,0:T(8,128)(2,1)} %shard_map.300.right, bf16[2048,4096]{1,0:T(8,128)(2,1)} %all-gather.6.cloned.1.call-done.weight), kind=kOutput, calls=%fused_computation.3 | convolution fusion | flops 17181966336 | bytes 29360128 | tf_op jit(solution)/shard_map/dot_general | solution.py:33
  508.7 15.1 %shard_map.308 = bf16[1024,4096]{1,0:T(8,128)(2,1)} custom-call(bf16[1024,1024]{1,0:T(8,128)(2,1)S(1)} %copy-done.6, bf16[1024,4096]{1,0:T(8,128)(2,1)} %shard_map.300.right, bf16[1024,4096]{1,0:T(8,128)(2,1)} %collective-permute-done.56.rest_0_), custom_call_target="tpu_custom_call" | custom-call | flops 8589934592 | bytes 16777216 | tf_op jit(solution)/shard_map/pallas_call | solution.py:367
  529.2 11.3 %collective-permute-done.39 = bf16[512,512]{0,1:T(8,128)(2,1)S(1)} collective-permute-done((bf16[512,512]{0,1:T(8,128)(2,1)S(1)}, bf16[512,512]{0,1:T(8,128)(2,1)S(1)}, u32[]{:S(2)}, u32[]{:S(2)}) %collective-permute-start.39) | collective-permute-done | bytes 524320 | tf_op jit(solution)/shard_map/ppermute | solution.py:503
  542.7 8.6 %collective-permute-done.38 = bf16[512,512]{0,1:T(8,128)(2,1)S(1)} collective-permute-done((bf16[512,512]{0,1:T(8,128)(2,1)S(1)}, bf16[512,512]{0,1:T(8,128)(2,1)S(1)}, u32[]{:S(2)}, u32[]{:S(2)}) %collective-permute-start.38) | collective-permute-done | bytes 524320 | tf_op jit(solution)/shard_map/ppermute | solution.py:503
  551.4 4.2 collective-permute-done.40
  556.0 9.1 %collective-permute-done.41 = bf16[512,512]{0,1:T(8,128)(2,1)S(1)} collective-permute-done((bf16[512,512]{0,1:T(8,128)(2,1)S(1)}, bf16[512,512]{0,1:T(8,128)(2,1)S(1)}, u32[]{:S(2)}, u32[]{:S(2)}) %collective-permute-start.41) | collective-permute-done | bytes 524320 | tf_op jit(solution)/shard_map/ppermute | solution.py:503
  576.5 4.3 convolution_convert_fusion.2
  584.0 11.9 %collective-permute-done.48 = bf16[512,512]{1,0:T(8,128)(2,1)S(1)} collective-permute-done((bf16[512,512]{1,0:T(8,128)(2,1)S(1)}, bf16[512,512]{1,0:T(8,128)(2,1)S(1)}, u32[]{:S(2)}, u32[]{:S(2)}) %collective-permute-start.48) | collective-permute-done | bytes 524320 | tf_op jit(solution)/shard_map/ppermute | solution.py:503
  601.6 7.6 collective-permute-done.49
  610.9 4.0 collective-permute-done.50
  614.8 4.1 collective-permute-done.52
  620.3 16.3 %shard_map.302 = (f32[1024,512]{1,0:T(8,128)}, f32[1024,512]{1,0:T(8,128)}, bf16[1024,512]{1,0:T(8,128)(2,1)S(1)}, f32[8,512]{1,0:T(8,128)S(1)}, f32[1024,128]{1,0:T(8,128)S(1)}) custom-call(bf16[1024,512]{1,0:T(8,128)(2,1)S(1)} %copy-done.27, bf16[1024,512]{1,0:T(8,128)(2,1)S(1)} %copy-done.29, bf16[1024,512]{1,0:T(8,128)(2,1)} %copy-done.30, ...), custom_call_target="tpu_custom_call" | custom-call | flops 5368709120 | bytes 15728640 | tf_op jit(solution)/shard_map/pallas_call | solution.py:231
  644.9 6.2 shard_map.303.grad_qkv.values.other
  651.1 9.1 %shard_map.304.other = bf16[1024,2048]{1,0:T(8,128)(2,1)} custom-call(bf16[1024,1024]{1,0:T(8,128)(2,1)} %get-tuple-element.223.other.token, bf16[1024,1536]{1,0:T(8,128)(2,1)} %shard_map.303.grad_qkv.values.other, bf16[1024,1024]{1,0:T(8,128)(2,1)} %maximum_bitcast_fusion.4.other.attended, bf16[1024,512]{1,0:T(8,128)(2,1)} %shard_map.301.grad_branch), custom_call_target="tpu_custom_call" | custom-call | flops 4294967296 | bytes 6291456 | tf_op jit(solution)/shard_map/pallas_call | solution.py:311
  665.6 11.6 %shard_map.306.other = bf16[1024,2048]{1,0:T(8,128)(2,1)} custom-call(s32[1]{0:T(128)} %bitcast.24.place, bf16[1024,1536]{1,0:T(8,128)(2,1)} %shard_map.305.grad_qkv.values, bf16[2048,2048]{1,0:T(8,128)(2,1)} %all-gather.4.cloned.1.call-done.weight, f32[1024,512]{1,0:T(8,128)} %copy.150.grad_hidden), custom_call_target="tpu_custom_call" | custom-call | flops 6442450944 | bytes 16777216 | tf_op jit(solution)/shard_map/pallas_call | solution.py:335
  677.2 9.7 %shard_map.310.values = bf16[1024,2048]{1,0:T(8,128)(2,1)} custom-call(bf16[1024,1024]{1,0:T(8,128)(2,1)} %get-tuple-element.224.other.token, bf16[1024,1536]{1,0:T(8,128)(2,1)} %shard_map.309.grad_qkv, bf16[1024,1024]{1,0:T(8,128)(2,1)} %maximum_bitcast_fusion.5.other.attended, bf16[1024,512]{1,0:T(8,128)(2,1)} %shard_map.301.grad_branch, ...), custom_call_target="tpu_custom_call" | custom-call | flops 4294967296 | bytes 6291456 | tf_op jit(solution)/shard_map/pallas_call | solution.py:311
  688.0 4.1 all-to-all-start.5
  705.3 4.9 shard_map.316
  712.1 17.5 %collective-permute-done.59 = bf16[256,1024]{1,0:T(8,128)(2,1)} collective-permute-done((bf16[256,1024]{1,0:T(8,128)(2,1)}, bf16[256,1024]{1,0:T(8,128)(2,1)}, u32[]{:S(2)}, u32[]{:S(2)}) %collective-permute-start.59) | collective-permute-done | bytes 524320 | tf_op jit(solution)/shard_map/ppermute | solution.py:503
  740.6 6.4 collective-permute-done.60
  753.7 6.1 collective-permute-done.65
  778.4 10.9 %shard_map.320 = (f32[64,16384]{1,0:T(8,128)}, f32[64,16384]{1,0:T(8,128)}, f32[64,16384]{1,0:T(8,128)}, f32[64,16384]{1,0:T(8,128)}) custom-call(bf16[256,4096]{1,0:T(8,128)(2,1)S(1)} %copy-done.5, f32[64,16384]{1,0:T(8,128)S(1)} %copy-done.3, f32[64,16384]{1,0:T(8,128)S(1)} %copy-done.21, f32[64,16384]{1,0:T(8,128)} %refs_3_.6), custom_call_target="tpu_custom_call" | custom-call | flops 12582912 | bytes 31457280 | tf_op jit(solution)/shard_map/pallas_call | solution.py:104
  795.7 7.4 shard_map.322
  (430 shorter events, 249.2 us)
Async XLA Ops:
  7.2 120.8 %all-gather.4.cloned.1.call-start = ((), (), s32[]{:S(2)}) async-start(), calls=%async_computation.10 | async-start | bytes 9437184 | tf_op jit(solution)/shard_map/all_gather | solution.py:601
  28.5 250.8 %all-gather.6.cloned.1.call-start = ((), (), s32[]{:S(2)}) async-start(), calls=%async_computation.11 | async-start | bytes 18874368 | tf_op jit(solution)/shard_map/all_gather | solution.py:602
  58.8 285.0 %all-gather.8.cloned.1.call-start = ((), (), s32[]{:S(2)}) async-start(), calls=%async_computation.12 | async-start | bytes 9437184 | tf_op jit(solution)/shard_map/all_gather | solution.py:603
  75.5 38.3 %collective-permute-start = (bf16[256,2048]{0,1:T(8,128)(2,1)S(1)}, bf16[256,2048]{0,1:T(8,128)(2,1)}, u32[]{:S(2)}, u32[]{:S(2)}) collective-permute-start(bf16[256,2048]{0,1:T(8,128)(2,1)S(1)} %copy.134), channel_id=1, source_target_pairs={{0,1},{1,0},{2,3},{3,2},{4,5},{5,4},{6,7},{7,6},{8,9},{9,8},{10,11... | collective-permute-start | bytes 3145736 | tf_op jit(solution)/shard_map/ppermute | solution.py:503
  76.5 40.1 %collective-permute-start.1 = (bf16[256,2048]{0,1:T(8,128)(2,1)S(1)}, bf16[256,2048]{0,1:T(8,128)(2,1)}, u32[]{:S(2)}, u32[]{:S(2)}) collective-permute-start(bf16[256,2048]{0,1:T(8,128)(2,1)S(1)} %copy.134), channel_id=1, source_target_pairs={{0,2},{1,3},{2,0},{3,1},{4,6},{5,7},{6,4},{7,5},{8,10},{9,11},{10,... | collective-permute-start | bytes 3145736 | tf_op jit(solution)/shard_map/ppermute | solution.py:503
  77.1 19.4 %collective-permute-start.7 = (f32[256]{0:T(256)S(1)}, f32[256]{0:T(256)S(1)}, u32[]{:S(2)}, u32[]{:S(2)}) collective-permute-start(f32[256]{0:T(256)S(1)} %reshape.206), channel_id=1, source_target_pairs={{0,1},{1,0},{2,3},{3,2},{4,5},{5,4},{6,7},{7,6},{8,9},{9,8},{10,11... | collective-permute-start | bytes 3080 | tf_op jit(solution)/shard_map/ppermute | solution.py:503
  78.6 19.2 %collective-permute-start.8 = (f32[256]{0:T(256)S(1)}, f32[256]{0:T(256)S(1)}, u32[]{:S(2)}, u32[]{:S(2)}) collective-permute-start(f32[256]{0:T(256)S(1)} %reshape.206), channel_id=1, source_target_pairs={{0,2},{1,3},{2,0},{3,1},{4,6},{5,7},{6,4},{7,5},{8,10},{9,11},{10,... | collective-permute-start | bytes 3080 | tf_op jit(solution)/shard_map/ppermute | solution.py:503
  79.7 18.7 %collective-permute-start.9 = (f32[256]{0:T(256)S(1)}, f32[256]{0:T(256)S(1)}, u32[]{:S(2)}, u32[]{:S(2)}) collective-permute-start(f32[256]{0:T(256)S(1)} %reshape.206), channel_id=1, source_target_pairs={{0,3},{1,2},{2,1},{3,0},{4,7},{5,6},{6,5},{7,4},{8,11},{9,10},{10,... | collective-permute-start | bytes 3080 | tf_op jit(solution)/shard_map/ppermute | solution.py:503
  168.0 19.9 %collective-permute-start.17 = (bf16[1024,512]{0,1:T(8,128)(2,1)S(1)}, bf16[1024,512]{0,1:T(8,128)(2,1)S(1)}, u32[]{:S(2)}, u32[]{:S(2)}) collective-permute-start(bf16[1024,512]{0,1:T(8,128)(2,1)S(1)} %copy.140), channel_id=1, source_target_pairs={{0,1},{1,0},{2,3},{3,2},{4,5},{5,4},{6,7},{7,6},{8,9},{9,8},{10,11... | collective-permute-start | bytes 3145736 | tf_op jit(solution)/shard_map/ppermute | solution.py:503
  169.2 27.0 %collective-permute-start.18 = (bf16[1024,512]{0,1:T(8,128)(2,1)S(1)}, bf16[1024,512]{0,1:T(8,128)(2,1)}, u32[]{:S(2)}, u32[]{:S(2)}) collective-permute-start(bf16[1024,512]{0,1:T(8,128)(2,1)S(1)} %copy.140), channel_id=1, source_target_pairs={{0,2},{1,3},{2,0},{3,1},{4,6},{5,7},{6,4},{7,5},{8,10},{9,11},{10,... | collective-permute-start | bytes 3145736 | tf_op jit(solution)/shard_map/ppermute | solution.py:503
  189.7 18.5 %collective-permute-start.19 = (bf16[512,512]{0,1:T(8,128)(2,1)}, bf16[512,512]{0,1:T(8,128)(2,1)}, u32[]{:S(2)}, u32[]{:S(2)}) collective-permute-start(bf16[512,512]{0,1:T(8,128)(2,1)} %slice.93), channel_id=1, source_target_pairs={{0,2},{1,3},{2,0},{3,1},{4,6},{5,7},{6,4},{7,5},{8,10},{9,11},{10,... | collective-permute-start | bytes 1572872 | tf_op jit(solution)/shard_map/ppermute | solution.py:503
  191.7 42.7 %all-to-all-start.1 = ((bf16[4,256,512]{1,2,0:T(8,128)(2,1)}), bf16[4,256,512]{1,2,0:T(8,128)(2,1)}, u32[]{:S(2)}, u32[]{:S(2)}) async-start(bf16[4,256,512]{1,2,0:T(8,128)(2,1)} %bitcast.86), calls=%async_computation.1 | async-start | bytes 2097152 | tf_op jit(solution)/shard_map/all_to_all | solution.py:614
  196.0 380.6 %reduce-scatter.4.cloned.1.call-start = ((), (), s32[]{:S(2)}) async-start(), calls=%async_computation.13 | async-start | bytes 9437184 | tf_op jit(solution)/shard_map/reduce_scatter | solution.py:695
  197.3 17.2 %collective-permute-start.20 = (bf16[512,512]{0,1:T(8,128)(2,1)S(1)}, bf16[512,512]{0,1:T(8,128)(2,1)S(1)}, u32[]{:S(2)}, u32[]{:S(2)}) collective-permute-start(bf16[512,512]{0,1:T(8,128)(2,1)S(1)} %slice.94), channel_id=1, source_target_pairs={{0,1},{1,0},{2,3},{3,2},{4,5},{5,4},{6,7},{7,6},{8,9},{9,8},{10,11... | collective-permute-start | bytes 1572872 | tf_op jit(solution)/shard_map/ppermute | solution.py:503
  232.2 19.1 %collective-permute-start.24 = (bf16[1024,512]{0,1:T(8,128)(2,1)}, bf16[1024,512]{0,1:T(8,128)(2,1)}, u32[]{:S(2)}, u32[]{:S(2)}) collective-permute-start(bf16[1024,512]{0,1:T(8,128)(2,1)} %get-tuple-element.153), channel_id=1, source_target_pairs={{0,1},{1,0},{2,3},{3,2},{4,5},{5,4},{6,7},{7,6},{8,9},{9,8},{10,11... | collective-permute-start | bytes 3145736 | tf_op jit(solution)/shard_map/ppermute | solution.py:503
  233.8 21.8 %collective-permute-start.25 = (bf16[1024,512]{0,1:T(8,128)(2,1)}, bf16[1024,512]{0,1:T(8,128)(2,1)}, u32[]{:S(2)}, u32[]{:S(2)}) collective-permute-start(bf16[1024,512]{0,1:T(8,128)(2,1)} %get-tuple-element.153), channel_id=1, source_target_pairs={{0,2},{1,3},{2,0},{3,1},{4,6},{5,7},{6,4},{7,5},{8,10},{9,11},{10,... | collective-permute-start | bytes 3145736 | tf_op jit(solution)/shard_map/ppermute | solution.py:503
  356.9 14.8 %collective-permute-start.29 = (bf16[256,1024]{1,0:T(8,128)(2,1)S(1)}, bf16[256,1024]{1,0:T(8,128)(2,1)S(1)}, u32[]{:S(2)}, u32[]{:S(2)}) collective-permute-start(bf16[256,1024]{1,0:T(8,128)(2,1)S(1)} %get-tuple-element.177), channel_id=1, source_target_pairs={{0,1},{1,0},{2,3},{3,2},{4,5},{5,4},{6,7},{7,6},{8,9},{9,8},{10,11... | collective-permute-start | bytes 1572872 | tf_op jit(solution)/shard_map/ppermute | solution.py:503
  358.4 23.8 %collective-permute-start.28 = (bf16[256,1024]{1,0:T(8,128)(2,1)S(1)}, bf16[256,1024]{1,0:T(8,128)(2,1)S(1)}, u32[]{:S(2)}, u32[]{:S(2)}) collective-permute-start(bf16[256,1024]{1,0:T(8,128)(2,1)S(1)} %get-tuple-element.174), channel_id=1, source_target_pairs={{0,1},{1,0},{2,3},{3,2},{4,5},{5,4},{6,7},{7,6},{8,9},{9,8},{10,11... | collective-permute-start | bytes 1572872 | tf_op jit(solution)/shard_map/ppermute | solution.py:503
  359.0 23.3 %collective-permute-start.32 = (bf16[256,1024]{1,0:T(8,128)(2,1)S(1)}, bf16[256,1024]{1,0:T(8,128)(2,1)S(1)}, u32[]{:S(2)}, u32[]{:S(2)}) collective-permute-start(bf16[256,1024]{1,0:T(8,128)(2,1)S(1)} %get-tuple-element.175), channel_id=1, source_target_pairs={{0,2},{1,3},{2,0},{3,1},{4,6},{5,7},{6,4},{7,5},{8,10},{9,11},{10,... | collective-permute-start | bytes 1572872 | tf_op jit(solution)/shard_map/ppermute | solution.py:503
  371.9 14.9 %collective-permute-start.30 = (bf16[256,1024]{1,0:T(8,128)(2,1)S(1)}, bf16[256,1024]{1,0:T(8,128)(2,1)S(1)}, u32[]{:S(2)}, u32[]{:S(2)}) collective-permute-start(bf16[256,1024]{1,0:T(8,128)(2,1)S(1)} %add_convert_fusion.11), channel_id=1, source_target_pairs={{0,2},{1,3},{2,0},{3,1},{4,6},{5,7},{6,4},{7,5},{8,10},{9,11},{10,... | collective-permute-start | bytes 1572872 | tf_op jit(solution)/shard_map/ppermute | solution.py:503
  373.5 22.3 %collective-permute-start.31 = (bf16[256,1024]{1,0:T(8,128)(2,1)S(1)}, bf16[256,1024]{1,0:T(8,128)(2,1)S(1)}, u32[]{:S(2)}, u32[]{:S(2)}) collective-permute-start(bf16[256,1024]{1,0:T(8,128)(2,1)S(1)} %get-tuple-element.176), channel_id=1, source_target_pairs={{0,2},{1,3},{2,0},{3,1},{4,6},{5,7},{6,4},{7,5},{8,10},{9,11},{10,... | collective-permute-start | bytes 1572872 | tf_op jit(solution)/shard_map/ppermute | solution.py:503
  401.9 22.0 %collective-permute-start.34 = (bf16[256,2048]{1,0:T(8,128)(2,1)S(1)}, bf16[256,2048]{1,0:T(8,128)(2,1)S(1)}, u32[]{:S(2)}, u32[]{:S(2)}) collective-permute-start(bf16[256,2048]{1,0:T(8,128)(2,1)S(1)} %get-tuple-element.151), channel_id=1, source_target_pairs={{0,1},{1,0},{2,3},{3,2},{4,5},{5,4},{6,7},{7,6},{8,9},{9,8},{10,11... | collective-permute-start | bytes 3145736 | tf_op jit(solution)/shard_map/ppermute | solution.py:503
  403.5 24.2 %collective-permute-start.35 = (bf16[256,2048]{1,0:T(8,128)(2,1)S(1)}, bf16[256,2048]{1,0:T(8,128)(2,1)S(1)}, u32[]{:S(2)}, u32[]{:S(2)}) collective-permute-start(bf16[256,2048]{1,0:T(8,128)(2,1)S(1)} %get-tuple-element.151), channel_id=1, source_target_pairs={{0,2},{1,3},{2,0},{3,1},{4,6},{5,7},{6,4},{7,5},{8,10},{9,11},{10,... | collective-permute-start | bytes 3145736 | tf_op jit(solution)/shard_map/ppermute | solution.py:503
  424.0 12.4 %collective-permute-start.36 = (bf16[256,1024]{1,0:T(8,128)(2,1)S(1)}, bf16[256,1024]{1,0:T(8,128)(2,1)S(1)}, u32[]{:S(2)}, u32[]{:S(2)}) collective-permute-start(bf16[256,1024]{1,0:T(8,128)(2,1)S(1)} %slice.99), channel_id=1, source_target_pairs={{0,2},{1,3},{2,0},{3,1},{4,6},{5,7},{6,4},{7,5},{8,10},{9,11},{10,... | collective-permute-start | bytes 1572872 | tf_op jit(solution)/shard_map/ppermute | solution.py:503
  450.5 237.4 %reduce-scatter.6.cloned.1.call-start = ((), (), s32[]{:S(2)}) async-start(), calls=%async_computation.14 | async-start | bytes 10485760 | tf_op jit(solution)/shard_map/reduce_scatter | solution.py:704
  481.5 25.6 %collective-permute-start.56 = (bf16[1024,4096]{1,0:T(8,128)(2,1)}, bf16[1024,4096]{1,0:T(8,128)(2,1)}, u32[]{:S(2)}, u32[]{:S(2)}) collective-permute-start(bf16[1024,4096]{1,0:T(8,128)(2,1)} %shard_map.299.other), channel_id=1, source_target_pairs={{0,4},{4,0},{1,5},{5,1},{2,6},{6,2},{3,7},{7,3},{8,12},{12,8},{9,1... | collective-permute-start | bytes 25165832 | tf_op jit(solution)/shard_map/ppermute | solution.py:473
  525.7 14.8 %collective-permute-start.39 = (bf16[512,512]{0,1:T(8,128)(2,1)S(1)}, bf16[512,512]{0,1:T(8,128)(2,1)S(1)}, u32[]{:S(2)}, u32[]{:S(2)}) collective-permute-start(bf16[512,512]{0,1:T(8,128)(2,1)S(1)} %get-tuple-element.171), channel_id=1, source_target_pairs={{0,1},{1,0},{2,3},{3,2},{4,5},{5,4},{6,7},{7,6},{8,9},{9,8},{10,11... | collective-permute-start | bytes 1572872 | tf_op jit(solution)/shard_map/ppermute | solution.py:503
  525.8 25.6 %collective-permute-start.38 = (bf16[512,512]{0,1:T(8,128)(2,1)S(1)}, bf16[512,512]{0,1:T(8,128)(2,1)S(1)}, u32[]{:S(2)}, u32[]{:S(2)}) collective-permute-start(bf16[512,512]{0,1:T(8,128)(2,1)S(1)} %get-tuple-element.168), channel_id=1, source_target_pairs={{0,1},{1,0},{2,3},{3,2},{4,5},{5,4},{6,7},{7,6},{8,9},{9,8},{10,11... | collective-permute-start | bytes 1572872 | tf_op jit(solution)/shard_map/ppermute | solution.py:503
  527.8 23.6 %collective-permute-start.42 = (bf16[512,512]{0,1:T(8,128)(2,1)S(1)}, bf16[512,512]{0,1:T(8,128)(2,1)S(1)}, u32[]{:S(2)}, u32[]{:S(2)}) collective-permute-start(bf16[512,512]{0,1:T(8,128)(2,1)S(1)} %get-tuple-element.169), channel_id=1, source_target_pairs={{0,2},{1,3},{2,0},{3,1},{4,6},{5,7},{6,4},{7,5},{8,10},{9,11},{10,... | collective-permute-start | bytes 1572872 | tf_op jit(solution)/shard_map/ppermute | solution.py:503
  540.6 14.9 %collective-permute-start.40 = (bf16[512,512]{0,1:T(8,128)(2,1)S(1)}, bf16[512,512]{0,1:T(8,128)(2,1)S(1)}, u32[]{:S(2)}, u32[]{:S(2)}) collective-permute-start(bf16[512,512]{0,1:T(8,128)(2,1)S(1)} %add_convert_fusion.9), channel_id=1, source_target_pairs={{0,2},{1,3},{2,0},{3,1},{4,6},{5,7},{6,4},{7,5},{8,10},{9,11},{10,... | collective-permute-start | bytes 1572872 | tf_op jit(solution)/shard_map/ppermute | solution.py:503
  542.0 23.2 %collective-permute-start.41 = (bf16[512,512]{0,1:T(8,128)(2,1)S(1)}, bf16[512,512]{0,1:T(8,128)(2,1)S(1)}, u32[]{:S(2)}, u32[]{:S(2)}) collective-permute-start(bf16[512,512]{0,1:T(8,128)(2,1)S(1)} %get-tuple-element.170), channel_id=1, source_target_pairs={{0,2},{1,3},{2,0},{3,1},{4,6},{5,7},{6,4},{7,5},{8,10},{9,11},{10,... | collective-permute-start | bytes 1572872 | tf_op jit(solution)/shard_map/ppermute | solution.py:503
  581.1 14.8 %collective-permute-start.48 = (bf16[512,512]{1,0:T(8,128)(2,1)S(1)}, bf16[512,512]{1,0:T(8,128)(2,1)S(1)}, u32[]{:S(2)}, u32[]{:S(2)}) collective-permute-start(bf16[512,512]{1,0:T(8,128)(2,1)S(1)} %get-tuple-element.165), channel_id=1, source_target_pairs={{0,1},{1,0},{2,3},{3,2},{4,5},{5,4},{6,7},{7,6},{8,9},{9,8},{10,11... | collective-permute-start | bytes 1572872 | tf_op jit(solution)/shard_map/ppermute | solution.py:503
  582.3 19.4 %collective-permute-start.47 = (bf16[512,512]{1,0:T(8,128)(2,1)S(1)}, bf16[512,512]{1,0:T(8,128)(2,1)S(1)}, u32[]{:S(2)}, u32[]{:S(2)}) collective-permute-start(bf16[512,512]{1,0:T(8,128)(2,1)S(1)} %get-tuple-element.162), channel_id=1, source_target_pairs={{0,1},{1,0},{2,3},{3,2},{4,5},{5,4},{6,7},{7,6},{8,9},{9,8},{10,11... | collective-permute-start | bytes 1572872 | tf_op jit(solution)/shard_map/ppermute | solution.py:503
  583.2 18.5 %collective-permute-start.51 = (bf16[512,512]{1,0:T(8,128)(2,1)S(1)}, bf16[512,512]{1,0:T(8,128)(2,1)S(1)}, u32[]{:S(2)}, u32[]{:S(2)}) collective-permute-start(bf16[512,512]{1,0:T(8,128)(2,1)S(1)} %get-tuple-element.163), channel_id=1, source_target_pairs={{0,2},{1,3},{2,0},{3,1},{4,6},{5,7},{6,4},{7,5},{8,10},{9,11},{10,... | collective-permute-start | bytes 1572872 | tf_op jit(solution)/shard_map/ppermute | solution.py:503
  596.1 13.1 %collective-permute-start.49 = (bf16[512,512]{1,0:T(8,128)(2,1)S(1)}, bf16[512,512]{1,0:T(8,128)(2,1)S(1)}, u32[]{:S(2)}, u32[]{:S(2)}) collective-permute-start(bf16[512,512]{1,0:T(8,128)(2,1)S(1)} %add_convert_fusion.7), channel_id=1, source_target_pairs={{0,2},{1,3},{2,0},{3,1},{4,6},{5,7},{6,4},{7,5},{8,10},{9,11},{10,... | collective-permute-start | bytes 1572872 | tf_op jit(solution)/shard_map/ppermute | solution.py:503
  597.1 17.8 %collective-permute-start.50 = (bf16[512,512]{1,0:T(8,128)(2,1)S(1)}, bf16[512,512]{1,0:T(8,128)(2,1)S(1)}, u32[]{:S(2)}, u32[]{:S(2)}) collective-permute-start(bf16[512,512]{1,0:T(8,128)(2,1)S(1)} %get-tuple-element.164), channel_id=1, source_target_pairs={{0,2},{1,3},{2,0},{3,1},{4,6},{5,7},{6,4},{7,5},{8,10},{9,11},{10,... | collective-permute-start | bytes 1572872 | tf_op jit(solution)/shard_map/ppermute | solution.py:503
  660.2 17.0 %collective-permute-start.57 = (bf16[1024,2048]{1,0:T(8,128)(2,1)}, bf16[1024,2048]{1,0:T(8,128)(2,1)}, u32[]{:S(2)}, u32[]{:S(2)}) collective-permute-start(bf16[1024,2048]{1,0:T(8,128)(2,1)} %shard_map.304.other), channel_id=1, source_target_pairs={{0,4},{4,0},{1,5},{5,1},{2,6},{6,2},{3,7},{7,3},{8,12},{12,8},{9,1... | collective-permute-start | bytes 12582920 | tf_op jit(solution)/shard_map/ppermute | solution.py:473
  662.0 24.9 %all-to-all-start.4 = ((bf16[4,64,2048]{2,1,0:T(8,128)(2,1)}), bf16[4,64,2048]{2,1,0:T(8,128)(2,1)S(1)}, u32[]{:S(2)}, u32[]{:S(2)}) async-start(bf16[4,64,2048]{2,1,0:T(8,128)(2,1)} %bitcast.26), calls=%async_computation.6 | async-start | bytes 2097152 | tf_op jit(solution)/shard_map/all_to_all | solution.py:692
  665.5 100.1 %reduce-scatter.8.cloned.1.call-start = ((), (), s32[]{:S(2)}) async-start(), calls=%async_computation.15 | async-start | bytes 5242880 | tf_op jit(solution)/shard_map/reduce_scatter | solution.py:735
  688.0 47.2 %all-to-all-start.5 = ((bf16[4,64,4096]{2,1,0:T(8,128)(2,1)}), bf16[4,64,4096]{2,1,0:T(8,128)(2,1)S(1)}, u32[]{:S(2)}, u32[]{:S(2)}) async-start(bf16[4,64,4096]{2,1,0:T(8,128)(2,1)} %bitcast.81), calls=%async_computation.7 | async-start | bytes 4194304 | tf_op jit(solution)/shard_map/all_to_all | solution.py:692
  695.3 34.3 %collective-permute-start.59 = (bf16[256,1024]{1,0:T(8,128)(2,1)}, bf16[256,1024]{1,0:T(8,128)(2,1)}, u32[]{:S(2)}, u32[]{:S(2)}) collective-permute-start(bf16[256,1024]{1,0:T(8,128)(2,1)} %get-tuple-element.159), channel_id=1, source_target_pairs={{0,1},{1,0},{2,3},{3,2},{4,5},{5,4},{6,7},{7,6},{8,9},{9,8},{10,11... | collective-permute-start | bytes 1572872 | tf_op jit(solution)/shard_map/ppermute | solution.py:503
  697.3 42.5 %collective-permute-start.58 = (bf16[256,1024]{1,0:T(8,128)(2,1)}, bf16[256,1024]{1,0:T(8,128)(2,1)S(1)}, u32[]{:S(2)}, u32[]{:S(2)}) collective-permute-start(bf16[256,1024]{1,0:T(8,128)(2,1)} %get-tuple-element.156), channel_id=1, source_target_pairs={{0,1},{1,0},{2,3},{3,2},{4,5},{5,4},{6,7},{7,6},{8,9},{9,8},{10,11... | collective-permute-start | bytes 1572872 | tf_op jit(solution)/shard_map/ppermute | solution.py:503
  697.3 42.8 %collective-permute-start.69 = (bf16[256,1024]{1,0:T(8,128)(2,1)S(1)}, bf16[256,1024]{1,0:T(8,128)(2,1)}, u32[]{:S(2)}, u32[]{:S(2)}) collective-permute-start(bf16[256,1024]{1,0:T(8,128)(2,1)S(1)} %get-tuple-element.157), channel_id=1, source_target_pairs={{0,2},{1,3},{2,0},{3,1},{4,6},{5,7},{6,4},{7,5},{8,10},{9,11},{10,... | collective-permute-start | bytes 1572872 | tf_op jit(solution)/shard_map/ppermute | solution.py:503
  731.8 15.2 %collective-permute-start.60 = (bf16[256,1024]{1,0:T(8,128)(2,1)}, bf16[256,1024]{1,0:T(8,128)(2,1)}, u32[]{:S(2)}, u32[]{:S(2)}) collective-permute-start(bf16[256,1024]{1,0:T(8,128)(2,1)} %add_convert_fusion.3), channel_id=1, source_target_pairs={{0,2},{1,3},{2,0},{3,1},{4,6},{5,7},{6,4},{7,5},{8,10},{9,11},{10,... | collective-permute-start | bytes 1572872 | tf_op jit(solution)/shard_map/ppermute | solution.py:503
  733.9 28.5 %collective-permute-start.68 = (bf16[256,1024]{1,0:T(8,128)(2,1)}, bf16[256,1024]{1,0:T(8,128)(2,1)}, u32[]{:S(2)}, u32[]{:S(2)}) collective-permute-start(bf16[256,1024]{1,0:T(8,128)(2,1)} %get-tuple-element.158), channel_id=1, source_target_pairs={{0,2},{1,3},{2,0},{3,1},{4,6},{5,7},{6,4},{7,5},{8,10},{9,11},{10,... | collective-permute-start | bytes 1572872 | tf_op jit(solution)/shard_map/ppermute | solution.py:503
  735.1 14.9 %collective-permute-start.62 = (f32[8192]{0:T(1024)S(1)}, f32[8192]{0:T(1024)S(1)}, u32[]{:S(2)}, u32[]{:S(2)}) collective-permute-start(f32[8192]{0:T(1024)S(1)} %add.450), channel_id=1, source_target_pairs={{0,8},{8,16},{16,24},{24,0},{1,9},{9,17},{17,25},{25,1},{2,10},{10... | collective-permute-start | bytes 98312 | tf_op jit(solution)/shard_map/ppermute | solution.py:477
  750.0 12.4 %collective-permute-start.70 = (bf16[256,1024]{1,0:T(8,128)(2,1)}, bf16[256,1024]{1,0:T(8,128)(2,1)}, u32[]{:S(2)}, u32[]{:S(2)}) collective-permute-start(bf16[256,1024]{1,0:T(8,128)(2,1)} %get-tuple-element.155), channel_id=1, source_target_pairs={{0,1},{1,0},{2,3},{3,2},{4,5},{5,4},{6,7},{7,6},{8,9},{9,8},{10,11... | collective-permute-start | bytes 1572872 | tf_op jit(solution)/shard_map/ppermute | solution.py:503
  765.7 23.6 %all-to-all-start.6 = ((bf16[4,64,2048]{2,1,0:T(8,128)(2,1)}), bf16[4,64,2048]{2,1,0:T(8,128)(2,1)S(1)}, u32[]{:S(2)}, u32[]{:S(2)}) async-start(bf16[4,64,2048]{2,1,0:T(8,128)(2,1)} %bitcast.82), calls=%async_computation.9 | async-start | bytes 2097152 | tf_op jit(solution)/shard_map/all_to_all | solution.py:692
  (96 other events, 1490.5 us)
Sparse Core Ops, SparseCore 0:
  28.6 82.0 all-gather.3
  112.3 149.6 all-gather.5
  263.5 80.2 all-gather.7
  450.7 87.1 reduce-scatter.3
  540.1 142.8 reduce-scatter.5
  688.1 77.5 reduce-scatter.7

commit v6 on v5

--- a/solution.py
+++ b/solution.py
@@ -374,7 +374,7 @@
         + [spec] * len(other),
         out_specs=spec,
         out_shape=jax.ShapeDtypeStruct((rows, columns), bf16),
-        compiler_params=pltpu.CompilerParams(vmem_limit_bytes=48 * 1024 * 1024),
+        compiler_params=pltpu.CompilerParams(vmem_limit_bytes=ALL_VMEM),
         cost_estimate=pl.CostEstimate(
             flops=2 * rows * length * columns, bytes_accessed=4 * rows * columns, transcendentals=0
         ),

time: 817 us -> 819 us (level)
    unnamed x135 -> x107, local copies, waits for them, and re-layouts: 42.1 us -> 40.5 us
  transfers between devices with their start and end apart: 81 -> 81, of which waited for: 49 -> 49; matrix products, arithmetic and copies ran while one was open for 17% -> 18% of each run, Pallas kernels for 19% -> 20%
where the time goes in v6:
time: 819 us; the launch traced here: 812 us
  waiting for transfers between devices  266 us (32%)
  Pallas kernels  166 us (20%)
  local copies, waits for them, and re-layouts  107 us (13%)
  starting transfers between devices  89.6 us (11%)
  matrix products  68.9 us (8%)
  blocking collectives  61.5 us (8%)
  other arithmetic  34.7 us (4%)
  between operations  17.4 us (2%)
    ppermute x61, waiting for transfers between devices, swap(): return lax.ppermute(values, FSDP, [(i, i ^ bit) for i in range(self.count)])  228 us
    dot_general x6, matrix products, mm(): lax.dot_general(left, right, (dims, ((), ())), preferred_element_type=f32)  68.9 us
    ppermute x61, starting transfers between devices, swap(): return lax.ppermute(values, FSDP, [(i, i ^ bit) for i in range(self.count)])  66.5 us
    all_to_all x3, blocking collectives, spread(): return lax.all_to_all(block, FSDP, 0, 0, tiled=True)  61.5 us
    unnamed x107, local copies, waits for them, and re-layouts  40.5 us
    all_gather x1, waiting for transfers between devices, per_device(): down_all = lax.all_gather(spread(w_down, 1), DP, axis=0, tiled=True)  33.8 us
    pallas_call x2, Pallas kernels, half_grad(): pl.pallas_call(half_grad_body, grid=(columns // size,), in_specs=[pl.Bloc...  30.2 us
    dynamic_update_slice x19, local copies, waits for them, and re-layouts, gather(): out = lax.dynamic_update_slice(out, part, start)  24.3 us
  transfers between devices with their start and end apart: 81, of which 49 were waited for; matrix products, arithmetic and copies ran while one was open for 18% of the time, Pallas kernels for 20%

profile of v6, /device:TPU:0, one launch (start us, length us, event | category | flops | bytes accessed | tf_op | source)
XLA Modules:
  0.0 811.8 jit_solution(8782168948790624799)
XLA Ops:
  9.2 19.2 %all_to_all.75 = bf16[4,64,2048]{2,1,0:T(8,128)(2,1)} all-to-all(bf16[4,64,2048]{2,1,0:T(8,128)(2,1)S(1)} %bitcast.77), channel_id=1, replica_groups=mesh['z'=4,'core'=2,'y'=2,'x'=2] {'y','x'}, dimensions={0} | all-to-all | bytes 2097152 | tf_op jit(solution)/shard_map/all_to_all | solution.py:599
  31.3 27.5 %all_to_all.76 = bf16[4,64,4096]{2,1,0:T(8,128)(2,1)} all-to-all(bf16[4,64,4096]{2,1,0:T(8,128)(2,1)S(1)} %bitcast.76), channel_id=1, replica_groups=mesh['z'=4,'core'=2,'y'=2,'x'=2] {'y','x'}, dimensions={0} | all-to-all | bytes 4194304 | tf_op jit(solution)/shard_map/all_to_all | solution.py:599
  59.2 14.8 %all_to_all.77 = bf16[4,64,2048]{2,1,0:T(8,128)(2,1)} all-to-all(bf16[4,64,2048]{2,1,0:T(8,128)(2,1)S(1)} %bitcast.78), channel_id=1, replica_groups=mesh['z'=4,'core'=2,'y'=2,'x'=2] {'y','x'}, dimensions={0} | all-to-all | bytes 2097152 | tf_op jit(solution)/shard_map/all_to_all | solution.py:599
  84.3 12.3 %collective-permute-done.7 = f32[256]{0:T(256)S(1)} collective-permute-done((f32[256]{0:T(256)S(1)}, f32[256]{0:T(256)S(1)}, u32[]{:S(2)}, u32[]{:S(2)}) %collective-permute-start.7) | collective-permute-done | bytes 1056 | tf_op jit(solution)/shard_map/ppermute | solution.py:503
  128.0 10.6 %fusion.refs_0_.refs_1_.refs_2_.refs_6_.refs_7_.raw = f32[1024,1536]{1,0:T(8,128)S(1)} fusion(bf16[1024,2048]{0,1:T(8,128)(2,1)} %constant_dynamic-update-slice_fusion.19, bf16[2048,2048]{1,0:T(8,128)(2,1)} %all-gather.4.cloned.1.call-done.weight), kind=kOutput, calls=%fused_computation.1 | convolution fusion | flops 6442450944 | bytes 16777216 | tf_op jit(solution)/shard_map/dot_general | solution.py:33
  145.8 17.7 %shard_map.287 = (bf16[1024,512]{1,0:T(8,128)(2,1)S(1)}, bf16[1024,512]{1,0:T(8,128)(2,1)S(1)}, bf16[1024,512]{1,0:T(8,128)(2,1)S(1)}, bf16[1024,512]{1,0:T(8,128)(2,1)}, f32[4,1024,1]{2,1,0:T(8,128)}) custom-call(f32[1024,1536]{1,0:T(8,128)} %copy-done.24, f32[1024,1536]{1,0:T(8,128)} %copy-done.24, f32[1024,1536]{1,0:T(8,128)} %copy-done.24, ...), custom_call_target="tpu_custom_call" | custom-call | flops 2147483648 | bytes 10485760 | tf_op jit(solution)/shard_map/pallas_call | solution.py:218
  169.9 17.9 %collective-permute-done.17 = bf16[1024,512]{0,1:T(8,128)(2,1)S(1)} collective-permute-done((bf16[1024,512]{0,1:T(8,128)(2,1)}, bf16[1024,512]{0,1:T(8,128)(2,1)S(1)}, u32[]{:S(2)}, u32[]{:S(2)}) %collective-permute-start.17) | collective-permute-done | bytes 1048608 | tf_op jit(solution)/shard_map/ppermute | solution.py:503
  192.6 4.2 all-to-all-start.1
  202.5 5.6 collective-permute-done.19
  209.3 6.1 collective-permute-done.20
  215.5 6.8 multiply_reduce_fusion.3
  249.2 4.4 collective-permute-done.24
  268.9 6.6 copy.143.values
  284.0 24.1 %shard_map.296 = (bf16[1024,4096]{1,0:T(8,128)(2,1)}, bf16[1024,2048]{1,0:T(8,128)(2,1)S(1)}) custom-call(bf16[1024,2048]{1,0:T(8,128)(2,1)} %shard_map.294.hidden, bf16[2048,4096]{1,0:T(8,128)(2,1)} %all-gather.6.cloned.1.call-done.weight), custom_call_target="tpu_custom_call" | custom-call | flops 17179869184 | bytes 37748736 | tf_op jit(solution)/shard_map/pallas_call | solution.py:410
  310.1 33.8 %all-gather.8.cloned.1.call-done.weight = bf16[2048,2048]{1,0:T(8,128)(2,1)} async-done(((bf16[256,2048]{1,0:T(8,128)(2,1)}), bf16[2048,2048]{1,0:T(8,128)(2,1)}) %all-gather.8.cloned.1.call-update) | async-done | bytes 8388624 | tf_op jit(solution)/shard_map/all_gather | solution.py:603
  343.9 12.8 %convolution_convert_fusion.3 = bf16[1024,2048]{1,0:T(8,128)(2,1)S(1)} fusion(bf16[1024,2048]{1,0:T(8,128)(2,1)} %copy-done.22, bf16[2048,2048]{1,0:T(8,128)(2,1)} %all-gather.8.cloned.1.call-done.weight), kind=kOutput, calls=%fused_computation.5 | convolution fusion | flops 8592031744 | bytes 16777216 | tf_op jit(solution)/shard_map/dot_general | solution.py:33
  360.5 11.2 %collective-permute-done.29 = bf16[256,1024]{1,0:T(8,128)(2,1)S(1)} collective-permute-done((bf16[256,1024]{1,0:T(8,128)(2,1)S(1)}, bf16[256,1024]{1,0:T(8,128)(2,1)S(1)}, u32[]{:S(2)}, u32[]{:S(2)}) %collective-permute-start.29) | collective-permute-done | bytes 524320 | tf_op jit(solution)/shard_map/ppermute | solution.py:503
  374.0 8.2 %collective-permute-done.28 = bf16[256,1024]{1,0:T(8,128)(2,1)S(1)} collective-permute-done((bf16[256,1024]{1,0:T(8,128)(2,1)S(1)}, bf16[256,1024]{1,0:T(8,128)(2,1)S(1)}, u32[]{:S(2)}, u32[]{:S(2)}) %collective-permute-start.28) | collective-permute-done | bytes 524320 | tf_op jit(solution)/shard_map/ppermute | solution.py:503
  382.3 4.6 collective-permute-done.30
  388.9 6.9 collective-permute-done.31
  405.0 18.9 %collective-permute-done.34 = bf16[256,2048]{1,0:T(8,128)(2,1)S(1)} collective-permute-done((bf16[256,2048]{1,0:T(8,128)(2,1)S(1)}, bf16[256,2048]{1,0:T(8,128)(2,1)S(1)}, u32[]{:S(2)}, u32[]{:S(2)}) %collective-permute-start.34) | collective-permute-done | bytes 1048608 | tf_op jit(solution)/shard_map/ppermute | solution.py:503
  428.3 8.1 collective-permute-done.36
  439.1 11.5 %convolution_convert_fusion = bf16[2048,2048]{1,0:T(8,128)(2,1)} fusion(bf16[1024,2048]{1,0:T(8,128)(2,1)S(1)} %constant_dynamic-update-slice_fusion.18.grad_mlp, bf16[1024,2048]{1,0:T(8,128)(2,1)S(1)} %copy-done.23), kind=kOutput, calls=%fused_computation | convolution fusion | flops 8594128896 | bytes 16777216 | tf_op jit(solution)/shard_map/dot_general | solution.py:33
  450.7 17.2 %shard_map.298.right.values = bf16[1024,4096]{1,0:T(8,128)(2,1)} custom-call(bf16[1024,2048]{1,0:T(8,128)(2,1)} %copy-done.36, bf16[2048,2048]{1,0:T(8,128)(2,1)} %all-gather.8.cloned.1.call-done.weight, bf16[1024,4096]{1,0:T(8,128)(2,1)} %get-tuple-element.47.both), custom_call_target="tpu_custom_call" | custom-call | flops 8589934592 | bytes 33554432 | tf_op jit(solution)/shard_map/pallas_call | solution.py:428
  467.9 14.3 %shard_map.299.other = bf16[1024,4096]{1,0:T(8,128)(2,1)} custom-call(bf16[1024,1024]{1,0:T(8,128)(2,1)} %maximum_bitcast_fusion.other.left, bf16[1024,4096]{1,0:T(8,128)(2,1)} %shard_map.298.right.values), custom_call_target="tpu_custom_call" | custom-call | flops 8589934592 | bytes 16777216 | tf_op jit(solution)/shard_map/pallas_call | solution.py:367
  482.2 22.9 %convolution_convert_fusion.1 = bf16[1024,2048]{0,1:T(8,128)(2,1)S(1)} fusion(bf16[1024,4096]{1,0:T(8,128)(2,1)} %shard_map.300.right, bf16[2048,4096]{1,0:T(8,128)(2,1)} %all-gather.6.cloned.1.call-done.weight), kind=kOutput, calls=%fused_computation.3 | convolution fusion | flops 17181966336 | bytes 29360128 | tf_op jit(solution)/shard_map/dot_general | solution.py:33
  507.8 15.9 %shard_map.308 = bf16[1024,4096]{1,0:T(8,128)(2,1)} custom-call(bf16[1024,1024]{1,0:T(8,128)(2,1)} %shard_map.307.left, bf16[1024,4096]{1,0:T(8,128)(2,1)} %shard_map.300.right, bf16[1024,4096]{1,0:T(8,128)(2,1)} %collective-permute-done.56.rest_0_), custom_call_target="tpu_custom_call" | custom-call | flops 8589934592 | bytes 16777216 | tf_op jit(solution)/shard_map/pallas_call | solution.py:367
  528.9 11.4 %collective-permute-done.39 = bf16[512,512]{0,1:T(8,128)(2,1)S(1)} collective-permute-done((bf16[512,512]{0,1:T(8,128)(2,1)S(1)}, bf16[512,512]{0,1:T(8,128)(2,1)S(1)}, u32[]{:S(2)}, u32[]{:S(2)}) %collective-permute-start.39) | collective-permute-done | bytes 524320 | tf_op jit(solution)/shard_map/ppermute | solution.py:503
  542.6 8.6 %collective-permute-done.38 = bf16[512,512]{0,1:T(8,128)(2,1)S(1)} collective-permute-done((bf16[512,512]{0,1:T(8,128)(2,1)S(1)}, bf16[512,512]{0,1:T(8,128)(2,1)S(1)}, u32[]{:S(2)}, u32[]{:S(2)}) %collective-permute-start.38) | collective-permute-done | bytes 524320 | tf_op jit(solution)/shard_map/ppermute | solution.py:503
  551.2 4.2 collective-permute-done.40
  555.9 9.2 %collective-permute-done.41 = bf16[512,512]{0,1:T(8,128)(2,1)S(1)} collective-permute-done((bf16[512,512]{0,1:T(8,128)(2,1)S(1)}, bf16[512,512]{0,1:T(8,128)(2,1)S(1)}, u32[]{:S(2)}, u32[]{:S(2)}) %collective-permute-start.41) | collective-permute-done | bytes 524320 | tf_op jit(solution)/shard_map/ppermute | solution.py:503
  578.6 4.3 convolution_convert_fusion.2
  585.8 12.3 %collective-permute-done.48 = bf16[512,512]{1,0:T(8,128)(2,1)S(1)} collective-permute-done((bf16[512,512]{1,0:T(8,128)(2,1)S(1)}, bf16[512,512]{1,0:T(8,128)(2,1)S(1)}, u32[]{:S(2)}, u32[]{:S(2)}) %collective-permute-start.48) | collective-permute-done | bytes 524320 | tf_op jit(solution)/shard_map/ppermute | solution.py:503
  604.1 7.2 collective-permute-done.49
  616.9 4.1 collective-permute-done.52
  622.3 16.2 %shard_map.302 = (f32[1024,512]{1,0:T(8,128)}, f32[1024,512]{1,0:T(8,128)}, bf16[1024,512]{1,0:T(8,128)(2,1)S(1)}, f32[8,512]{1,0:T(8,128)S(1)}, f32[1024,128]{1,0:T(8,128)S(1)}) custom-call(bf16[1024,512]{1,0:T(8,128)(2,1)S(1)} %get-tuple-element.44.refs_0_, bf16[1024,512]{1,0:T(8,128)(2,1)S(1)} %copy-done.19, bf16[1024,512]{1,0:T(8,128)(2,1)} %copy-done.20, ...), custom_call_target="tpu_custom_call" | custom-call | flops 5368709120 | bytes 15728640 | tf_op jit(solution)/shard_map/pallas_call | solution.py:231
  646.7 6.2 shard_map.303.grad_qkv.values.other
  653.0 9.0 %shard_map.304.other = bf16[1024,2048]{1,0:T(8,128)(2,1)} custom-call(bf16[1024,1024]{1,0:T(8,128)(2,1)} %get-tuple-element.223.other.token, bf16[1024,1536]{1,0:T(8,128)(2,1)} %shard_map.303.grad_qkv.values.other, bf16[1024,1024]{1,0:T(8,128)(2,1)} %maximum_bitcast_fusion.4.other.attended, bf16[1024,512]{1,0:T(8,128)(2,1)} %shard_map.301.grad_branch), custom_call_target="tpu_custom_call" | custom-call | flops 4294967296 | bytes 6291456 | tf_op jit(solution)/shard_map/pallas_call | solution.py:311
  667.3 11.6 %shard_map.306.other = bf16[1024,2048]{1,0:T(8,128)(2,1)} custom-call(s32[1]{0:T(128)} %bitcast.24.place, bf16[1024,1536]{1,0:T(8,128)(2,1)} %shard_map.305.grad_qkv.values, bf16[2048,2048]{1,0:T(8,128)(2,1)} %all-gather.4.cloned.1.call-done.weight, f32[1024,512]{1,0:T(8,128)} %copy.150.grad_hidden), custom_call_target="tpu_custom_call" | custom-call | flops 6442450944 | bytes 16777216 | tf_op jit(solution)/shard_map/pallas_call | solution.py:335
  678.9 9.7 %shard_map.310.values = bf16[1024,2048]{1,0:T(8,128)(2,1)} custom-call(bf16[1024,1024]{1,0:T(8,128)(2,1)} %get-tuple-element.224.other.token, bf16[1024,1536]{1,0:T(8,128)(2,1)} %shard_map.309.grad_qkv, bf16[1024,1024]{1,0:T(8,128)(2,1)} %maximum_bitcast_fusion.5.other.attended, bf16[1024,512]{1,0:T(8,128)(2,1)} %shard_map.301.grad_branch, ...), custom_call_target="tpu_custom_call" | custom-call | flops 4294967296 | bytes 6291456 | tf_op jit(solution)/shard_map/pallas_call | solution.py:311
  689.7 4.1 all-to-all-start.5
  707.2 4.9 shard_map.316
  714.0 17.4 %collective-permute-done.59 = bf16[256,1024]{1,0:T(8,128)(2,1)} collective-permute-done((bf16[256,1024]{1,0:T(8,128)(2,1)}, bf16[256,1024]{1,0:T(8,128)(2,1)}, u32[]{:S(2)}, u32[]{:S(2)}) %collective-permute-start.59) | collective-permute-done | bytes 524320 | tf_op jit(solution)/shard_map/ppermute | solution.py:503
  737.5 4.2 collective-permute-done.58
  742.6 5.3 collective-permute-done.60
  754.5 6.1 collective-permute-done.65
  780.0 10.9 %shard_map.320 = (f32[64,16384]{1,0:T(8,128)}, f32[64,16384]{1,0:T(8,128)}, f32[64,16384]{1,0:T(8,128)}, f32[64,16384]{1,0:T(8,128)}) custom-call(bf16[256,4096]{1,0:T(8,128)(2,1)S(1)} %copy-done.5, f32[64,16384]{1,0:T(8,128)S(1)} %copy-done.3, f32[64,16384]{1,0:T(8,128)S(1)} %copy-done.13, f32[64,16384]{1,0:T(8,128)} %refs_3_.6), custom_call_target="tpu_custom_call" | custom-call | flops 12582912 | bytes 31457280 | tf_op jit(solution)/shard_map/pallas_call | solution.py:104
  797.3 7.4 shard_map.322
  (402 shorter events, 255.7 us)
Async XLA Ops:
  7.2 120.8 %all-gather.4.cloned.1.call-start = ((), (), s32[]{:S(2)}) async-start(), calls=%async_computation.10 | async-start | bytes 9437184 | tf_op jit(solution)/shard_map/all_gather | solution.py:601
  28.5 255.5 %all-gather.6.cloned.1.call-start = ((), (), s32[]{:S(2)}) async-start(), calls=%async_computation.11 | async-start | bytes 18874368 | tf_op jit(solution)/shard_map/all_gather | solution.py:602
  58.8 285.1 %all-gather.8.cloned.1.call-start = ((), (), s32[]{:S(2)}) async-start(), calls=%async_computation.12 | async-start | bytes 9437184 | tf_op jit(solution)/shard_map/all_gather | solution.py:603
  75.5 38.3 %collective-permute-start = (bf16[256,2048]{0,1:T(8,128)(2,1)S(1)}, bf16[256,2048]{0,1:T(8,128)(2,1)}, u32[]{:S(2)}, u32[]{:S(2)}) collective-permute-start(bf16[256,2048]{0,1:T(8,128)(2,1)S(1)} %copy.134), channel_id=1, source_target_pairs={{0,1},{1,0},{2,3},{3,2},{4,5},{5,4},{6,7},{7,6},{8,9},{9,8},{10,11... | collective-permute-start | bytes 3145736 | tf_op jit(solution)/shard_map/ppermute | solution.py:503
  76.5 40.1 %collective-permute-start.1 = (bf16[256,2048]{0,1:T(8,128)(2,1)S(1)}, bf16[256,2048]{0,1:T(8,128)(2,1)}, u32[]{:S(2)}, u32[]{:S(2)}) collective-permute-start(bf16[256,2048]{0,1:T(8,128)(2,1)S(1)} %copy.134), channel_id=1, source_target_pairs={{0,2},{1,3},{2,0},{3,1},{4,6},{5,7},{6,4},{7,5},{8,10},{9,11},{10,... | collective-permute-start | bytes 3145736 | tf_op jit(solution)/shard_map/ppermute | solution.py:503
  77.2 19.4 %collective-permute-start.7 = (f32[256]{0:T(256)S(1)}, f32[256]{0:T(256)S(1)}, u32[]{:S(2)}, u32[]{:S(2)}) collective-permute-start(f32[256]{0:T(256)S(1)} %reshape.206), channel_id=1, source_target_pairs={{0,1},{1,0},{2,3},{3,2},{4,5},{5,4},{6,7},{7,6},{8,9},{9,8},{10,11... | collective-permute-start | bytes 3080 | tf_op jit(solution)/shard_map/ppermute | solution.py:503
  78.6 19.2 %collective-permute-start.8 = (f32[256]{0:T(256)S(1)}, f32[256]{0:T(256)S(1)}, u32[]{:S(2)}, u32[]{:S(2)}) collective-permute-start(f32[256]{0:T(256)S(1)} %reshape.206), channel_id=1, source_target_pairs={{0,2},{1,3},{2,0},{3,1},{4,6},{5,7},{6,4},{7,5},{8,10},{9,11},{10,... | collective-permute-start | bytes 3080 | tf_op jit(solution)/shard_map/ppermute | solution.py:503
  79.7 18.7 %collective-permute-start.9 = (f32[256]{0:T(256)S(1)}, f32[256]{0:T(256)S(1)}, u32[]{:S(2)}, u32[]{:S(2)}) collective-permute-start(f32[256]{0:T(256)S(1)} %reshape.206), channel_id=1, source_target_pairs={{0,3},{1,2},{2,1},{3,0},{4,7},{5,6},{6,5},{7,4},{8,11},{9,10},{10,... | collective-permute-start | bytes 3080 | tf_op jit(solution)/shard_map/ppermute | solution.py:503
  167.8 20.0 %collective-permute-start.17 = (bf16[1024,512]{0,1:T(8,128)(2,1)}, bf16[1024,512]{0,1:T(8,128)(2,1)S(1)}, u32[]{:S(2)}, u32[]{:S(2)}) collective-permute-start(bf16[1024,512]{0,1:T(8,128)(2,1)} %copy.140), channel_id=1, source_target_pairs={{0,1},{1,0},{2,3},{3,2},{4,5},{5,4},{6,7},{7,6},{8,9},{9,8},{10,11... | collective-permute-start | bytes 3145736 | tf_op jit(solution)/shard_map/ppermute | solution.py:503
  168.9 28.2 %collective-permute-start.18 = (bf16[1024,512]{0,1:T(8,128)(2,1)}, bf16[1024,512]{0,1:T(8,128)(2,1)}, u32[]{:S(2)}, u32[]{:S(2)}) collective-permute-start(bf16[1024,512]{0,1:T(8,128)(2,1)} %copy.140), channel_id=1, source_target_pairs={{0,2},{1,3},{2,0},{3,1},{4,6},{5,7},{6,4},{7,5},{8,10},{9,11},{10,... | collective-permute-start | bytes 3145736 | tf_op jit(solution)/shard_map/ppermute | solution.py:503
  189.6 18.5 %collective-permute-start.19 = (bf16[512,512]{0,1:T(8,128)(2,1)}, bf16[512,512]{0,1:T(8,128)(2,1)}, u32[]{:S(2)}, u32[]{:S(2)}) collective-permute-start(bf16[512,512]{0,1:T(8,128)(2,1)} %slice.93), channel_id=1, source_target_pairs={{0,2},{1,3},{2,0},{3,1},{4,6},{5,7},{6,4},{7,5},{8,10},{9,11},{10,... | collective-permute-start | bytes 1572872 | tf_op jit(solution)/shard_map/ppermute | solution.py:503
  192.6 43.9 %all-to-all-start.1 = ((bf16[4,256,512]{1,2,0:T(8,128)(2,1)}), bf16[4,256,512]{1,2,0:T(8,128)(2,1)}, u32[]{:S(2)}, u32[]{:S(2)}) async-start(bf16[4,256,512]{1,2,0:T(8,128)(2,1)} %bitcast.86), calls=%async_computation.1 | async-start | bytes 2097152 | tf_op jit(solution)/shard_map/all_to_all | solution.py:614
  196.9 381.7 %reduce-scatter.4.cloned.1.call-start = ((), (), s32[]{:S(2)}) async-start(), calls=%async_computation.13 | async-start | bytes 9437184 | tf_op jit(solution)/shard_map/reduce_scatter | solution.py:695
  198.4 17.1 %collective-permute-start.20 = (bf16[512,512]{0,1:T(8,128)(2,1)S(1)}, bf16[512,512]{0,1:T(8,128)(2,1)S(1)}, u32[]{:S(2)}, u32[]{:S(2)}) collective-permute-start(bf16[512,512]{0,1:T(8,128)(2,1)S(1)} %slice.94), channel_id=1, source_target_pairs={{0,1},{1,0},{2,3},{3,2},{4,5},{5,4},{6,7},{7,6},{8,9},{9,8},{10,11... | collective-permute-start | bytes 1572872 | tf_op jit(solution)/shard_map/ppermute | solution.py:503
  234.4 19.2 %collective-permute-start.24 = (bf16[1024,512]{0,1:T(8,128)(2,1)}, bf16[1024,512]{0,1:T(8,128)(2,1)}, u32[]{:S(2)}, u32[]{:S(2)}) collective-permute-start(bf16[1024,512]{0,1:T(8,128)(2,1)} %get-tuple-element.153), channel_id=1, source_target_pairs={{0,1},{1,0},{2,3},{3,2},{4,5},{5,4},{6,7},{7,6},{8,9},{9,8},{10,11... | collective-permute-start | bytes 3145736 | tf_op jit(solution)/shard_map/ppermute | solution.py:503
  235.9 21.8 %collective-permute-start.25 = (bf16[1024,512]{0,1:T(8,128)(2,1)}, bf16[1024,512]{0,1:T(8,128)(2,1)}, u32[]{:S(2)}, u32[]{:S(2)}) collective-permute-start(bf16[1024,512]{0,1:T(8,128)(2,1)} %get-tuple-element.153), channel_id=1, source_target_pairs={{0,2},{1,3},{2,0},{3,1},{4,6},{5,7},{6,4},{7,5},{8,10},{9,11},{10,... | collective-permute-start | bytes 3145736 | tf_op jit(solution)/shard_map/ppermute | solution.py:503
  356.9 14.8 %collective-permute-start.29 = (bf16[256,1024]{1,0:T(8,128)(2,1)S(1)}, bf16[256,1024]{1,0:T(8,128)(2,1)S(1)}, u32[]{:S(2)}, u32[]{:S(2)}) collective-permute-start(bf16[256,1024]{1,0:T(8,128)(2,1)S(1)} %get-tuple-element.177), channel_id=1, source_target_pairs={{0,1},{1,0},{2,3},{3,2},{4,5},{5,4},{6,7},{7,6},{8,9},{9,8},{10,11... | collective-permute-start | bytes 1572872 | tf_op jit(solution)/shard_map/ppermute | solution.py:503
  358.5 23.8 %collective-permute-start.28 = (bf16[256,1024]{1,0:T(8,128)(2,1)S(1)}, bf16[256,1024]{1,0:T(8,128)(2,1)S(1)}, u32[]{:S(2)}, u32[]{:S(2)}) collective-permute-start(bf16[256,1024]{1,0:T(8,128)(2,1)S(1)} %get-tuple-element.174), channel_id=1, source_target_pairs={{0,1},{1,0},{2,3},{3,2},{4,5},{5,4},{6,7},{7,6},{8,9},{9,8},{10,11... | collective-permute-start | bytes 1572872 | tf_op jit(solution)/shard_map/ppermute | solution.py:503
  359.0 23.3 %collective-permute-start.32 = (bf16[256,1024]{1,0:T(8,128)(2,1)S(1)}, bf16[256,1024]{1,0:T(8,128)(2,1)S(1)}, u32[]{:S(2)}, u32[]{:S(2)}) collective-permute-start(bf16[256,1024]{1,0:T(8,128)(2,1)S(1)} %get-tuple-element.175), channel_id=1, source_target_pairs={{0,2},{1,3},{2,0},{3,1},{4,6},{5,7},{6,4},{7,5},{8,10},{9,11},{10,... | collective-permute-start | bytes 1572872 | tf_op jit(solution)/shard_map/ppermute | solution.py:503
  371.9 14.9 %collective-permute-start.30 = (bf16[256,1024]{1,0:T(8,128)(2,1)S(1)}, bf16[256,1024]{1,0:T(8,128)(2,1)S(1)}, u32[]{:S(2)}, u32[]{:S(2)}) collective-permute-start(bf16[256,1024]{1,0:T(8,128)(2,1)S(1)} %add_convert_fusion.11), channel_id=1, source_target_pairs={{0,2},{1,3},{2,0},{3,1},{4,6},{5,7},{6,4},{7,5},{8,10},{9,11},{10,... | collective-permute-start | bytes 1572872 | tf_op jit(solution)/shard_map/ppermute | solution.py:503
  373.5 22.3 %collective-permute-start.31 = (bf16[256,1024]{1,0:T(8,128)(2,1)S(1)}, bf16[256,1024]{1,0:T(8,128)(2,1)S(1)}, u32[]{:S(2)}, u32[]{:S(2)}) collective-permute-start(bf16[256,1024]{1,0:T(8,128)(2,1)S(1)} %get-tuple-element.176), channel_id=1, source_target_pairs={{0,2},{1,3},{2,0},{3,1},{4,6},{5,7},{6,4},{7,5},{8,10},{9,11},{10,... | collective-permute-start | bytes 1572872 | tf_op jit(solution)/shard_map/ppermute | solution.py:503
  402.0 22.0 %collective-permute-start.34 = (bf16[256,2048]{1,0:T(8,128)(2,1)S(1)}, bf16[256,2048]{1,0:T(8,128)(2,1)S(1)}, u32[]{:S(2)}, u32[]{:S(2)}) collective-permute-start(bf16[256,2048]{1,0:T(8,128)(2,1)S(1)} %get-tuple-element.151), channel_id=1, source_target_pairs={{0,1},{1,0},{2,3},{3,2},{4,5},{5,4},{6,7},{7,6},{8,9},{9,8},{10,11... | collective-permute-start | bytes 3145736 | tf_op jit(solution)/shard_map/ppermute | solution.py:503
  403.6 24.2 %collective-permute-start.35 = (bf16[256,2048]{1,0:T(8,128)(2,1)S(1)}, bf16[256,2048]{1,0:T(8,128)(2,1)S(1)}, u32[]{:S(2)}, u32[]{:S(2)}) collective-permute-start(bf16[256,2048]{1,0:T(8,128)(2,1)S(1)} %get-tuple-element.151), channel_id=1, source_target_pairs={{0,2},{1,3},{2,0},{3,1},{4,6},{5,7},{6,4},{7,5},{8,10},{9,11},{10,... | collective-permute-start | bytes 3145736 | tf_op jit(solution)/shard_map/ppermute | solution.py:503
  424.0 12.4 %collective-permute-start.36 = (bf16[256,1024]{1,0:T(8,128)(2,1)S(1)}, bf16[256,1024]{1,0:T(8,128)(2,1)S(1)}, u32[]{:S(2)}, u32[]{:S(2)}) collective-permute-start(bf16[256,1024]{1,0:T(8,128)(2,1)S(1)} %slice.99), channel_id=1, source_target_pairs={{0,2},{1,3},{2,0},{3,1},{4,6},{5,7},{6,4},{7,5},{8,10},{9,11},{10,... | collective-permute-start | bytes 1572872 | tf_op jit(solution)/shard_map/ppermute | solution.py:503
  450.6 239.0 %reduce-scatter.6.cloned.1.call-start = ((), (), s32[]{:S(2)}) async-start(), calls=%async_computation.14 | async-start | bytes 10485760 | tf_op jit(solution)/shard_map/reduce_scatter | solution.py:704
  482.2 25.6 %collective-permute-start.56 = (bf16[1024,4096]{1,0:T(8,128)(2,1)}, bf16[1024,4096]{1,0:T(8,128)(2,1)}, u32[]{:S(2)}, u32[]{:S(2)}) collective-permute-start(bf16[1024,4096]{1,0:T(8,128)(2,1)} %shard_map.299.other), channel_id=1, source_target_pairs={{0,4},{4,0},{1,5},{5,1},{2,6},{6,2},{3,7},{7,3},{8,12},{12,8},{9,1... | collective-permute-start | bytes 25165832 | tf_op jit(solution)/shard_map/ppermute | solution.py:473
  525.6 14.8 %collective-permute-start.39 = (bf16[512,512]{0,1:T(8,128)(2,1)S(1)}, bf16[512,512]{0,1:T(8,128)(2,1)S(1)}, u32[]{:S(2)}, u32[]{:S(2)}) collective-permute-start(bf16[512,512]{0,1:T(8,128)(2,1)S(1)} %get-tuple-element.171), channel_id=1, source_target_pairs={{0,1},{1,0},{2,3},{3,2},{4,5},{5,4},{6,7},{7,6},{8,9},{9,8},{10,11... | collective-permute-start | bytes 1572872 | tf_op jit(solution)/shard_map/ppermute | solution.py:503
  525.7 25.6 %collective-permute-start.38 = (bf16[512,512]{0,1:T(8,128)(2,1)S(1)}, bf16[512,512]{0,1:T(8,128)(2,1)S(1)}, u32[]{:S(2)}, u32[]{:S(2)}) collective-permute-start(bf16[512,512]{0,1:T(8,128)(2,1)S(1)} %get-tuple-element.168), channel_id=1, source_target_pairs={{0,1},{1,0},{2,3},{3,2},{4,5},{5,4},{6,7},{7,6},{8,9},{9,8},{10,11... | collective-permute-start | bytes 1572872 | tf_op jit(solution)/shard_map/ppermute | solution.py:503
  527.7 23.6 %collective-permute-start.42 = (bf16[512,512]{0,1:T(8,128)(2,1)S(1)}, bf16[512,512]{0,1:T(8,128)(2,1)S(1)}, u32[]{:S(2)}, u32[]{:S(2)}) collective-permute-start(bf16[512,512]{0,1:T(8,128)(2,1)S(1)} %get-tuple-element.169), channel_id=1, source_target_pairs={{0,2},{1,3},{2,0},{3,1},{4,6},{5,7},{6,4},{7,5},{8,10},{9,11},{10,... | collective-permute-start | bytes 1572872 | tf_op jit(solution)/shard_map/ppermute | solution.py:503
  540.5 14.9 %collective-permute-start.40 = (bf16[512,512]{0,1:T(8,128)(2,1)S(1)}, bf16[512,512]{0,1:T(8,128)(2,1)S(1)}, u32[]{:S(2)}, u32[]{:S(2)}) collective-permute-start(bf16[512,512]{0,1:T(8,128)(2,1)S(1)} %add_convert_fusion.9), channel_id=1, source_target_pairs={{0,2},{1,3},{2,0},{3,1},{4,6},{5,7},{6,4},{7,5},{8,10},{9,11},{10,... | collective-permute-start | bytes 1572872 | tf_op jit(solution)/shard_map/ppermute | solution.py:503
  541.8 23.3 %collective-permute-start.41 = (bf16[512,512]{0,1:T(8,128)(2,1)S(1)}, bf16[512,512]{0,1:T(8,128)(2,1)S(1)}, u32[]{:S(2)}, u32[]{:S(2)}) collective-permute-start(bf16[512,512]{0,1:T(8,128)(2,1)S(1)} %get-tuple-element.170), channel_id=1, source_target_pairs={{0,2},{1,3},{2,0},{3,1},{4,6},{5,7},{6,4},{7,5},{8,10},{9,11},{10,... | collective-permute-start | bytes 1572872 | tf_op jit(solution)/shard_map/ppermute | solution.py:503
  583.2 14.9 %collective-permute-start.48 = (bf16[512,512]{1,0:T(8,128)(2,1)S(1)}, bf16[512,512]{1,0:T(8,128)(2,1)S(1)}, u32[]{:S(2)}, u32[]{:S(2)}) collective-permute-start(bf16[512,512]{1,0:T(8,128)(2,1)S(1)} %get-tuple-element.165), channel_id=1, source_target_pairs={{0,1},{1,0},{2,3},{3,2},{4,5},{5,4},{6,7},{7,6},{8,9},{9,8},{10,11... | collective-permute-start | bytes 1572872 | tf_op jit(solution)/shard_map/ppermute | solution.py:503
  584.3 19.8 %collective-permute-start.47 = (bf16[512,512]{1,0:T(8,128)(2,1)S(1)}, bf16[512,512]{1,0:T(8,128)(2,1)S(1)}, u32[]{:S(2)}, u32[]{:S(2)}) collective-permute-start(bf16[512,512]{1,0:T(8,128)(2,1)S(1)} %get-tuple-element.162), channel_id=1, source_target_pairs={{0,1},{1,0},{2,3},{3,2},{4,5},{5,4},{6,7},{7,6},{8,9},{9,8},{10,11... | collective-permute-start | bytes 1572872 | tf_op jit(solution)/shard_map/ppermute | solution.py:503
  585.3 18.9 %collective-permute-start.51 = (bf16[512,512]{1,0:T(8,128)(2,1)S(1)}, bf16[512,512]{1,0:T(8,128)(2,1)S(1)}, u32[]{:S(2)}, u32[]{:S(2)}) collective-permute-start(bf16[512,512]{1,0:T(8,128)(2,1)S(1)} %get-tuple-element.163), channel_id=1, source_target_pairs={{0,2},{1,3},{2,0},{3,1},{4,6},{5,7},{6,4},{7,5},{8,10},{9,11},{10,... | collective-permute-start | bytes 1572872 | tf_op jit(solution)/shard_map/ppermute | solution.py:503
  598.3 13.0 %collective-permute-start.49 = (bf16[512,512]{1,0:T(8,128)(2,1)S(1)}, bf16[512,512]{1,0:T(8,128)(2,1)S(1)}, u32[]{:S(2)}, u32[]{:S(2)}) collective-permute-start(bf16[512,512]{1,0:T(8,128)(2,1)S(1)} %add_convert_fusion.7), channel_id=1, source_target_pairs={{0,2},{1,3},{2,0},{3,1},{4,6},{5,7},{6,4},{7,5},{8,10},{9,11},{10,... | collective-permute-start | bytes 1572872 | tf_op jit(solution)/shard_map/ppermute | solution.py:503
  598.9 18.0 %collective-permute-start.50 = (bf16[512,512]{1,0:T(8,128)(2,1)S(1)}, bf16[512,512]{1,0:T(8,128)(2,1)S(1)}, u32[]{:S(2)}, u32[]{:S(2)}) collective-permute-start(bf16[512,512]{1,0:T(8,128)(2,1)S(1)} %get-tuple-element.164), channel_id=1, source_target_pairs={{0,2},{1,3},{2,0},{3,1},{4,6},{5,7},{6,4},{7,5},{8,10},{9,11},{10,... | collective-permute-start | bytes 1572872 | tf_op jit(solution)/shard_map/ppermute | solution.py:503
  661.9 17.0 %collective-permute-start.57 = (bf16[1024,2048]{1,0:T(8,128)(2,1)}, bf16[1024,2048]{1,0:T(8,128)(2,1)}, u32[]{:S(2)}, u32[]{:S(2)}) collective-permute-start(bf16[1024,2048]{1,0:T(8,128)(2,1)} %shard_map.304.other), channel_id=1, source_target_pairs={{0,4},{4,0},{1,5},{5,1},{2,6},{6,2},{3,7},{7,3},{8,12},{12,8},{9,1... | collective-permute-start | bytes 12582920 | tf_op jit(solution)/shard_map/ppermute | solution.py:473
  663.8 24.9 %all-to-all-start.4 = ((bf16[4,64,2048]{2,1,0:T(8,128)(2,1)}), bf16[4,64,2048]{2,1,0:T(8,128)(2,1)S(1)}, u32[]{:S(2)}, u32[]{:S(2)}) async-start(bf16[4,64,2048]{2,1,0:T(8,128)(2,1)} %bitcast.26), calls=%async_computation.6 | async-start | bytes 2097152 | tf_op jit(solution)/shard_map/all_to_all | solution.py:692
  667.3 100.0 %reduce-scatter.8.cloned.1.call-start = ((), (), s32[]{:S(2)}) async-start(), calls=%async_computation.15 | async-start | bytes 5242880 | tf_op jit(solution)/shard_map/reduce_scatter | solution.py:735
  689.7 46.5 %all-to-all-start.5 = ((bf16[4,64,4096]{2,1,0:T(8,128)(2,1)}), bf16[4,64,4096]{2,1,0:T(8,128)(2,1)S(1)}, u32[]{:S(2)}, u32[]{:S(2)}) async-start(bf16[4,64,4096]{2,1,0:T(8,128)(2,1)} %bitcast.81), calls=%async_computation.7 | async-start | bytes 4194304 | tf_op jit(solution)/shard_map/all_to_all | solution.py:692
  697.2 34.2 %collective-permute-start.59 = (bf16[256,1024]{1,0:T(8,128)(2,1)}, bf16[256,1024]{1,0:T(8,128)(2,1)}, u32[]{:S(2)}, u32[]{:S(2)}) collective-permute-start(bf16[256,1024]{1,0:T(8,128)(2,1)} %get-tuple-element.159), channel_id=1, source_target_pairs={{0,1},{1,0},{2,3},{3,2},{4,5},{5,4},{6,7},{7,6},{8,9},{9,8},{10,11... | collective-permute-start | bytes 1572872 | tf_op jit(solution)/shard_map/ppermute | solution.py:503
  699.1 42.6 %collective-permute-start.58 = (bf16[256,1024]{1,0:T(8,128)(2,1)}, bf16[256,1024]{1,0:T(8,128)(2,1)}, u32[]{:S(2)}, u32[]{:S(2)}) collective-permute-start(bf16[256,1024]{1,0:T(8,128)(2,1)} %get-tuple-element.156), channel_id=1, source_target_pairs={{0,1},{1,0},{2,3},{3,2},{4,5},{5,4},{6,7},{7,6},{8,9},{9,8},{10,11... | collective-permute-start | bytes 1572872 | tf_op jit(solution)/shard_map/ppermute | solution.py:503
  699.2 42.5 %collective-permute-start.69 = (bf16[256,1024]{1,0:T(8,128)(2,1)}, bf16[256,1024]{1,0:T(8,128)(2,1)}, u32[]{:S(2)}, u32[]{:S(2)}) collective-permute-start(bf16[256,1024]{1,0:T(8,128)(2,1)} %get-tuple-element.157), channel_id=1, source_target_pairs={{0,2},{1,3},{2,0},{3,1},{4,6},{5,7},{6,4},{7,5},{8,10},{9,11},{10,... | collective-permute-start | bytes 1572872 | tf_op jit(solution)/shard_map/ppermute | solution.py:503
  732.8 15.0 %collective-permute-start.60 = (bf16[256,1024]{1,0:T(8,128)(2,1)S(1)}, bf16[256,1024]{1,0:T(8,128)(2,1)}, u32[]{:S(2)}, u32[]{:S(2)}) collective-permute-start(bf16[256,1024]{1,0:T(8,128)(2,1)S(1)} %add_convert_fusion.3), channel_id=1, source_target_pairs={{0,2},{1,3},{2,0},{3,1},{4,6},{5,7},{6,4},{7,5},{8,10},{9,11},{10,... | collective-permute-start | bytes 1572872 | tf_op jit(solution)/shard_map/ppermute | solution.py:503
  735.0 28.3 %collective-permute-start.68 = (bf16[256,1024]{1,0:T(8,128)(2,1)}, bf16[256,1024]{1,0:T(8,128)(2,1)}, u32[]{:S(2)}, u32[]{:S(2)}) collective-permute-start(bf16[256,1024]{1,0:T(8,128)(2,1)} %get-tuple-element.158), channel_id=1, source_target_pairs={{0,2},{1,3},{2,0},{3,1},{4,6},{5,7},{6,4},{7,5},{8,10},{9,11},{10,... | collective-permute-start | bytes 1572872 | tf_op jit(solution)/shard_map/ppermute | solution.py:503
  736.2 14.7 %collective-permute-start.62 = (f32[8192]{0:T(1024)S(1)}, f32[8192]{0:T(1024)S(1)}, u32[]{:S(2)}, u32[]{:S(2)}) collective-permute-start(f32[8192]{0:T(1024)S(1)} %add.450), channel_id=1, source_target_pairs={{0,8},{8,16},{16,24},{24,0},{1,9},{9,17},{17,25},{25,1},{2,10},{10... | collective-permute-start | bytes 98312 | tf_op jit(solution)/shard_map/ppermute | solution.py:477
  750.9 12.4 %collective-permute-start.70 = (bf16[256,1024]{1,0:T(8,128)(2,1)}, bf16[256,1024]{1,0:T(8,128)(2,1)}, u32[]{:S(2)}, u32[]{:S(2)}) collective-permute-start(bf16[256,1024]{1,0:T(8,128)(2,1)} %get-tuple-element.155), channel_id=1, source_target_pairs={{0,1},{1,0},{2,3},{3,2},{4,5},{5,4},{6,7},{7,6},{8,9},{9,8},{10,11... | collective-permute-start | bytes 1572872 | tf_op jit(solution)/shard_map/ppermute | solution.py:503
  767.3 23.6 %all-to-all-start.6 = ((bf16[4,64,2048]{2,1,0:T(8,128)(2,1)}), bf16[4,64,2048]{2,1,0:T(8,128)(2,1)S(1)}, u32[]{:S(2)}, u32[]{:S(2)}) async-start(bf16[4,64,2048]{2,1,0:T(8,128)(2,1)} %bitcast.82), calls=%async_computation.9 | async-start | bytes 2097152 | tf_op jit(solution)/shard_map/all_to_all | solution.py:692
  (82 other events, 1167.2 us)
Sparse Core Ops, SparseCore 0:
  28.6 82.0 all-gather.3
  112.3 149.6 all-gather.5
  263.5 80.3 all-gather.7
  450.7 87.1 reduce-scatter.3
  540.1 142.8 reduce-scatter.5
  689.8 77.4 reduce-scatter.7
